TPU v7x, 512 devices: a whole 4x8x8 slice. The times are simulated.
512 devices in a mesh: grp: 16 (over z, core), tp: 32 (over y, x).
Axes of the slice: x: 4, y: 8, z: 8, core: 2. Of those that a mesh axis runs over, the one named last changes fastest.
Arguments:
- residual_input: bfloat16 [2048, 5120], P('grp', 'tp'), may hold values from -6 to 6
- input_norm_gain: float32 [5120], replicated, may hold values from 0.1 to 1.9
- query_weight: bfloat16 [5120, 4096], P(None, 'tp'), may hold values from -0.078125 to 0.078125
- key_value_weight: bfloat16 [5120, 1024], P(None, 'tp'), may hold values from -0.3125 to 0.3125
- shared_down_factors: bfloat16 [5120, 48], replicated, may hold values from -0.078125 to 0.078125
- query_up_factors: bfloat16 [16, 16, 4096], P(None, None, 'tp'), may hold values from -1 to 1
- key_value_up_factors: bfloat16 [16, 16, 1024], replicated, may hold values from -1 to 1
- paged_base_keys: bfloat16 [2048, 128, 512], P(('grp', 'tp')), may hold values from -100 to 100
- paged_base_values: bfloat16 [2048, 128, 512], P(('grp', 'tp')), may hold values from -6 to 6
- paged_down_factors: bfloat16 [2048, 128, 32], P(('grp', 'tp')), may hold values from -6 to 6
- adapter_of_row: int32 [2048], P('grp'), may hold values from 0 to 15
- document_of_row: int32 [2048, 1], P('grp'), may hold values from 0 to 15; in each aligned block of 128 rows (0 to 127, 128 to 255, ...) at most 16 rows name the same one
- document_page_slots: int32 [16, 128], replicated, may hold values from 0 to 2047, as said below
Outputs:
- attended: bfloat16 [2048, 4096], P('grp', 'tp')
Inputs may be any that keep to these rules, and one draw needn't show every extreme that they name: `document_of_row`: in each aligned block of 128 rows no document is named by more than 16 rows. `document_page_slots`: each page slot is used once; all pages of one document lie on the 32 devices of one index of grp, 4 on each, documents and indices of grp one to one.
All inputs are finite; a program needn't handle non-finite values.
Results may differ from a plain program's by a relative error of at most 0.034.
Values may be sent and summed in bfloat16 or wider, within the bound.
No kernel may reach another device: no remote copies, remote signals or barrier semaphores. Data moves between devices by JAX's collectives and lax.ppermute only.
A program may use at most 64 MiB of HBM per device.

v0:
```python
import jax
import jax.numpy as jnp
from jax import lax
from jax.sharding import PartitionSpec as P

HEAD_SIZE = 128


def merge_slices(numerator, factor_sum, maxima, totals):
    peak_all = jnp.max(maxima, axis=-1)
    weight = jnp.exp(maxima - peak_all[..., None])
    numerator = jnp.sum(numerator * weight[..., None], axis=-2)
    factor_sum = jnp.sum(factor_sum * weight[..., None], axis=-2)
    totals = jnp.sum(totals * weight, axis=-1)
    return (numerator, factor_sum, peak_all, totals)


def attend_local(
    query_matrix,
    down_factors,
    paged_base_keys,
    paged_base_values,
    paged_down_factors,
    heads_kv,
    low_rank_width,
):
    item_count = query_matrix.shape[0]
    head_size = paged_base_keys.shape[-1] // heads_kv
    all_heads = query_matrix.shape[1] // head_size
    query_group_size = all_heads // heads_kv
    local_tokens = paged_base_keys.shape[0] * paged_base_keys.shape[1]
    score_scaling = head_size ** (-0.5)
    key_heads = paged_base_keys.reshape(local_tokens, heads_kv, head_size).transpose(1, 0, 2)
    value_heads = paged_base_values.reshape(local_tokens, heads_kv, head_size).transpose(1, 0, 2)
    factor_flat = paged_down_factors.reshape(local_tokens, 2 * low_rank_width)
    cached_key = factor_flat[:, :low_rank_width]
    cached_value = factor_flat[:, low_rank_width:]
    query_head_count = query_matrix.reshape(
        item_count, heads_kv, query_group_size, head_size
    ).transpose(1, 0, 2, 3)
    factor_heads = down_factors.reshape(
        item_count, heads_kv, query_group_size, low_rank_width
    ).transpose(1, 0, 2, 3)

    def one_head(bundle):
        query_one, factor_one, key_one, value_one = bundle
        scores = (
            jnp.einsum("ngd,ld->ngl", query_one, key_one, preferred_element_type=jnp.float32)
            + jnp.einsum("ngj,lj->ngl", factor_one, cached_key, preferred_element_type=jnp.float32)
        ) * score_scaling
        maxima = jnp.max(scores, -1)
        weights = jnp.exp(scores - maxima[..., None])
        totals = jnp.sum(weights, -1)
        rounded = weights.astype(jnp.bfloat16)
        numerator = jnp.einsum(
            "ngl,ld->ngd", rounded, value_one, preferred_element_type=jnp.float32
        )
        factor_sum = jnp.einsum(
            "ngl,lj->ngj", rounded, cached_value, preferred_element_type=jnp.float32
        )
        return (numerator, factor_sum, maxima, totals)

    numerator, factor_sum, maxima, totals = lax.map(
        one_head, (query_head_count, factor_heads, key_heads, value_heads)
    )
    numerator = numerator.transpose(1, 0, 2, 3).reshape(item_count, all_heads, head_size)
    factor_sum = factor_sum.transpose(1, 0, 2, 3).reshape(item_count, all_heads, low_rank_width)
    maxima = maxima.transpose(1, 0, 2).reshape(item_count, all_heads)
    totals = totals.transpose(1, 0, 2).reshape(item_count, all_heads)
    return (numerator, factor_sum, maxima, totals)


def per_device(
    residual_input,
    input_norm_gain,
    query_weight,
    key_value_weight,
    shared_down_factors,
    query_up_factors,
    key_value_up_factors,
    paged_base_keys,
    paged_base_values,
    paged_down_factors,
    adapter_of_row,
    document_of_row,
    document_page_slots,
):
    tp_count = lax.axis_size("tp")
    grp_count = lax.axis_size("grp")
    tp_index = lax.axis_index("tp")
    low_rank_width = shared_down_factors.shape[1] // 3
    key_value_width = key_value_up_factors.shape[2] // 2
    head_size = HEAD_SIZE
    heads_kv = key_value_width // head_size
    row_count = residual_input.shape[0]
    score_scaling = head_size ** (-0.5)
    gathered = lax.all_gather(residual_input, "tp", axis=1, tiled=True).astype(jnp.float32)
    normed_input = (
        gathered
        * lax.rsqrt(jnp.mean(gathered * gathered, -1, keepdims=True) + 1e-06)
        * input_norm_gain
    ).astype(jnp.bfloat16)
    low_rank_part = jnp.dot(
        normed_input, shared_down_factors, preferred_element_type=jnp.float32
    ).astype(jnp.bfloat16)
    query_low_rank = low_rank_part[:, :low_rank_width]
    key_low_rank = low_rank_part[:, low_rank_width : 2 * low_rank_width]
    value_low_rank = low_rank_part[:, 2 * low_rank_width :]
    query_update = query_up_factors[adapter_of_row]
    query_part = (
        jnp.dot(normed_input, query_weight, preferred_element_type=jnp.float32)
        + jnp.einsum("ep,epg->eg", query_low_rank, query_update, preferred_element_type=jnp.float32)
    ).astype(jnp.bfloat16)
    key_value_columns = key_value_weight.shape[1]
    key_value_start = tp_index * key_value_columns
    key_value_update = lax.dynamic_slice_in_dim(
        key_value_up_factors, key_value_start, key_value_columns, 2
    )[adapter_of_row]
    key_value_low = jnp.where(key_value_start < key_value_width, key_low_rank, value_low_rank)
    kv_part = (
        jnp.dot(normed_input, key_value_weight, preferred_element_type=jnp.float32)
        + jnp.einsum(
            "ep,epg->eg", key_value_low, key_value_update, preferred_element_type=jnp.float32
        )
    ).astype(jnp.bfloat16)
    heads_here = query_part.shape[1] // head_size
    query_group_size = heads_here * tp_count // heads_kv
    key_value_head = tp_index * heads_here // query_group_size
    key_column_count = lax.dynamic_slice_in_dim(
        key_value_up_factors, key_value_head * head_size, head_size, 2
    )[adapter_of_row]
    my_queries = query_part.reshape(row_count, heads_here, head_size)
    factor_part = jnp.einsum(
        "rhd,rjd->rhj", my_queries, key_column_count, preferred_element_type=jnp.float32
    ).astype(jnp.bfloat16)
    factor_part = factor_part.reshape(row_count, heads_here * low_rank_width)
    query_matrix, down_factors, fresh_kv = (
        lax.all_gather(query_part, "tp", axis=1, tiled=True),
        lax.all_gather(factor_part, "tp", axis=1, tiled=True),
        lax.all_gather(kv_part, "tp", axis=1, tiled=True),
    )
    doc_pages = document_page_slots.shape[1]
    owner_of_doc = document_page_slots[:, 0] // doc_pages
    doc_ids = document_of_row[:, 0]
    doc_match = (doc_ids[:, None] == jnp.arange(document_page_slots.shape[0])[None, :]).astype(
        jnp.int32
    )
    target = jnp.sum(doc_match * owner_of_doc[None, :], 1)
    target_match = (target[:, None] == jnp.arange(grp_count)[None, :]).astype(jnp.int32)
    earlier = jnp.cumsum(target_match, 0) - target_match
    capacity = 2 * row_count // grp_count
    slot_of = target * capacity + jnp.sum(earlier * target_match, 1)
    placing = (jnp.arange(grp_count * capacity)[:, None] == slot_of[None, :]).astype(jnp.bfloat16)
    send_queries = (
        jnp.dot(placing, query_matrix, preferred_element_type=jnp.float32)
        .astype(jnp.bfloat16)
        .reshape(grp_count, capacity, -1)
    )
    send_factors = (
        jnp.dot(placing, down_factors, preferred_element_type=jnp.float32)
        .astype(jnp.bfloat16)
        .reshape(grp_count, capacity, -1)
    )
    query_in = lax.all_to_all(send_queries, "grp", split_axis=0, concat_axis=0, tiled=True)
    factor_in = lax.all_to_all(send_factors, "grp", split_axis=0, concat_axis=0, tiled=True)
    per_source = query_in.shape[1]
    item_count = query_in.shape[0] * per_source
    query_flat = query_in.reshape(item_count, -1)
    factor_flat = factor_in.reshape(item_count, -1)
    numerator, factor_sum, maxima, totals = attend_local(
        query_flat,
        factor_flat,
        paged_base_keys,
        paged_base_values,
        paged_down_factors,
        heads_kv,
        low_rank_width,
    )
    all_heads = numerator.shape[1]
    returned = (
        lax.all_to_all(
            numerator.reshape(grp_count, per_source, all_heads, head_size),
            "grp",
            split_axis=0,
            concat_axis=0,
            tiled=True,
        ),
        lax.all_to_all(
            factor_sum.reshape(grp_count, per_source, all_heads, low_rank_width),
            "grp",
            split_axis=0,
            concat_axis=0,
            tiled=True,
        ),
        lax.all_to_all(
            maxima.reshape(grp_count, per_source, all_heads),
            "grp",
            split_axis=0,
            concat_axis=0,
            tiled=True,
        ),
        lax.all_to_all(
            totals.reshape(grp_count, per_source, all_heads),
            "grp",
            split_axis=0,
            concat_axis=0,
            tiled=True,
        ),
    )
    numerator, factor_sum, maxima, totals = [
        piece.reshape((grp_count * capacity,) + piece.shape[2:])[slot_of] for piece in returned
    ]
    numerator, factor_sum, maxima, totals = (
        lax.all_to_all(numerator[:, :, None, :], "tp", split_axis=1, concat_axis=2, tiled=True),
        lax.all_to_all(factor_sum[:, :, None, :], "tp", split_axis=1, concat_axis=2, tiled=True),
        lax.all_to_all(maxima[:, :, None], "tp", split_axis=1, concat_axis=2, tiled=True),
        lax.all_to_all(totals[:, :, None], "tp", split_axis=1, concat_axis=2, tiled=True),
    )
    numerator, factor_sum, maxima, totals = merge_slices(numerator, factor_sum, maxima, totals)
    own_key = lax.dynamic_slice_in_dim(fresh_kv, key_value_head * head_size, head_size, 1)
    value_own = lax.dynamic_slice_in_dim(
        fresh_kv, key_value_width + key_value_head * head_size, head_size, 1
    )
    own_token_score = (
        jnp.einsum("rhd,rd->rh", my_queries, own_key, preferred_element_type=jnp.float32)
        * score_scaling
    )
    peak_all = jnp.maximum(maxima, own_token_score)
    old_scale = jnp.exp(maxima - peak_all)
    own_weight = jnp.exp(own_token_score - peak_all)
    numerator = (
        numerator * old_scale[..., None]
        + own_weight[..., None] * value_own.astype(jnp.float32)[:, None, :]
    )
    factor_sum = factor_sum * old_scale[..., None]
    totals = totals * old_scale + own_weight
    value_column_count = lax.dynamic_slice_in_dim(
        key_value_up_factors, key_value_width + key_value_head * head_size, head_size, 2
    )[adapter_of_row]
    value_shift = jnp.einsum(
        "rhj,rjd->rhd",
        factor_sum,
        value_column_count.astype(jnp.float32),
        precision=lax.Precision.HIGHEST,
    )
    result = ((numerator + value_shift) / totals[..., None]).astype(jnp.bfloat16)
    return result.reshape(row_count, heads_here * head_size)


def solution(mesh):
    in_specs = (
        P("grp", "tp"),
        P(),
        P(None, "tp"),
        P(None, "tp"),
        P(),
        P(None, None, "tp"),
        P(),
        P(("grp", "tp"), None, None),
        P(("grp", "tp"), None, None),
        P(("grp", "tp"), None, None),
        P("grp"),
        P("grp", None),
        P(),
    )
    out_specs = P("grp", "tp")
    return jax.shard_map(
        per_device, mesh=mesh, in_specs=in_specs, out_specs=out_specs, check_vma=False
    )
```

profile of v0, /device:TPU:24, one launch (start us, length us, event | category | flops | bytes accessed | tf_op | source)
XLA Modules:
  0.0 580.4 jit_solution(15996799056777764881)
XLA Ops:
  9.5 86.2 %all-gather.3.cloned.1.call-done = bf16[128,5120]{0,1:T(8,128)(2,1)} async-done(((bf16[128,160]{0,1:T(8,128)(2,1)}), bf16[128,5120]{0,1:T(8,128)(2,1)}) %all-gather.3.cloned.1.call-update) | async-done | bytes 1310736 | tf_op jit(solution)/shard_map/all_gather | solution.py:97
  106.8 37.7 %all_gather.14 = bf16[128,512]{0,1:T(8,128)(2,1)S(1)} all-gather(bf16[128,16]{0,1:T(8,128)(2,1)S(1)} %bitcast.156), channel_id=1, replica_groups=mesh['grp'=16,'tp'=32] {'tp'}, dimensions={1}, use_global_device_ids=true | all-gather | bytes 135168 | tf_op jit(solution)/shard_map/all_gather | solution.py:139
  145.4 7.5 %all-to-all-start.1 = ((bf16[16,16,512]{2,1,0:T(8,128)(2,1)}), bf16[16,16,512]{2,1,0:T(8,128)(2,1)S(1)}, u32[]{:S(2)}, u32[]{:S(2)}) async-start(bf16[16,16,512]{2,1,0:T(8,128)(2,1)} %bitcast.21), calls=%async_computation.1 | async-start | bytes 524288 | tf_op jit(solution)/shard_map/all_to_all | solution.py:165
  152.9 25.0 %all-gather.5.cloned.1.call-done = bf16[128,4096]{1,0:T(8,128)(2,1)} async-done(((bf16[128,128]{1,0:T(8,128)(2,1)}), bf16[128,4096]{1,0:T(8,128)(2,1)}) %all-gather.5.cloned.1.call-update) | async-done | bytes 1048592 | tf_op jit(solution)/shard_map/all_gather | solution.py:138
  177.9 3.2 convolution_convert_fusion
  181.2 7.6 %all-to-all-start = ((bf16[16,16,4096]{2,1,0:T(8,128)(2,1)}), bf16[16,16,4096]{2,1,0:T(8,128)(2,1)}, u32[]{:S(2)}, u32[]{:S(2)}) async-start(bf16[16,16,4096]{2,1,0:T(8,128)(2,1)} %bitcast.16), calls=%async_computation | async-start | bytes 4194304 | tf_op jit(solution)/shard_map/all_to_all | solution.py:164
  190.9 2.7 reshape_reshape.19
  195.9 42.0 %all-to-all-done = bf16[16,16,4096]{2,1,0:T(8,128)(2,1)} async-done(((bf16[16,16,4096]{2,1,0:T(8,128)(2,1)}), bf16[16,16,4096]{2,1,0:T(8,128)(2,1)}, u32[]{:S(2)}, u32[]{:S(2)}) %all-to-all-start) | async-done | bytes 2097184 | tf_op jit(solution)/shard_map/all_to_all | solution.py:164
  240.0 37.5 %while.16 = (s32[]{:T(128)}, f32[4,256,8,128]{3,1,2,0:T(8,128)}, f32[4,256,8,16]{1,3,2,0:T(8,128)}, f32[4,256,8]{1,2,0:T(8,128)}, f32[4,256,8]{1,2,0:T(8,128)S(1...) while((s32[]{:T(128)}, f32[4,256,8,128]{3,1,2,0:T(8,128)}, ...), condition=%wide.region_7.8_spmd, body=%wide.region_4.7_spmd.sunk | while | flops 613412864 | bytes 28353680 | solution.py:63
  246.7 2.7 fusion.71
  256.1 2.7 fusion.71
  265.5 2.7 fusion.71
  274.8 2.7 fusion.71
  278.5 4.7 all-to-all-start.8
  285.1 5.9 %all-to-all-done.8 = f32[16,1,512]{2,1,0:T(1,128)S(1)} async-done(((f32[16,1,512]{2,1,0:T(1,128)}), f32[16,1,512]{2,1,0:T(1,128)S(1)}, u32[]{:S(2)}, u32[]{:S(2)}) %all-to-all-start.8) | async-done | bytes 32800 | tf_op jit(solution)/shard_map/all_to_all | solution.py:202
  291.0 3.5 all-to-all-start.4
  297.1 5.1 all-to-all-done.4
  302.1 8.7 %all-to-all-start.9 = ((f32[128,32,1]{0,2,1:T(1,128)}), f32[128,32,1]{0,2,1:T(1,128)S(1)}, u32[]{:S(2)}, u32[]{:S(2)}) async-start(f32[128,32,1]{0,2,1:T(1,128)} %copy.61), calls=%async_computation.9 | async-start | bytes 32768 | tf_op jit(solution)/shard_map/all_to_all | solution.py:217
  312.9 4.8 all-to-all-done.9
  317.7 6.7 %all-to-all-start.5 = ((f32[128,32,1]{0,2,1:T(1,128)}), f32[128,32,1]{0,2,1:T(1,128)S(1)}, u32[]{:S(2)}, u32[]{:S(2)}) async-start(f32[128,32,1]{0,2,1:T(1,128)} %copy.55), calls=%async_computation.5 | async-start | bytes 32768 | tf_op jit(solution)/shard_map/all_to_all | solution.py:216
  324.4 2.7 reshape_reshape.22
  327.0 4.0 copy.58
  332.9 3.8 all-to-all-start.6
  336.7 6.6 %copy.52 = f32[16,16,32,128]{3,2,1,0:T(8,128)} copy(f32[16,16,32,128]{3,1,0,2:T(8,128)} %bitcast.142) | data formatting | bytes 8388608 | tf_op jit(solution)/shard_map/reshape;reshape | solution.py:182
  343.2 9.1 %all-to-all-done.6 = f32[16,1,8192]{2,1,0:T(1,128)S(1)} async-done(((f32[16,1,8192]{2,1,0:T(1,128)}), f32[16,1,8192]{2,1,0:T(1,128)S(1)}, u32[]{:S(2)}, u32[]{:S(2)}) %all-to-all-start.6) | async-done | bytes 524320 | tf_op jit(solution)/shard_map/all_to_all | solution.py:188
  352.4 4.5 all-to-all-start.2
  364.2 87.0 %all-to-all-done.2 = f32[16,16,32,128]{3,2,1,0:T(8,128)} async-done(((f32[16,16,32,128]{3,2,1,0:T(8,128)}), f32[16,16,32,128]{3,2,1,0:T(8,128)}, u32[]{:S(2)}, u32[]{:S(2)}) %all-to-all-start.2) | async-done | bytes 4194336 | tf_op jit(solution)/shard_map/all_to_all | solution.py:181
  451.1 9.9 %all-to-all-start.7 = ((f32[128,32,1,16]{0,3,2,1:T(8,128)}), f32[128,32,1,16]{0,3,2,1:T(8,128)}, u32[]{:S(2)}, u32[]{:S(2)}) async-start(f32[128,32,1,16]{0,3,2,1:T(8,128)} %copy.59), calls=%async_computation.7 | async-start | bytes 524288 | tf_op jit(solution)/shard_map/all_to_all | solution.py:215
  461.0 2.9 gather_fusion.2
  466.4 5.0 all-to-all-done.7
  471.4 6.2 %all-to-all-start.3 = ((f32[128,32,1,128]{3,0,2,1:T(8,128)}), f32[128,32,1,128]{3,0,2,1:T(8,128)S(1)}, u32[]{:S(2)}, u32[]{:S(2)}) async-start(f32[128,32,1,128]{3,0,2,1:T(8,128)} %copy.53), calls=%async_computation.3 | async-start | bytes 4194304 | tf_op jit(solution)/shard_map/all_to_all | solution.py:214
  488.5 77.9 %all_gather.15 = bf16[128,1024]{0,1:T(8,128)(2,1)S(1)} all-gather(bf16[128,32]{0,1:T(8,128)(2,1)S(1)} %fusion.23), channel_id=1, replica_groups=mesh['grp'=16,'tp'=32] {'tp'}, dimensions={1}, use_global_device_ids=true | all-gather | bytes 270336 | tf_op jit(solution)/shard_map/all_gather | solution.py:140
  (151 shorter events, 84.7 us)
Async XLA Ops:
  6.5 94.7 %copy-start = (bf16[5120,128]{1,0:T(8,128)(2,1)S(1)}, bf16[5120,128]{1,0:T(8,128)(2,1)}, u32[]{:S(2)}) copy-start(bf16[5120,128]{1,0:T(8,128)(2,1)} %param.17) | copy-start | bytes 3932164
  6.5 89.2 %all-gather.3.cloned.1.call-start = ((), (), s32[]{:S(2)}) async-start(), calls=%async_computation.10 | async-start | bytes 1351680 | tf_op jit(solution)/shard_map/all_gather | solution.py:97
  7.3 170.7 %all-gather.5.cloned.1.call-start = ((), (), s32[]{:S(2)}) async-start(), calls=%async_computation.11 | async-start | bytes 1081344 | tf_op jit(solution)/shard_map/all_gather | solution.py:138
  8.0 96.7 %copy-start.12 = (s32[1024]{0:T(1024)}, s32[1024]{0:T(1024)S(1)}, u32[]{:S(2)}) copy-start(s32[1024]{0:T(1024)S(1)} %pad_clamp_fusion.1) | copy-start | bytes 12292
  8.0 93.3 %copy-start.18 = (f32[5120]{0:T(1024)S(1)}, f32[5120]{0:T(1024)}, u32[]{:S(2)}) copy-start(f32[5120]{0:T(1024)} %param.16) | copy-start | bytes 61444
  95.8 5.5 copy-start.1
  97.9 5.3 copy-start.20
  100.2 3.0 copy-start.13
  100.2 3.1 copy-start.19
  145.4 35.7 %all-to-all-start.1 = ((bf16[16,16,512]{2,1,0:T(8,128)(2,1)}), bf16[16,16,512]{2,1,0:T(8,128)(2,1)S(1)}, u32[]{:S(2)}, u32[]{:S(2)}) async-start(bf16[16,16,512]{2,1,0:T(8,128)(2,1)} %bitcast.21), calls=%async_computation.1 | async-start | bytes 524288 | tf_op jit(solution)/shard_map/all_to_all | solution.py:165
  181.2 7.6 %copy-start.4 = (bf16[4,128,512]{2,1,0:T(8,128)(2,1)S(1)}, bf16[4,128,512]{2,1,0:T(8,128)(2,1)}, u32[]{:S(2)}) copy-start(bf16[4,128,512]{2,1,0:T(8,128)(2,1)} %param.22) | copy-start | bytes 1572868
  181.2 7.6 %copy-start.2 = (bf16[16,16,512]{2,1,0:T(8,128)(2,1)}, bf16[16,16,512]{2,1,0:T(8,128)(2,1)S(1)}, u32[]{:S(2)}) copy-start(bf16[16,16,512]{2,1,0:T(8,128)(2,1)S(1)} %all-to-all-done.1) | copy-start | bytes 786436
  181.2 8.7 %copy-start.5 = (bf16[4,128,512]{2,1,0:T(8,128)(2,1)S(1)}, bf16[4,128,512]{2,1,0:T(8,128)(2,1)}, u32[]{:S(2)}) copy-start(bf16[4,128,512]{2,1,0:T(8,128)(2,1)} %param.23) | copy-start | bytes 1572868
  181.2 56.8 %all-to-all-start = ((bf16[16,16,4096]{2,1,0:T(8,128)(2,1)}), bf16[16,16,4096]{2,1,0:T(8,128)(2,1)}, u32[]{:S(2)}, u32[]{:S(2)}) async-start(bf16[16,16,4096]{2,1,0:T(8,128)(2,1)} %bitcast.16), calls=%async_computation | async-start | bytes 4194304 | tf_op jit(solution)/shard_map/all_to_all | solution.py:164
  188.8 2.2 copy-start.11
  277.5 46.9 %copy-start.3 = (f32[4,256,8,16]{1,3,2,0:T(8,128)S(1)}, f32[4,256,8,16]{1,3,2,0:T(8,128)}, u32[]{:S(2)}) copy-start(f32[4,256,8,16]{1,3,2,0:T(8,128)} %get-tuple-element.67) | copy-start | bytes 1572868
  278.5 12.4 %all-to-all-start.8 = ((f32[16,1,512]{2,1,0:T(1,128)}), f32[16,1,512]{2,1,0:T(1,128)S(1)}, u32[]{:S(2)}, u32[]{:S(2)}) async-start(f32[16,1,512]{2,1,0:T(1,128)} %reshape.366), calls=%async_computation.8 | async-start | bytes 65536 | tf_op jit(solution)/shard_map/all_to_all | solution.py:202
  291.0 11.2 %all-to-all-start.4 = ((f32[16,1,512]{2,1,0:T(1,128)}), f32[16,1,512]{2,1,0:T(1,128)S(1)}, u32[]{:S(2)}, u32[]{:S(2)}) async-start(f32[16,1,512]{2,1,0:T(1,128)} %reshape.364), calls=%async_computation.4 | async-start | bytes 65536 | tf_op jit(solution)/shard_map/all_to_all | solution.py:195
  302.1 15.5 %all-to-all-start.9 = ((f32[128,32,1]{0,2,1:T(1,128)}), f32[128,32,1]{0,2,1:T(1,128)S(1)}, u32[]{:S(2)}, u32[]{:S(2)}) async-start(f32[128,32,1]{0,2,1:T(1,128)} %copy.61), calls=%async_computation.9 | async-start | bytes 32768 | tf_op jit(solution)/shard_map/all_to_all | solution.py:217
  317.7 6.7 %copy-start.9 = (f32[128,32,1]{0,2,1:T(1,128)}, f32[128,32,1]{0,2,1:T(1,128)S(1)}, u32[]{:S(2)}) copy-start(f32[128,32,1]{0,2,1:T(1,128)S(1)} %all-to-all-done.9) | copy-start | bytes 49156
  317.7 15.2 %all-to-all-start.5 = ((f32[128,32,1]{0,2,1:T(1,128)}), f32[128,32,1]{0,2,1:T(1,128)S(1)}, u32[]{:S(2)}, u32[]{:S(2)}) async-start(f32[128,32,1]{0,2,1:T(1,128)} %copy.55), calls=%async_computation.5 | async-start | bytes 32768 | tf_op jit(solution)/shard_map/all_to_all | solution.py:216
  332.9 19.5 %all-to-all-start.6 = ((f32[16,1,8192]{2,1,0:T(1,128)}), f32[16,1,8192]{2,1,0:T(1,128)S(1)}, u32[]{:S(2)}, u32[]{:S(2)}) async-start(f32[16,1,8192]{2,1,0:T(1,128)} %reshape.362), calls=%async_computation.6 | async-start | bytes 1048576 | tf_op jit(solution)/shard_map/all_to_all | solution.py:188
  352.4 98.8 %all-to-all-start.2 = ((f32[16,16,32,128]{3,2,1,0:T(8,128)}), f32[16,16,32,128]{3,2,1,0:T(8,128)}, u32[]{:S(2)}, u32[]{:S(2)}) async-start(f32[16,16,32,128]{3,2,1,0:T(8,128)} %copy.52), calls=%async_computation.2 | async-start | bytes 8388608 | tf_op jit(solution)/shard_map/all_to_all | solution.py:181
  451.1 20.3 %all-to-all-start.7 = ((f32[128,32,1,16]{0,3,2,1:T(8,128)}), f32[128,32,1,16]{0,3,2,1:T(8,128)}, u32[]{:S(2)}, u32[]{:S(2)}) async-start(f32[128,32,1,16]{0,3,2,1:T(8,128)} %copy.59), calls=%async_computation.7 | async-start | bytes 524288 | tf_op jit(solution)/shard_map/all_to_all | solution.py:215
  471.4 99.1 %all-to-all-start.3 = ((f32[128,32,1,128]{3,0,2,1:T(8,128)}), f32[128,32,1,128]{3,0,2,1:T(8,128)S(1)}, u32[]{:S(2)}, u32[]{:S(2)}) async-start(f32[128,32,1,128]{3,0,2,1:T(8,128)} %copy.53), calls=%async_computation.3 | async-start | bytes 4194304 | tf_op jit(solution)/shard_map/all_to_all | solution.py:214
  485.6 81.6 %copy-start.7 = (f32[128,128]{0,1:T(8,128)S(1)}, f32[128,128]{0,1:T(8,128)}, u32[]{:S(2)}) copy-start(f32[128,128]{0,1:T(8,128)} %copy.73) | copy-start | bytes 196612
  486.2 81.0 %copy-start.10 = (f32[128,32,1]{0,2,1:T(1,128)S(1)}, f32[128,32,1]{0,2,1:T(1,128)}, u32[]{:S(2)}) copy-start(f32[128,32,1]{0,2,1:T(1,128)} %copy-done.9) | copy-start | bytes 49156
  567.8 1.1 copy-start.14
  567.8 1.1 copy-start.8
  567.8 4.2 copy-start.16
  567.8 4.2 copy-start.17
  569.0 3.1 copy-start.15
  (1 other events, 0.7 us)
Sparse Core Ops, SparseCore 0:
  10.5 85.2 all-gather.2
  103.3 74.5 all-gather.4
where the time goes:
time: 583 us; the launch traced here: 580 us
  waiting for transfers between devices  271 us (46%)
  blocking collectives  116 us (20%)
  starting transfers between devices  63.1 us (11%)
  local copies, waits for them, and re-layouts  56.2 us (10%)
  matrix products  42 us (7%)
  other arithmetic  18.5 us (3%)
  between operations  14 us (2%)
    all_to_all x1, waiting for transfers between devices, per_device(): lax.all_to_all(numerator.reshape(grp_count, per_source, all_heads, head_s...  87 us
    all_gather x1, waiting for transfers between devices, per_device(): lax.all_gather(residual_input, 'tp', axis=1, tiled=True).astype(jnp.float32)  86.2 us
    all_gather x1, blocking collectives, per_device(): lax.all_gather(kv_part, 'tp', axis=1, tiled=True)  77.9 us
    all_to_all x1, waiting for transfers between devices, per_device(): lax.all_to_all(send_queries, 'grp', split_axis=0, concat_axis=0, tiled=True)  42 us
    all_gather x1, blocking collectives, per_device(): lax.all_gather(factor_part, 'tp', axis=1, tiled=True)  37.7 us
    all_gather x1, waiting for transfers between devices, per_device(): lax.all_gather(query_part, 'tp', axis=1, tiled=True)  25 us
  transfers between devices with their start and end apart: 12, of which 9 were waited for; matrix products, arithmetic and copies ran while one was open for 11% of the time, Pallas kernels for 0%

commit v1 on v0

v1 whole, which is shorter than its diff:
```python
import functools
import math

import jax
import jax.numpy as jnp
from jax import lax
from jax.experimental import pallas as pl
from jax.experimental.pallas import tpu as pltpu
from jax.sharding import Mesh, PartitionSpec as P

HEAD_SIZE = 128
RANK = 16
LANES = 128
Y_HIGH, Y_LOW, X = 4, 2, 4
Y = Y_HIGH * Y_LOW
BLOCK = Y_LOW * X
SLOTS = 256
TILES = SLOTS // LANES
QUERY_ROWS = HEAD_SIZE + RANK
MESSAGE_ROWS = TILES * QUERY_ROWS + 32
RETURN_ROWS = TILES * HEAD_SIZE + 16
PIECE_TOKENS = 512
SCORE_SCALE = HEAD_SIZE**-0.5
F32 = jnp.float32
BF16 = jnp.bfloat16
VMEM = pl.BlockSpec(memory_space=pltpu.VMEM)
SMEM = pl.BlockSpec(memory_space=pltpu.SMEM)


def dot(left, right, left_dim, right_dim):
    return lax.dot_general(
        left, right, (((left_dim,), (right_dim,)), ((), ())), preferred_element_type=F32
    )


def call(kernel, out_shape, in_specs, scratch=(), flops=0, moved=0, limit=32):
    return pl.pallas_call(
        kernel,
        out_shape=out_shape,
        in_specs=in_specs,
        out_specs=jax.tree.map(lambda _: VMEM, out_shape),
        scratch_shapes=list(scratch),
        compiler_params=pltpu.CompilerParams(vmem_limit_bytes=limit * 1024 * 1024),
        cost_estimate=pl.CostEstimate(flops=flops, bytes_accessed=moved, transcendentals=0),
    )


def shape(*dims, dtype=BF16):
    return jax.ShapeDtypeStruct(dims, dtype)


def of_adapter(low, adapters):
    repeated = jnp.concatenate([low] * 16, axis=0)
    adapter = lax.broadcasted_iota(jnp.int32, repeated.shape, 0) // RANK
    return jnp.where(adapter == adapters, repeated, jnp.zeros_like(repeated))


def split_float(value):
    high = value.astype(BF16).astype(F32)
    middle = (value - high).astype(BF16).astype(F32)
    return high, middle, value - high - middle


def pack_kernel(place, keys, values, factors, *pieces):
    own = place[1]
    factors_t = factors[...].astype(F32).T.astype(BF16)
    for shift, piece in enumerate(pieces):
        head = lax.rem(own + shift, Y_HIGH)
        columns = pl.ds(pl.multiple_of(head * HEAD_SIZE, HEAD_SIZE), HEAD_SIZE)
        piece[0:PIECE_TOKENS, :] = keys[:, columns]
        piece[PIECE_TOKENS : 2 * PIECE_TOKENS, :] = values[:, columns]
        for page in range(PIECE_TOKENS // LANES):
            start = 2 * PIECE_TOKENS + page * 2 * RANK
            piece[start : start + 2 * RANK, :] = factors_t[:, page * LANES : (page + 1) * LANES]


def project_kernel(
    groups,
    place,
    page_slots,
    features,
    query_weight,
    key_value_weight,
    down,
    gain,
    query_up,
    key_value_up,
    adapters,
    documents,
    message,
    fresh,
    queries_t,
    placing,
    normed,
    weights,
    update,
):
    device = place[0]
    part = gain.shape[1]
    width = normed.shape[0]
    rows = features.shape[-1]

    squares = jnp.zeros((part, rows), F32)
    for x in range(X):
        for y in range(Y):
            block = features[x, y].astype(F32)
            squares = squares + block * block
    scale = lax.rsqrt(jnp.sum(squares, axis=0, keepdims=True) / width + 1e-06)
    gain_t = gain[...].T
    for x in range(X):
        for y in range(Y):
            t = y * X + x
            block = features[x, y].astype(F32) * scale * gain_t[:, t : t + 1]
            normed[t * part : (t + 1) * part, :] = block.astype(BF16)
    weights[:, 0:HEAD_SIZE] = query_weight[...]
    weights[:, HEAD_SIZE:] = jnp.concatenate(
        [key_value_weight[...], down[...], jnp.zeros((width, HEAD_SIZE - 80), BF16)], axis=1
    )
    total = dot(normed[...], weights[...], 0, 0).T

    adapter = adapters[...]
    low = total[HEAD_SIZE + 32 : HEAD_SIZE + 80].astype(BF16)
    query_update = dot(query_up[...], of_adapter(low[0:RANK], adapter), 0, 0)
    queries = (total[0:HEAD_SIZE] + query_update).astype(BF16)
    queries_t[...] = queries

    is_key = device < Y * X // 2
    low_kv = jnp.where(is_key, low[RANK : 2 * RANK], low[2 * RANK :])
    columns = pl.ds(pl.multiple_of(device // X * HEAD_SIZE, HEAD_SIZE), HEAD_SIZE)
    update[...] = dot(key_value_up[:, columns], of_adapter(low_kv, adapter), 0, 0)
    mine = pl.ds(pl.multiple_of(lax.rem(device, X) * 32, 32), 32)
    fresh[...] = (total[HEAD_SIZE : HEAD_SIZE + 32] + update[mine, :]).astype(BF16)

    document = documents[...]
    target = jnp.zeros_like(document)
    for d in range(page_slots.shape[0]):
        target = jnp.where(document == d, page_slots[d, 0] // page_slots.shape[1], target)
    capacity = SLOTS // groups
    group = lax.broadcasted_iota(jnp.int32, (16, rows), 0)
    match = (group == target).astype(F32)
    before = (
        lax.broadcasted_iota(jnp.int32, (rows, rows), 0)
        < lax.broadcasted_iota(jnp.int32, (rows, rows), 1)
    ).astype(F32)
    earlier = dot(match.astype(BF16), before.astype(BF16), 1, 0)
    position = jnp.sum(earlier * match, axis=0, keepdims=True).astype(jnp.int32)
    slot = target * capacity + position
    place_here = lax.broadcasted_iota(jnp.int32, (SLOTS, rows), 0) == slot
    placed = place_here.astype(F32)
    placing[...] = placed.astype(BF16)
    message[:, 0:capacity, :] = (
        dot(placed.astype(BF16), queries, 1, 1).astype(BF16).reshape(groups, capacity, HEAD_SIZE)
    )
    slot_adapter = jnp.sum(placed * adapter.astype(F32), axis=1, keepdims=True)
    message[:, capacity:, :] = (
        jnp.broadcast_to(slot_adapter, (SLOTS, LANES)).astype(BF16).reshape(groups, capacity, LANES)
    )


def factor_kernel(groups, place, received, fresh, key_value_up, message, slot_adapters):
    capacity = SLOTS // groups
    queries = received[:, 0:capacity, :].reshape(SLOTS, HEAD_SIZE)
    queries_t = queries.astype(F32).T.astype(BF16)
    adapters = received[:, capacity:, :].reshape(SLOTS, LANES).astype(F32).T[0:1]
    slot_adapters[...] = jnp.broadcast_to(adapters, slot_adapters.shape)
    columns = pl.ds(pl.multiple_of(place[1] * HEAD_SIZE, HEAD_SIZE), HEAD_SIZE)
    every = dot(key_value_up[:, columns], queries, 1, 1)
    adapter = (lax.broadcasted_iota(jnp.int32, every.shape, 0) // RANK).astype(F32)
    kept = jnp.where(adapter == adapters, every, 0.0)
    factors = kept[0:RANK]
    for a in range(1, 16):
        factors = factors + kept[a * RANK : (a + 1) * RANK]
    factors = factors.astype(BF16)
    new = fresh[...]
    for member in range(BLOCK):
        for tile in range(TILES):
            lanes = slice(tile * LANES, (tile + 1) * LANES)
            start = tile * QUERY_ROWS
            message[member, start : start + HEAD_SIZE, :] = queries_t[:, lanes]
            message[member, start + HEAD_SIZE : start + QUERY_ROWS, :] = factors[:, lanes]
        message[member, TILES * QUERY_ROWS :, :] = new


def attend_kernel(
    place,
    queries,
    slot_adapters,
    key_value_up,
    piece_0,
    piece_1,
    piece_2,
    piece_3,
    message,
    keys,
    values_t,
    query,
    scores,
):
    pieces = (piece_0, piece_1, piece_2, piece_3)
    tokens = PIECE_TOKENS * len(pieces)
    depth = 2 * HEAD_SIZE
    value_rows = values_t.shape[0]
    ones = (
        lax.broadcasted_iota(jnp.int32, (value_rows - QUERY_ROWS, tokens), 0) == 0
    ).astype(F32)
    values_t[QUERY_ROWS:, :] = ones.astype(BF16)
    for index, piece in enumerate(pieces):
        for page in range(PIECE_TOKENS // LANES):
            start = page * LANES
            here = slice(index * PIECE_TOKENS + start, index * PIECE_TOKENS + start + LANES)
            row = 2 * PIECE_TOKENS + page * 2 * RANK
            factors = piece[row : row + 2 * RANK, :]
            key_factors = jnp.concatenate(
                [factors[0:RANK].astype(F32), jnp.zeros((LANES - RANK, LANES), F32)], axis=0
            )
            keys[here, 0:HEAD_SIZE] = piece[start : start + LANES, :]
            keys[here, HEAD_SIZE:] = key_factors.T.astype(BF16)
            value = piece[PIECE_TOKENS + start : PIECE_TOKENS + start + LANES, :]
            values_t[0:HEAD_SIZE, here] = value.astype(F32).T.astype(BF16)
            values_t[HEAD_SIZE:QUERY_ROWS, here] = factors[RANK:]
    query[QUERY_ROWS:, :] = jnp.zeros((depth - QUERY_ROWS, SLOTS), BF16)

    columns = pl.ds(pl.multiple_of((place[1] + Y_HIGH) * HEAD_SIZE, HEAD_SIZE), HEAD_SIZE)
    value_up = key_value_up[:, columns]
    adapters = slot_adapters[0:1, :].astype(jnp.int32)
    chunk = 512

    def one_head(head, carry):
        for tile in range(TILES):
            query[0:QUERY_ROWS, tile * LANES : (tile + 1) * LANES] = queries[
                head, tile * QUERY_ROWS : (tile + 1) * QUERY_ROWS, :
            ]
        highest = None
        for start in range(0, tokens, chunk):
            score = dot(keys[start : start + chunk, :], query[...], 1, 0)
            scores[start : start + chunk, :] = score
            top = jnp.max(score.reshape(chunk // 8, 8, SLOTS), axis=0)
            highest = top if highest is None else jnp.maximum(highest, top)
        peak = jnp.max(highest, axis=0, keepdims=True)
        total = jnp.zeros((value_rows, SLOTS), F32)
        for start in range(0, tokens, chunk):
            shifted = scores[start : start + chunk, :] - peak
            weight = jnp.exp2(shifted * (SCORE_SCALE * math.log2(math.e))).astype(BF16)
            total = total + dot(values_t[:, start : start + chunk], weight, 1, 0)
        mass = total[QUERY_ROWS : QUERY_ROWS + 1]
        inverse = 1.0 / mass
        low = (total[HEAD_SIZE:QUERY_ROWS] * inverse).astype(BF16)
        shift = dot(value_up, of_adapter(low, adapters), 0, 0)
        result = (total[0:HEAD_SIZE] * inverse + shift).astype(BF16)
        log_mass = peak * SCORE_SCALE + jnp.log(mass)
        parts = split_float(log_mass)
        stats = [part[:, tile * LANES : (tile + 1) * LANES] for tile in range(TILES) for part in parts]
        stats = jnp.concatenate(stats + [jnp.zeros((16 - len(stats), LANES), F32)], axis=0)
        for tile in range(TILES):
            message[head, tile * HEAD_SIZE : (tile + 1) * HEAD_SIZE, :] = result[
                :, tile * LANES : (tile + 1) * LANES
            ]
        message[head, TILES * HEAD_SIZE :, :] = stats.astype(BF16)
        return carry

    lax.fori_loop(0, BLOCK, one_head, 0)


def merge_kernel(groups, partials, message):
    capacity = SLOTS // groups
    stats = [partials[member, TILES * HEAD_SIZE :, :].astype(F32) for member in range(BLOCK)]
    results, masses = [], []
    for tile in range(TILES):
        first = 3 * tile
        logs = [s[first : first + 1] + s[first + 1 : first + 2] + s[first + 2 : first + 3] for s in stats]
        peak = functools.reduce(jnp.maximum, logs)
        weights = [jnp.exp(one - peak) for one in logs]
        whole = functools.reduce(jnp.add, weights)
        rows = slice(tile * HEAD_SIZE, (tile + 1) * HEAD_SIZE)
        total = jnp.zeros((HEAD_SIZE, LANES), F32)
        for member in range(BLOCK):
            total = total + partials[member, rows, :].astype(F32) * weights[member]
        results.append((total / whole).T.astype(BF16))
        parts = list(split_float(peak + jnp.log(whole)))
        parts = jnp.concatenate(parts + [jnp.zeros((LANES - 3, LANES), F32)], axis=0)
        masses.append(parts.T.astype(BF16))
    message[:, 0:capacity, :] = jnp.concatenate(results, axis=0).reshape(groups, capacity, HEAD_SIZE)
    message[:, capacity:, :] = jnp.concatenate(masses, axis=0).reshape(groups, capacity, LANES)


def finish_kernel(groups, received, placing, queries_t, gathered, out):
    capacity = SLOTS // groups
    place = placing[...]
    shared = dot(received[:, 0:capacity, :].reshape(SLOTS, HEAD_SIZE), place, 0, 0)
    stats = dot(received[:, capacity:, :].reshape(SLOTS, LANES), place, 0, 0)
    log_mass = stats[0:1] + stats[1:2] + stats[2:3]
    new = gathered[:, TILES * QUERY_ROWS :, :]
    key = new[0:X].reshape(HEAD_SIZE, LANES).astype(F32)
    value = new[X:].reshape(HEAD_SIZE, LANES).astype(F32)
    own = jnp.sum(queries_t[...].astype(F32) * key, axis=0, keepdims=True) * SCORE_SCALE
    peak = jnp.maximum(log_mass, own)
    shared_weight = jnp.exp(log_mass - peak)
    own_weight = jnp.exp(own - peak)
    result = (shared * shared_weight + value * own_weight) / (shared_weight + own_weight)
    out[...] = result.T.astype(BF16)


def per_device(
    residual_input,
    input_norm_gain,
    query_weight,
    key_value_weight,
    shared_down_factors,
    query_up_factors,
    key_value_up_factors,
    paged_base_keys,
    paged_base_values,
    paged_down_factors,
    adapter_of_row,
    document_of_row,
    document_page_slots,
):
    groups = lax.axis_size("grp")
    capacity = SLOTS // groups
    rows, part = residual_input.shape
    width = part * Y * X
    y_high = lax.axis_index("yh")
    device = (y_high * Y_LOW + lax.axis_index("yl")) * X + lax.axis_index("x")
    place = jnp.stack([device, y_high]).astype(jnp.int32)
    query_up = query_up_factors.reshape(-1, HEAD_SIZE)
    key_value_up = key_value_up_factors.reshape(-1, key_value_up_factors.shape[2])

    features = jnp.broadcast_to(residual_input.T[None], (Y, part, rows))
    features = lax.all_to_all(features, ("yh", "yl"), 0, 0, tiled=True)

    piece_rows = 2 * PIECE_TOKENS + 2 * RANK * PIECE_TOKENS // LANES
    pieces = call(
        pack_kernel,
        [shape(piece_rows, HEAD_SIZE)] * Y_HIGH,
        [SMEM, VMEM, VMEM, VMEM],
        moved=3 * 1024 * 1024,
    )(
        place,
        paged_base_keys.reshape(PIECE_TOKENS, -1),
        paged_base_values.reshape(PIECE_TOKENS, -1),
        paged_down_factors.reshape(PIECE_TOKENS, -1),
    )
    pieces = [pieces[0]] + [
        lax.ppermute(pieces[s], "yh", [(i, (i + s) % Y_HIGH) for i in range(Y_HIGH)])
        for s in range(1, Y_HIGH)
    ]

    features = jnp.broadcast_to(features.reshape(1, Y * part, rows), (X, Y * part, rows))
    features = lax.all_to_all(features, "x", 0, 0, tiled=True).reshape(X, Y, part, rows)

    message, fresh, queries_t, placing = call(
        functools.partial(project_kernel, groups),
        [
            shape(groups, 2 * capacity, HEAD_SIZE),
            shape(32, rows),
            shape(HEAD_SIZE, rows),
            shape(SLOTS, rows),
        ],
        [SMEM, SMEM] + [VMEM] * 9,
        [
            pltpu.VMEM((width, rows), BF16),
            pltpu.VMEM((width, 2 * HEAD_SIZE), BF16),
            pltpu.VMEM((HEAD_SIZE, rows), F32),
        ],
        flops=2 * width * rows * 256,
        moved=6 * 1024 * 1024,
    )(
        place,
        document_page_slots,
        features,
        query_weight,
        key_value_weight,
        shared_down_factors,
        input_norm_gain.reshape(Y * X, part),
        query_up,
        key_value_up,
        adapter_of_row.reshape(1, rows),
        document_of_row.reshape(1, rows),
    )
    fresh = lax.ppermute(
        fresh,
        ("yh", "yl"),
        [(y, 2 * y if y < Y_HIGH else 2 * (y - Y_HIGH) + 1) for y in range(Y)],
    )
    received = lax.all_to_all(message, "grp", 0, 0, tiled=True)

    message, slot_adapters = call(
        functools.partial(factor_kernel, groups),
        [shape(BLOCK, MESSAGE_ROWS, LANES), shape(8, SLOTS, dtype=F32)],
        [SMEM] + [VMEM] * 3,
        flops=2 * 256 * 256 * 128,
        moved=1024 * 1024,
    )(place, received, fresh, key_value_up)
    gathered = lax.all_to_all(message, ("yl", "x"), 0, 0, tiled=True)

    tokens = PIECE_TOKENS * Y_HIGH
    message = call(
        attend_kernel,
        shape(BLOCK, RETURN_ROWS, LANES),
        [SMEM] + [VMEM] * 7,
        [
            pltpu.VMEM((tokens, 2 * HEAD_SIZE), BF16),
            pltpu.VMEM((QUERY_ROWS + 16, tokens), BF16),
            pltpu.VMEM((2 * HEAD_SIZE, SLOTS), BF16),
            pltpu.VMEM((tokens, SLOTS), F32),
        ],
        flops=4 * SLOTS * BLOCK * tokens * 256,
        moved=3 * 1024 * 1024,
    )(place, gathered, slot_adapters, key_value_up, *pieces)
    partials = lax.all_to_all(message, ("yl", "x"), 0, 0, tiled=True)

    message = call(
        functools.partial(merge_kernel, groups),
        shape(groups, 2 * capacity, HEAD_SIZE),
        [VMEM],
        flops=SLOTS * HEAD_SIZE * 16,
        moved=1024 * 1024,
    )(partials)
    received = lax.all_to_all(message, "grp", 0, 0, tiled=True)

    return call(
        functools.partial(finish_kernel, groups),
        shape(rows, HEAD_SIZE),
        [VMEM] * 4,
        flops=2 * SLOTS * rows * 256,
        moved=1024 * 1024,
    )(received, placing, queries_t, gathered)


def solution(mesh):
    groups = mesh.devices.shape[0]
    split = Mesh(
        mesh.devices.reshape(groups, Y_HIGH, Y_LOW, X), ("grp", "yh", "yl", "x")
    )
    tp = ("yh", "yl", "x")
    in_specs = (
        P("grp", tp),
        P(),
        P(None, tp),
        P(None, tp),
        P(),
        P(None, None, tp),
        P(),
        P(("grp",) + tp, None, None),
        P(("grp",) + tp, None, None),
        P(("grp",) + tp, None, None),
        P("grp"),
        P("grp", None),
        P(),
    )
    return jax.shard_map(
        per_device, mesh=split, in_specs=in_specs, out_specs=P("grp", tp), check_vma=False
    )
```

time: 583 us -> 156 us (0.27)
  the two profiles are of different devices: /device:TPU:24 before, /device:TPU:1 now
where the time goes in v1:
time: 156 us; the launch traced here: 155 us
  waiting for transfers between devices  46.4 us (30%)
  blocking collectives  46 us (29%)
  starting transfers between devices  34.3 us (22%)
  Pallas kernels  20.1 us (13%)
  local copies, waits for them, and re-layouts  8.02 us (5%)
    ppermute x3, waiting for transfers between devices, per_device(): lax.ppermute(pieces[s], 'yh', [(i, (i + s) % Y_HIGH) for i in range(Y_HIG...  26.1 us
    all_to_all x1, blocking collectives, per_device(): features = lax.all_to_all(features, ('yh', 'yl'), 0, 0, tiled=True)  18.1 us
    all_to_all x1, blocking collectives, per_device(): received = lax.all_to_all(message, 'grp', 0, 0, tiled=True)  14.5 us
    all_to_all x1, starting transfers between devices, per_device(): received = lax.all_to_all(message, 'grp', 0, 0, tiled=True)  14.2 us
    all_to_all x1, blocking collectives, per_device(): partials = lax.all_to_all(message, ('yl', 'x'), 0, 0, tiled=True)  13.4 us
    pallas_call x1, Pallas kernels, per_device(): call(attend_kernel, shape(BLOCK, RETURN_ROWS, LANES), [SMEM] + [VMEM] * 7...  12.9 us
    all_to_all x1, waiting for transfers between devices, per_device(): lax.all_to_all(features, 'x', 0, 0, tiled=True).reshape(X, Y, part, rows)  11.8 us
    ppermute x3, starting transfers between devices, per_device(): lax.ppermute(pieces[s], 'yh', [(i, (i + s) % Y_HIGH) for i in range(Y_HIG...  10.8 us
  transfers between devices with their start and end apart: 7, of which 5 were waited for; matrix products, arithmetic and copies ran while one was open for 2% of the time, Pallas kernels for 0%

profile of v1, /device:TPU:1, one launch (start us, length us, event | category | flops | bytes accessed | tf_op | source)
XLA Modules:
  0.0 155.1 jit_solution(15623770565053456538)
XLA Ops:
  0.0 0.8 broadcast_in_dim.6
  0.8 18.1 %all_to_all.30 = bf16[8,160,128]{2,1,0:T(8,128)(2,1)S(1)} all-to-all(bf16[8,160,128]{2,1,0:T(8,128)(2,1)S(1)} %broadcast_in_dim.6), channel_id=1, replica_groups=mesh['grp'=16,'yh'=4,'yl'=2,'x'=4] {'yh','yl'}, dimensions={0} | all-to-all | bytes 655360 | tf_op jit(solution)/shard_map/all_to_all | solution.py:329
  19.0 1.2 broadcast_in_dim.15
  20.2 5.1 %all-to-all-start.1 = ((bf16[4,1280,128]{2,1,0:T(8,128)(2,1)}), bf16[4,1280,128]{2,1,0:T(8,128)(2,1)S(1)}, u32[]{:S(2)}, u32[]{:S(2)}) async-start(bf16[4,1280,128]{2,1,0:T(8,128)(2,1)} %broadcast_in_dim.15), calls=%async_computation.1 | async-start | bytes 2621440 | tf_op jit(solution)/shard_map/all_to_all | solution.py:349
  25.3 1.4 copy.14.key_value_weight
  26.7 0.0 copy-start.8
  26.7 1.7 %copy.15.down = bf16[5120,48]{1,0:T(8,128)(2,1)S(1)} copy(bf16[5120,48]{0,1:T(8,128)(2,1)} %param.17) | data formatting | bytes 983040 | tf_op args[4]
  28.5 0.1 reshape.31.gain
  28.5 0.1 pad_add_fusion.place
  28.6 11.8 %all-to-all-done.1 = bf16[4,1280,128]{2,1,0:T(8,128)(2,1)S(1)} async-done(((bf16[4,1280,128]{2,1,0:T(8,128)(2,1)}), bf16[4,1280,128]{2,1,0:T(8,128)(2,1)S(1)}, u32[]{:S(2)}, u32[]{:S(2)}) %all-to-all-start.1) | async-done | bytes 1310752 | tf_op jit(solution)/shard_map/all_to_all | solution.py:349
  40.5 1.3 copy-done
  41.8 1.3 copy-done.2
  43.1 3.7 %shard_map.127 = (bf16[16,32,128]{2,1,0:T(8,128)(2,1)}, bf16[32,128]{1,0:T(8,128)(2,1)S(1)}, bf16[128,128]{1,0:T(8,128)(2,1)S(1)}, bf16[256,128]{1,0:T(8,128)(2,1)S(1)}) custom-call(s32[2]{0:T(128)S(1)} %pad_add_fusion.place, s32[16,128]{1,0:T(8,128)S(1)} %copy-done.6, bf16[4,8,160,128]{3,2,1,0:T(8,128)(2,1)S(1)} %bitcast.12, ...), custom_call_target="tpu_custom_call" | custom-call | flops 335544320 | bytes 6291456 | tf_op jit(solution)/shard_map/pallas_call | solution.py:351
  46.8 14.2 %all-to-all-start.2 = ((bf16[16,32,128]{2,1,0:T(8,128)(2,1)}), bf16[16,32,128]{2,1,0:T(8,128)(2,1)S(1)}, u32[]{:S(2)}, u32[]{:S(2)}) async-start(bf16[16,32,128]{2,1,0:T(8,128)(2,1)} %get-tuple-element.15), calls=%async_computation.2 | async-start | bytes 262144 | tf_op jit(solution)/shard_map/all_to_all | solution.py:385
  61.1 0.6 collective-permute-start
  61.7 0.0 collective-permute-done.fresh
  61.7 8.5 %all-to-all-done.2.received = bf16[16,32,128]{2,1,0:T(8,128)(2,1)S(1)} async-done(((bf16[16,32,128]{2,1,0:T(8,128)(2,1)}), bf16[16,32,128]{2,1,0:T(8,128)(2,1)S(1)}, u32[]{:S(2)}, u32[]{:S(2)}) %all-to-all-start.2) | async-done | bytes 131104 | tf_op jit(solution)/shard_map/all_to_all | solution.py:385
  70.2 1.6 %shard_map.128 = (bf16[8,320,128]{2,1,0:T(8,128)(2,1)}, f32[8,256]{1,0:T(8,128)S(1)}) custom-call(s32[2]{0:T(128)S(1)} %pad_add_fusion.place, bf16[16,32,128]{2,1,0:T(8,128)(2,1)S(1)} %all-to-all-done.2.received, bf16[32,128]{1,0:T(8,128)(2,1)S(1)} %collective-permute-done.fresh, bf16[256,1024]{1,0:T(8,128)(2,1)S(1)} %bitcast.14), custom_call_target="tpu_custom_call" | custom-call | flops 16777216 | bytes 1048576 | tf_op jit(solution)/shard_map/pallas_call | solution.py:387
  71.8 3.5 %all-to-all-start.3 = ((bf16[8,320,128]{2,1,0:T(8,128)(2,1)}), bf16[8,320,128]{2,1,0:T(8,128)(2,1)S(1)}, u32[]{:S(2)}, u32[]{:S(2)}) async-start(bf16[8,320,128]{2,1,0:T(8,128)(2,1)} %get-tuple-element.17), calls=%async_computation.3 | async-start | bytes 1310720 | tf_op jit(solution)/shard_map/all_to_all | solution.py:394
  75.4 0.1 copy.16
  75.5 0.7 shard_map.129
  76.3 1.9 %collective-permute-start.1 = (bf16[1152,128]{1,0:T(8,128)(2,1)S(1)}, bf16[1152,128]{1,0:T(8,128)(2,1)S(1)}, u32[]{:S(2)}, u32[]{:S(2)}) collective-permute-start(bf16[1152,128]{1,0:T(8,128)(2,1)S(1)} %get-tuple-element.20), channel_id=1, source_target_pairs={{0,8},{8,16},{16,24},{24,0},{1,9},{9,17},{17,25},{25,1},{2,10},{10... | collective-permute-start | bytes 884744 | tf_op jit(solution)/shard_map/ppermute | solution.py:344
  78.2 5.7 %collective-permute-start.2 = (bf16[1152,128]{1,0:T(8,128)(2,1)S(1)}, bf16[1152,128]{1,0:T(8,128)(2,1)S(1)}, u32[]{:S(2)}, u32[]{:S(2)}) collective-permute-start(bf16[1152,128]{1,0:T(8,128)(2,1)S(1)} %get-tuple-element.21), channel_id=1, source_target_pairs={{0,16},{8,24},{16,0},{24,8},{1,17},{9,25},{17,1},{25,9},{2,18},{10... | collective-permute-start | bytes 884744 | tf_op jit(solution)/shard_map/ppermute | solution.py:344
  84.0 3.1 %collective-permute-start.3 = (bf16[1152,128]{1,0:T(8,128)(2,1)S(1)}, bf16[1152,128]{1,0:T(8,128)(2,1)S(1)}, u32[]{:S(2)}, u32[]{:S(2)}) collective-permute-start(bf16[1152,128]{1,0:T(8,128)(2,1)S(1)} %get-tuple-element.22), channel_id=1, source_target_pairs={{0,24},{8,0},{16,8},{24,16},{1,25},{9,1},{17,9},{25,17},{2,26},{10... | collective-permute-start | bytes 884744 | tf_op jit(solution)/shard_map/ppermute | solution.py:344
  87.1 12.7 %collective-permute-done.1.piece_1 = bf16[1152,128]{1,0:T(8,128)(2,1)S(1)} collective-permute-done((bf16[1152,128]{1,0:T(8,128)(2,1)S(1)}, bf16[1152,128]{1,0:T(8,128)(2,1)S(1)}, u32[]{:S(2)}, u32[]{:S(2)}) %collective-permute-start.1) | collective-permute-done | bytes 294944 | tf_op jit(solution)/shard_map/ppermute | solution.py:344
  99.8 8.5 %collective-permute-done.2.piece_2 = bf16[1152,128]{1,0:T(8,128)(2,1)S(1)} collective-permute-done((bf16[1152,128]{1,0:T(8,128)(2,1)S(1)}, bf16[1152,128]{1,0:T(8,128)(2,1)S(1)}, u32[]{:S(2)}, u32[]{:S(2)}) %collective-permute-start.2) | collective-permute-done | bytes 294944 | tf_op jit(solution)/shard_map/ppermute | solution.py:344
  108.4 4.8 %collective-permute-done.3.piece_3 = bf16[1152,128]{1,0:T(8,128)(2,1)S(1)} collective-permute-done((bf16[1152,128]{1,0:T(8,128)(2,1)S(1)}, bf16[1152,128]{1,0:T(8,128)(2,1)S(1)}, u32[]{:S(2)}, u32[]{:S(2)}) %collective-permute-start.3) | collective-permute-done | bytes 294944 | tf_op jit(solution)/shard_map/ppermute | solution.py:344
  113.2 12.9 %shard_map.130 = bf16[8,272,128]{2,1,0:T(8,128)(2,1)S(1)} custom-call(s32[2]{0:T(128)S(1)} %pad_add_fusion.place, bf16[8,320,128]{2,1,0:T(8,128)(2,1)S(1)} %all-to-all-done.3.queries.gathered, f32[8,256]{1,0:T(8,128)S(1)} %get-tuple-element.18.slot_adapters, bf16[256,1024]{1,0:T(8,128)(2,1)S(1)} %bitcast.15, ...), custom_call_target="tpu_custom_call" | custom-call | flops 4294967296 | bytes 3145728 | tf_op jit(solution)/shard_map/pallas_call | solution.py:397
  126.1 13.4 %all_to_all.31.partials = bf16[8,272,128]{2,1,0:T(8,128)(2,1)S(1)} all-to-all(bf16[8,272,128]{2,1,0:T(8,128)(2,1)S(1)} %shard_map.130), channel_id=1, replica_groups=mesh['grp'=16,'yh'=4,'yl'=2,'x'=4] {'yl','x'}, dimensions={0} | all-to-all | bytes 1114112 | tf_op jit(solution)/shard_map/all_to_all | solution.py:410
  139.4 0.2 shard_map.131
  139.6 14.5 %all_to_all.32.received = bf16[16,32,128]{2,1,0:T(8,128)(2,1)S(1)} all-to-all(bf16[16,32,128]{2,1,0:T(8,128)(2,1)S(1)} %shard_map.131), channel_id=1, replica_groups=mesh['grp'=16,'yh'=4,'yl'=2,'x'=4] {'grp'}, dimensions={0} | all-to-all | bytes 262144 | tf_op jit(solution)/shard_map/all_to_all | solution.py:419
  154.1 0.9 shard_map.132
  (22 shorter events, 0.0 us)
Async XLA Ops:
  20.2 5.1 %copy-start.9 = (bf16[5120,32]{0,1:T(8,128)(2,1)S(1)}, bf16[5120,32]{0,1:T(8,128)(2,1)}, u32[]{:S(2)}) copy-start(bf16[5120,32]{0,1:T(8,128)(2,1)} %param.16) | copy-start | bytes 983044
  20.2 20.2 %all-to-all-start.1 = ((bf16[4,1280,128]{2,1,0:T(8,128)(2,1)}), bf16[4,1280,128]{2,1,0:T(8,128)(2,1)S(1)}, u32[]{:S(2)}, u32[]{:S(2)}) async-start(bf16[4,1280,128]{2,1,0:T(8,128)(2,1)} %broadcast_in_dim.15), calls=%async_computation.1 | async-start | bytes 2621440 | tf_op jit(solution)/shard_map/all_to_all | solution.py:349
  25.3 3.1 %copy-start.11 = (f32[5120]{0:T(1024)S(1)}, f32[5120]{0:T(1024)}, u32[]{:S(2)}) copy-start(f32[5120]{0:T(1024)} %param.14) | copy-start | bytes 61444
  26.7 13.7 %copy-start.1 = (bf16[16,16,1024]{2,1,0:T(8,128)(2,1)S(1)}, bf16[16,16,1024]{2,1,0:T(8,128)(2,1)}, u32[]{:S(2)}) copy-start(bf16[16,16,1024]{2,1,0:T(8,128)(2,1)} %param.19) | copy-start | bytes 1572868
  26.7 13.7 %copy-start.5 = (bf16[16,16,128]{2,1,0:T(8,128)(2,1)S(1)}, bf16[16,16,128]{2,1,0:T(8,128)(2,1)}, u32[]{:S(2)}) copy-start(bf16[16,16,128]{2,1,0:T(8,128)(2,1)} %param.18) | copy-start | bytes 196612
  26.7 13.7 %copy-start.6 = (s32[16,128]{1,0:T(8,128)S(1)}, s32[16,128]{1,0:T(8,128)}, u32[]{:S(2)}) copy-start(s32[16,128]{1,0:T(8,128)} %page_slots.1) | copy-start | bytes 24580
  26.7 13.7 %copy-start.7 = (s32[128]{0:T(128)S(1)}, s32[128]{0:T(128)}, u32[]{:S(2)}) copy-start(s32[128]{0:T(128)} %param.23) | copy-start | bytes 1540
  26.7 13.7 %copy-start.8 = (s32[128,1]{0,1:T(1,128)S(1)}, s32[128,1]{0,1:T(1,128)}, u32[]{:S(2)}) copy-start(s32[128,1]{0,1:T(1,128)} %param.24) | copy-start | bytes 1540
  40.4 1.3 copy-start
  41.8 1.3 copy-start.2
  46.8 28.6 %copy-start.10 = (bf16[4,128,32]{1,2,0:T(8,128)(2,1)S(1)}, bf16[4,128,32]{1,2,0:T(8,128)(2,1)}, u32[]{:S(2)}) copy-start(bf16[4,128,32]{1,2,0:T(8,128)(2,1)} %param.22) | copy-start | bytes 98308
  46.8 28.7 %copy-start.3 = (bf16[4,128,512]{2,1,0:T(8,128)(2,1)S(1)}, bf16[4,128,512]{2,1,0:T(8,128)(2,1)}, u32[]{:S(2)}) copy-start(bf16[4,128,512]{2,1,0:T(8,128)(2,1)} %param.20) | copy-start | bytes 1572868
  46.8 28.7 %copy-start.4 = (bf16[4,128,512]{2,1,0:T(8,128)(2,1)S(1)}, bf16[4,128,512]{2,1,0:T(8,128)(2,1)}, u32[]{:S(2)}) copy-start(bf16[4,128,512]{2,1,0:T(8,128)(2,1)} %param.21) | copy-start | bytes 1572868
  46.8 23.4 %all-to-all-start.2 = ((bf16[16,32,128]{2,1,0:T(8,128)(2,1)}), bf16[16,32,128]{2,1,0:T(8,128)(2,1)S(1)}, u32[]{:S(2)}, u32[]{:S(2)}) async-start(bf16[16,32,128]{2,1,0:T(8,128)(2,1)} %get-tuple-element.15), calls=%async_computation.2 | async-start | bytes 262144 | tf_op jit(solution)/shard_map/all_to_all | solution.py:385
  61.1 0.7 collective-permute-start
  71.8 41.3 %all-to-all-start.3 = ((bf16[8,320,128]{2,1,0:T(8,128)(2,1)}), bf16[8,320,128]{2,1,0:T(8,128)(2,1)S(1)}, u32[]{:S(2)}, u32[]{:S(2)}) async-start(bf16[8,320,128]{2,1,0:T(8,128)(2,1)} %get-tuple-element.17), calls=%async_computation.3 | async-start | bytes 1310720 | tf_op jit(solution)/shard_map/all_to_all | solution.py:394
  76.3 23.5 %collective-permute-start.1 = (bf16[1152,128]{1,0:T(8,128)(2,1)S(1)}, bf16[1152,128]{1,0:T(8,128)(2,1)S(1)}, u32[]{:S(2)}, u32[]{:S(2)}) collective-permute-start(bf16[1152,128]{1,0:T(8,128)(2,1)S(1)} %get-tuple-element.20), channel_id=1, source_target_pairs={{0,8},{8,16},{16,24},{24,0},{1,9},{9,17},{17,25},{25,1},{2,10},{10... | collective-permute-start | bytes 884744 | tf_op jit(solution)/shard_map/ppermute | solution.py:344
  78.2 30.2 %collective-permute-start.2 = (bf16[1152,128]{1,0:T(8,128)(2,1)S(1)}, bf16[1152,128]{1,0:T(8,128)(2,1)S(1)}, u32[]{:S(2)}, u32[]{:S(2)}) collective-permute-start(bf16[1152,128]{1,0:T(8,128)(2,1)S(1)} %get-tuple-element.21), channel_id=1, source_target_pairs={{0,16},{8,24},{16,0},{24,8},{1,17},{9,25},{17,1},{25,9},{2,18},{10... | collective-permute-start | bytes 884744 | tf_op jit(solution)/shard_map/ppermute | solution.py:344
  84.0 29.2 %collective-permute-start.3 = (bf16[1152,128]{1,0:T(8,128)(2,1)S(1)}, bf16[1152,128]{1,0:T(8,128)(2,1)S(1)}, u32[]{:S(2)}, u32[]{:S(2)}) collective-permute-start(bf16[1152,128]{1,0:T(8,128)(2,1)S(1)} %get-tuple-element.22), channel_id=1, source_target_pairs={{0,24},{8,0},{16,8},{24,16},{1,25},{9,1},{17,9},{25,17},{2,26},{10... | collective-permute-start | bytes 884744 | tf_op jit(solution)/shard_map/ppermute | solution.py:344

commit v2 on v1

--- a/solution.py
+++ b/solution.py
@@ -20,6 +20,7 @@
 MESSAGE_ROWS = TILES * QUERY_ROWS + 32
 RETURN_ROWS = TILES * HEAD_SIZE + 16
 PIECE_TOKENS = 512
+PIECES = ((0, 0, 512), (1, 0, 512), (3, 0, 512), (2, 0, 256), (2, 256, 256))
 SCORE_SCALE = HEAD_SIZE**-0.5
 F32 = jnp.float32
 BF16 = jnp.bfloat16
@@ -63,15 +64,13 @@
 
 def pack_kernel(place, keys, values, factors, *pieces):
     own = place[1]
-    factors_t = factors[...].astype(F32).T.astype(BF16)
-    for shift, piece in enumerate(pieces):
+    for (shift, start, count), piece in zip(PIECES, pieces):
         head = lax.rem(own + shift, Y_HIGH)
         columns = pl.ds(pl.multiple_of(head * HEAD_SIZE, HEAD_SIZE), HEAD_SIZE)
-        piece[0:PIECE_TOKENS, :] = keys[:, columns]
-        piece[PIECE_TOKENS : 2 * PIECE_TOKENS, :] = values[:, columns]
-        for page in range(PIECE_TOKENS // LANES):
-            start = 2 * PIECE_TOKENS + page * 2 * RANK
-            piece[start : start + 2 * RANK, :] = factors_t[:, page * LANES : (page + 1) * LANES]
+        piece[0:count, :] = keys[start : start + count, columns]
+        piece[count : 2 * count, :] = values[start : start + count, columns]
+        first = start // LANES * 2 * RANK
+        piece[2 * count :, :] = factors[first : first + count // LANES * 2 * RANK, :]
 
 
 def project_kernel(
@@ -112,16 +111,15 @@
             t = y * X + x
             block = features[x, y].astype(F32) * scale * gain_t[:, t : t + 1]
             normed[t * part : (t + 1) * part, :] = block.astype(BF16)
-    weights[:, 0:HEAD_SIZE] = query_weight[...]
-    weights[:, HEAD_SIZE:] = jnp.concatenate(
-        [key_value_weight[...], down[...], jnp.zeros((width, HEAD_SIZE - 80), BF16)], axis=1
-    )
-    total = dot(normed[...], weights[...], 0, 0).T
+    weights[0:32, :] = key_value_weight[...]
+    weights[32:, :] = down[...]
+    query_total = dot(query_weight[...], normed[...], 0, 0)
+    total = dot(weights[...], normed[...], 1, 0)
 
     adapter = adapters[...]
-    low = total[HEAD_SIZE + 32 : HEAD_SIZE + 80].astype(BF16)
+    low = total[32:].astype(BF16)
     query_update = dot(query_up[...], of_adapter(low[0:RANK], adapter), 0, 0)
-    queries = (total[0:HEAD_SIZE] + query_update).astype(BF16)
+    queries = (query_total + query_update).astype(BF16)
     queries_t[...] = queries
 
     is_key = device < Y * X // 2
@@ -129,7 +127,7 @@
     columns = pl.ds(pl.multiple_of(device // X * HEAD_SIZE, HEAD_SIZE), HEAD_SIZE)
     update[...] = dot(key_value_up[:, columns], of_adapter(low_kv, adapter), 0, 0)
     mine = pl.ds(pl.multiple_of(lax.rem(device, X) * 32, 32), 32)
-    fresh[...] = (total[HEAD_SIZE : HEAD_SIZE + 32] + update[mine, :]).astype(BF16)
+    fresh[...] = (total[0:32] + update[mine, :]).astype(BF16)
 
     document = documents[...]
     target = jnp.zeros_like(document)
@@ -181,65 +179,58 @@
         message[member, TILES * QUERY_ROWS :, :] = new
 
 
-def attend_kernel(
-    place,
-    queries,
-    slot_adapters,
-    key_value_up,
-    piece_0,
-    piece_1,
-    piece_2,
-    piece_3,
-    message,
-    keys,
-    values_t,
-    query,
-    scores,
-):
-    pieces = (piece_0, piece_1, piece_2, piece_3)
-    tokens = PIECE_TOKENS * len(pieces)
-    depth = 2 * HEAD_SIZE
-    value_rows = values_t.shape[0]
-    ones = (
-        lax.broadcasted_iota(jnp.int32, (value_rows - QUERY_ROWS, tokens), 0) == 0
-    ).astype(F32)
-    values_t[QUERY_ROWS:, :] = ones.astype(BF16)
-    for index, piece in enumerate(pieces):
-        for page in range(PIECE_TOKENS // LANES):
+def prepare_kernel(*refs):
+    pieces, (keys, values_t) = refs[:-2], refs[-2:]
+    tokens = keys.shape[0]
+    ones = lax.broadcasted_iota(jnp.int32, (values_t.shape[0] - QUERY_ROWS, tokens), 0) == 0
+    values_t[QUERY_ROWS:, :] = ones.astype(F32).astype(BF16)
+    base = 0
+    for (_, _, count), piece in zip(PIECES, pieces):
+        for page in range(count // LANES):
             start = page * LANES
-            here = slice(index * PIECE_TOKENS + start, index * PIECE_TOKENS + start + LANES)
-            row = 2 * PIECE_TOKENS + page * 2 * RANK
+            here = slice(base + start, base + start + LANES)
+            row = 2 * count + page * 2 * RANK
             factors = piece[row : row + 2 * RANK, :]
             key_factors = jnp.concatenate(
                 [factors[0:RANK].astype(F32), jnp.zeros((LANES - RANK, LANES), F32)], axis=0
             )
             keys[here, 0:HEAD_SIZE] = piece[start : start + LANES, :]
             keys[here, HEAD_SIZE:] = key_factors.T.astype(BF16)
-            value = piece[PIECE_TOKENS + start : PIECE_TOKENS + start + LANES, :]
+            value = piece[count + start : count + start + LANES, :]
             values_t[0:HEAD_SIZE, here] = value.astype(F32).T.astype(BF16)
             values_t[HEAD_SIZE:QUERY_ROWS, here] = factors[RANK:]
-    query[QUERY_ROWS:, :] = jnp.zeros((depth - QUERY_ROWS, SLOTS), BF16)
-
+        base += count
+
+
+def attend_kernel(
+    place, queries, slot_adapters, key_value_up, keys, values_t, message, query, scores
+):
+    tokens = keys.shape[0]
+    depth = 2 * HEAD_SIZE
+    value_rows = values_t.shape[0]
+    query[:, QUERY_ROWS:, :] = jnp.zeros((2, depth - QUERY_ROWS, SLOTS), BF16)
     columns = pl.ds(pl.multiple_of((place[1] + Y_HIGH) * HEAD_SIZE, HEAD_SIZE), HEAD_SIZE)
     value_up = key_value_up[:, columns]
     adapters = slot_adapters[0:1, :].astype(jnp.int32)
     chunk = 512
 
-    def one_head(head, carry):
+    def score_head(head, side):
         for tile in range(TILES):
-            query[0:QUERY_ROWS, tile * LANES : (tile + 1) * LANES] = queries[
+            query[side, 0:QUERY_ROWS, tile * LANES : (tile + 1) * LANES] = queries[
                 head, tile * QUERY_ROWS : (tile + 1) * QUERY_ROWS, :
             ]
         highest = None
         for start in range(0, tokens, chunk):
-            score = dot(keys[start : start + chunk, :], query[...], 1, 0)
-            scores[start : start + chunk, :] = score
+            score = dot(keys[start : start + chunk, :], query[side], 1, 0)
+            scores[side, start : start + chunk, :] = score
             top = jnp.max(score.reshape(chunk // 8, 8, SLOTS), axis=0)
             highest = top if highest is None else jnp.maximum(highest, top)
-        peak = jnp.max(highest, axis=0, keepdims=True)
+        return jnp.max(highest, axis=0, keepdims=True)
+
+    def sum_head(head, side, peak):
         total = jnp.zeros((value_rows, SLOTS), F32)
         for start in range(0, tokens, chunk):
-            shifted = scores[start : start + chunk, :] - peak
+            shifted = scores[side, start : start + chunk, :] - peak
             weight = jnp.exp2(shifted * (SCORE_SCALE * math.log2(math.e))).astype(BF16)
             total = total + dot(values_t[:, start : start + chunk], weight, 1, 0)
         mass = total[QUERY_ROWS : QUERY_ROWS + 1]
@@ -247,8 +238,7 @@
         low = (total[HEAD_SIZE:QUERY_ROWS] * inverse).astype(BF16)
         shift = dot(value_up, of_adapter(low, adapters), 0, 0)
         result = (total[0:HEAD_SIZE] * inverse + shift).astype(BF16)
-        log_mass = peak * SCORE_SCALE + jnp.log(mass)
-        parts = split_float(log_mass)
+        parts = split_float(peak * SCORE_SCALE + jnp.log(mass))
         stats = [part[:, tile * LANES : (tile + 1) * LANES] for tile in range(TILES) for part in parts]
         stats = jnp.concatenate(stats + [jnp.zeros((16 - len(stats), LANES), F32)], axis=0)
         for tile in range(TILES):
@@ -256,9 +246,15 @@
                 :, tile * LANES : (tile + 1) * LANES
             ]
         message[head, TILES * HEAD_SIZE :, :] = stats.astype(BF16)
+
+    def two_heads(pair, carry):
+        first = score_head(2 * pair, 0)
+        second = score_head(2 * pair + 1, 1)
+        sum_head(2 * pair, 0, first)
+        sum_head(2 * pair + 1, 1, second)
         return carry
 
-    lax.fori_loop(0, BLOCK, one_head, 0)
+    lax.fori_loop(0, BLOCK // 2, two_heads, 0)
 
 
 def merge_kernel(groups, partials, message):
@@ -298,6 +294,10 @@
     own_weight = jnp.exp(own - peak)
     result = (shared * shared_weight + value * own_weight) / (shared_weight + own_weight)
     out[...] = result.T.astype(BF16)
+
+
+def send(value, shift):
+    return lax.ppermute(value, "yh", [(i, (i + shift) % Y_HIGH) for i in range(Y_HIGH)])
 
 
 def per_device(
@@ -326,25 +326,22 @@
     key_value_up = key_value_up_factors.reshape(-1, key_value_up_factors.shape[2])
 
     features = jnp.broadcast_to(residual_input.T[None], (Y, part, rows))
-    features = lax.all_to_all(features, ("yh", "yl"), 0, 0, tiled=True)
-
-    piece_rows = 2 * PIECE_TOKENS + 2 * RANK * PIECE_TOKENS // LANES
     pieces = call(
         pack_kernel,
-        [shape(piece_rows, HEAD_SIZE)] * Y_HIGH,
+        [shape(2 * n + 2 * RANK * n // LANES, HEAD_SIZE) for _, _, n in PIECES],
         [SMEM, VMEM, VMEM, VMEM],
         moved=3 * 1024 * 1024,
     )(
         place,
         paged_base_keys.reshape(PIECE_TOKENS, -1),
         paged_base_values.reshape(PIECE_TOKENS, -1),
-        paged_down_factors.reshape(PIECE_TOKENS, -1),
-    )
-    pieces = [pieces[0]] + [
-        lax.ppermute(pieces[s], "yh", [(i, (i + s) % Y_HIGH) for i in range(Y_HIGH)])
-        for s in range(1, Y_HIGH)
-    ]
-
+        paged_down_factors.transpose(0, 2, 1).reshape(-1, LANES),
+    )
+    features, pieces = lax.optimization_barrier((features, pieces))
+    own, right, left, far_right, far_left = pieces
+    right, left = send(right, 1), send(left, -1)
+    far_right, far_left = send(far_right, 1), send(far_left, -1)
+    features = lax.all_to_all(features, ("yh", "yl"), 0, 0, tiled=True)
     features = jnp.broadcast_to(features.reshape(1, Y * part, rows), (X, Y * part, rows))
     features = lax.all_to_all(features, "x", 0, 0, tiled=True).reshape(X, Y, part, rows)
 
@@ -359,7 +356,7 @@
         [SMEM, SMEM] + [VMEM] * 9,
         [
             pltpu.VMEM((width, rows), BF16),
-            pltpu.VMEM((width, 2 * HEAD_SIZE), BF16),
+            pltpu.VMEM((32 + 3 * RANK, width), BF16),
             pltpu.VMEM((HEAD_SIZE, rows), F32),
         ],
         flops=2 * width * rows * 256,
@@ -369,8 +366,8 @@
         document_page_slots,
         features,
         query_weight,
-        key_value_weight,
-        shared_down_factors,
+        key_value_weight.T,
+        shared_down_factors.T,
         input_norm_gain.reshape(Y * X, part),
         query_up,
         key_value_up,
@@ -382,6 +379,10 @@
         ("yh", "yl"),
         [(y, 2 * y if y < Y_HIGH else 2 * (y - Y_HIGH) + 1) for y in range(Y)],
     )
+    message, right, left, far_right, far_left = lax.optimization_barrier(
+        (message, right, left, far_right, far_left)
+    )
+    far_right, far_left = send(far_right, 1), send(far_left, -1)
     received = lax.all_to_all(message, "grp", 0, 0, tiled=True)
 
     message, slot_adapters = call(
@@ -391,22 +392,28 @@
         flops=2 * 256 * 256 * 128,
         moved=1024 * 1024,
     )(place, received, fresh, key_value_up)
+    message, far_right, far_left = lax.optimization_barrier((message, far_right, far_left))
+    pieces = (own, right, left, far_right, far_left)
     gathered = lax.all_to_all(message, ("yl", "x"), 0, 0, tiled=True)
 
     tokens = PIECE_TOKENS * Y_HIGH
+    keys, values_t = call(
+        prepare_kernel,
+        [shape(tokens, 2 * HEAD_SIZE), shape(QUERY_ROWS + 16, tokens)],
+        [VMEM] * len(pieces),
+        moved=3 * 1024 * 1024,
+    )(*pieces)
     message = call(
         attend_kernel,
         shape(BLOCK, RETURN_ROWS, LANES),
-        [SMEM] + [VMEM] * 7,
+        [SMEM] + [VMEM] * 5,
         [
-            pltpu.VMEM((tokens, 2 * HEAD_SIZE), BF16),
-            pltpu.VMEM((QUERY_ROWS + 16, tokens), BF16),
-            pltpu.VMEM((2 * HEAD_SIZE, SLOTS), BF16),
-            pltpu.VMEM((tokens, SLOTS), F32),
+            pltpu.VMEM((2, 2 * HEAD_SIZE, SLOTS), BF16),
+            pltpu.VMEM((2, tokens, SLOTS), F32),
         ],
         flops=4 * SLOTS * BLOCK * tokens * 256,
         moved=3 * 1024 * 1024,
-    )(place, gathered, slot_adapters, key_value_up, *pieces)
+    )(place, gathered, slot_adapters, key_value_up, keys, values_t)
     partials = lax.all_to_all(message, ("yl", "x"), 0, 0, tiled=True)
 
     message = call(

time: 156 us -> 144 us (0.923)
  waiting for transfers between devices: 46.4 us -> 14.5 us
  starting transfers between devices: 34.3 us -> 50 us
  blocking collectives: 46 us -> 51.2 us
  Pallas kernels: 20.1 us -> 17.3 us
  local copies, waits for them, and re-layouts: 8.02 us -> 10.1 us
    ppermute x3 -> x6, waiting for transfers between devices: 26.1 us -> 7.1 us  [send(): lax.ppermute(value, 'yh', [(i, (i + shift) % Y_HIGH) for i in range(Y_HIG...]
    ppermute x3 -> x6, starting transfers between devices: 10.8 us -> 23 us  [send(): lax.ppermute(value, 'yh', [(i, (i + shift) % Y_HIGH) for i in range(Y_HIG...]
    all_to_all x1, waiting for transfers between devices: 11.8 us -> 0.3 us  [per_device(): lax.all_to_all(features, 'x', 0, 0, tiled=True).reshape(X, Y, part, rows)]
    all_to_all x1, waiting for transfers between devices: 8.5 us -> 0.01 us  [per_device(): received = lax.all_to_all(message, 'grp', 0, 0, tiled=True)]
    all_to_all x1, waiting for transfers between devices: 0.01 us -> 7.1 us  [per_device(): gathered = lax.all_to_all(message, ('yl', 'x'), 0, 0, tiled=True)]
    all_to_all x1, starting transfers between devices: 3.54 us -> 8.28 us  [per_device(): gathered = lax.all_to_all(message, ('yl', 'x'), 0, 0, tiled=True)]
    all_to_all x1, blocking collectives: 14.5 us -> 17.8 us  [per_device(): received = lax.all_to_all(message, 'grp', 0, 0, tiled=True)]
    unnamed x27 -> x44, local copies, waits for them, and re-layouts: 5.9 us -> 7.92 us
  transfers between devices with their start and end apart: 7 -> 10, of which waited for: 5 -> 5; matrix products, arithmetic and copies ran while one was open for 2% -> 0% of each run, Pallas kernels for 0% -> 4%
where the time goes in v2:
time: 144 us; the launch traced here: 143 us
  blocking collectives  51.2 us (36%)
  starting transfers between devices  50 us (35%)
  Pallas kernels  17.3 us (12%)
  waiting for transfers between devices  14.5 us (10%)
  local copies, waits for them, and re-layouts  10.1 us (7%)
    ppermute x6, starting transfers between devices, send(): lax.ppermute(value, 'yh', [(i, (i + shift) % Y_HIGH) for i in range(Y_HIG...  23 us
    all_to_all x1, blocking collectives, per_device(): features = lax.all_to_all(features, ('yh', 'yl'), 0, 0, tiled=True)  18.1 us
    all_to_all x1, blocking collectives, per_device(): received = lax.all_to_all(message, 'grp', 0, 0, tiled=True)  17.8 us
    all_to_all x1, blocking collectives, per_device(): partials = lax.all_to_all(message, ('yl', 'x'), 0, 0, tiled=True)  15.3 us
    all_to_all x1, starting transfers between devices, per_device(): received = lax.all_to_all(message, 'grp', 0, 0, tiled=True)  12.2 us
    pallas_call x1, Pallas kernels, per_device(): call(attend_kernel, shape(BLOCK, RETURN_ROWS, LANES), [SMEM] + [VMEM] * 5...  9.55 us
    all_to_all x1, starting transfers between devices, per_device(): gathered = lax.all_to_all(message, ('yl', 'x'), 0, 0, tiled=True)  8.28 us
    unnamed x44, local copies, waits for them, and re-layouts  7.92 us
  transfers between devices with their start and end apart: 10, of which 5 were waited for; matrix products, arithmetic and copies ran while one was open for 0% of the time, Pallas kernels for 4%

profile of v2, /device:TPU:1, one launch (start us, length us, event | category | flops | bytes accessed | tf_op | source)
XLA Modules:
  0.0 143.4 jit_solution(16775233994340779733)
XLA Ops:
  0.1 1.0 copy-done.2
  1.1 1.0 copy-done.3
  2.2 0.8 copy-done.12
  2.9 0.7 shard_map.127
  3.7 0.7 copy-done.19
  4.4 0.9 broadcast_in_dim.6
  5.2 18.1 %all_to_all.30 = bf16[8,160,128]{2,1,0:T(8,128)(2,1)S(1)} all-to-all(bf16[8,160,128]{2,1,0:T(8,128)(2,1)S(1)} %broadcast_in_dim.6), channel_id=1, replica_groups=mesh['grp'=16,'yh'=4,'yl'=2,'x'=4] {'yh','yl'}, dimensions={0} | all-to-all | bytes 655360 | tf_op jit(solution)/shard_map/all_to_all | solution.py:344
  23.4 1.2 broadcast_in_dim.15
  24.7 5.1 %all-to-all-start.1 = ((bf16[4,1280,128]{2,1,0:T(8,128)(2,1)}), bf16[4,1280,128]{2,1,0:T(8,128)(2,1)S(1)}, u32[]{:S(2)}, u32[]{:S(2)}) async-start(bf16[4,1280,128]{2,1,0:T(8,128)(2,1)} %broadcast_in_dim.15), calls=%async_computation.1 | async-start | bytes 2621440 | tf_op jit(solution)/shard_map/all_to_all | solution.py:346
  29.8 1.9 %collective-permute-start = (bf16[1152,128]{1,0:T(8,128)(2,1)}, bf16[1152,128]{1,0:T(8,128)(2,1)}, u32[]{:S(2)}, u32[]{:S(2)}) collective-permute-start(bf16[1152,128]{1,0:T(8,128)(2,1)} %copy-done.17), channel_id=1, source_target_pairs={{0,8},{8,16},{16,24},{24,0},{1,9},{9,17},{17,25},{25,1},{2,10},{10... | collective-permute-start | bytes 884744 | tf_op jit(solution)/shard_map/ppermute | solution.py:300
  31.7 5.5 %collective-permute-start.1 = (bf16[1152,128]{1,0:T(8,128)(2,1)}, bf16[1152,128]{1,0:T(8,128)(2,1)}, u32[]{:S(2)}, u32[]{:S(2)}) collective-permute-start(bf16[1152,128]{1,0:T(8,128)(2,1)} %copy-done.16), channel_id=1, source_target_pairs={{0,24},{8,0},{16,8},{24,16},{1,25},{9,1},{17,9},{25,17},{2,26},{10... | collective-permute-start | bytes 884744 | tf_op jit(solution)/shard_map/ppermute | solution.py:300
  37.2 1.9 %collective-permute-start.2 = (bf16[576,128]{1,0:T(8,128)(2,1)}, bf16[576,128]{1,0:T(8,128)(2,1)}, u32[]{:S(2)}, u32[]{:S(2)}) collective-permute-start(bf16[576,128]{1,0:T(8,128)(2,1)} %copy-done.19), channel_id=1, source_target_pairs={{0,8},{8,16},{16,24},{24,0},{1,9},{9,17},{17,25},{25,1},{2,10},{10... | collective-permute-start | bytes 442376 | tf_op jit(solution)/shard_map/ppermute | solution.py:300
  39.1 5.5 %collective-permute-start.3 = (bf16[576,128]{1,0:T(8,128)(2,1)}, bf16[576,128]{1,0:T(8,128)(2,1)}, u32[]{:S(2)}, u32[]{:S(2)}) collective-permute-start(bf16[576,128]{1,0:T(8,128)(2,1)} %copy-done.18), channel_id=1, source_target_pairs={{0,24},{8,0},{16,8},{24,16},{1,25},{9,1},{17,9},{25,17},{2,26},{10... | collective-permute-start | bytes 442376 | tf_op jit(solution)/shard_map/ppermute | solution.py:300
  45.0 1.0 copy-done.4
  46.1 0.8 copy-done.9
  46.9 0.7 copy-done.15
  47.6 2.7 %shard_map.128 = (bf16[16,32,128]{2,1,0:T(8,128)(2,1)S(1)}, bf16[32,128]{1,0:T(8,128)(2,1)S(1)}, bf16[128,128]{1,0:T(8,128)(2,1)S(1)}, bf16[256,128]{1,0:T(8,128)(2,1)S(1)}) custom-call(s32[2]{0:T(128)S(1)} %pad_add_fusion.place, s32[16,128]{1,0:T(8,128)S(1)} %copy-done.13, bf16[4,8,160,128]{3,2,1,0:T(8,128)(2,1)S(1)} %bitcast.16, ...), custom_call_target="tpu_custom_call" | custom-call | flops 335544320 | bytes 6291456 | tf_op jit(solution)/shard_map/pallas_call | solution.py:348
  50.3 0.6 copy-done.8
  52.1 2.8 %collective-permute-done.3 = bf16[576,128]{1,0:T(8,128)(2,1)} collective-permute-done((bf16[576,128]{1,0:T(8,128)(2,1)}, bf16[576,128]{1,0:T(8,128)(2,1)}, u32[]{:S(2)}, u32[]{:S(2)}) %collective-permute-start.3) | collective-permute-done | bytes 147488 | tf_op jit(solution)/shard_map/ppermute | solution.py:300
  55.0 12.2 %all-to-all-start.2 = ((bf16[16,32,128]{2,1,0:T(8,128)(2,1)}), bf16[16,32,128]{2,1,0:T(8,128)(2,1)S(1)}, u32[]{:S(2)}, u32[]{:S(2)}) async-start(bf16[16,32,128]{2,1,0:T(8,128)(2,1)} %copy-done.8), calls=%async_computation.2 | async-start | bytes 262144 | tf_op jit(solution)/shard_map/all_to_all | solution.py:386
  67.2 4.2 %collective-permute-start.5 = (bf16[576,128]{1,0:T(8,128)(2,1)}, bf16[576,128]{1,0:T(8,128)(2,1)S(1)}, u32[]{:S(2)}, u32[]{:S(2)}) collective-permute-start(bf16[576,128]{1,0:T(8,128)(2,1)} %collective-permute-done.2), channel_id=1, source_target_pairs={{0,8},{8,16},{16,24},{24,0},{1,9},{9,17},{17,25},{25,1},{2,10},{10... | collective-permute-start | bytes 442376 | tf_op jit(solution)/shard_map/ppermute | solution.py:300
  71.4 4.0 %collective-permute-start.6 = (bf16[576,128]{1,0:T(8,128)(2,1)}, bf16[576,128]{1,0:T(8,128)(2,1)S(1)}, u32[]{:S(2)}, u32[]{:S(2)}) collective-permute-start(bf16[576,128]{1,0:T(8,128)(2,1)} %collective-permute-done.3), channel_id=1, source_target_pairs={{0,24},{8,0},{16,8},{24,16},{1,25},{9,1},{17,9},{25,17},{2,26},{10... | collective-permute-start | bytes 442376 | tf_op jit(solution)/shard_map/ppermute | solution.py:300
  75.5 1.4 collective-permute-start.4
  76.8 1.6 %shard_map.129 = (bf16[8,320,128]{2,1,0:T(8,128)(2,1)}, f32[8,256]{1,0:T(8,128)S(1)}) custom-call(s32[2]{0:T(128)S(1)} %pad_add_fusion.place, bf16[16,32,128]{2,1,0:T(8,128)(2,1)S(1)} %all-to-all-done.2.received, bf16[32,128]{1,0:T(8,128)(2,1)S(1)} %collective-permute-done.4.fresh, bf16[256,1024]{1,0:T(8,128)(2,1)S(1)} %bitcast.18), custom_call_target="tpu_custom_call" | custom-call | flops 16777216 | bytes 1048576 | tf_op jit(solution)/shard_map/pallas_call | solution.py:388
  79.0 3.7 %collective-permute-done.6.refs_4_ = bf16[576,128]{1,0:T(8,128)(2,1)S(1)} collective-permute-done((bf16[576,128]{1,0:T(8,128)(2,1)}, bf16[576,128]{1,0:T(8,128)(2,1)S(1)}, u32[]{:S(2)}, u32[]{:S(2)}) %collective-permute-start.6) | collective-permute-done | bytes 147488 | tf_op jit(solution)/shard_map/ppermute | solution.py:300
  82.7 8.3 %all-to-all-start.3 = ((bf16[8,320,128]{2,1,0:T(8,128)(2,1)}), bf16[8,320,128]{2,1,0:T(8,128)(2,1)S(1)}, u32[]{:S(2)}, u32[]{:S(2)}) async-start(bf16[8,320,128]{2,1,0:T(8,128)(2,1)} %get-tuple-element.48), calls=%async_computation.3 | async-start | bytes 1310720 | tf_op jit(solution)/shard_map/all_to_all | solution.py:397
  91.0 1.5 %shard_map.130 = (bf16[2048,256]{1,0:T(8,128)(2,1)S(1)}, bf16[160,2048]{1,0:T(8,128)(2,1)S(1)}) custom-call(bf16[1152,128]{1,0:T(8,128)(2,1)S(1)} %copy-done.7, bf16[1152,128]{1,0:T(8,128)(2,1)} %collective-permute-done.refs_1_, bf16[1152,128]{1,0:T(8,128)(2,1)} %collective-permute-done.1.refs_2_, bf16[576,128]{1,0:T(8,128)(2,1)S(1)} %collective-permute-done.5.refs_3_, ...), custom_call_target="tpu_custom_call" | custom-call | bytes 3145728 | tf_op jit(solution)/shard_map/pallas_call | solution.py:400
  92.5 7.1 %all-to-all-done.3.queries.gathered = bf16[8,320,128]{2,1,0:T(8,128)(2,1)S(1)} async-done(((bf16[8,320,128]{2,1,0:T(8,128)(2,1)}), bf16[8,320,128]{2,1,0:T(8,128)(2,1)S(1)}, u32[]{:S(2)}, u32[]{:S(2)}) %all-to-all-start.3) | async-done | bytes 655392 | tf_op jit(solution)/shard_map/all_to_all | solution.py:397
  99.6 9.6 %shard_map.131 = bf16[8,272,128]{2,1,0:T(8,128)(2,1)S(1)} custom-call(s32[2]{0:T(128)S(1)} %pad_add_fusion.place, bf16[8,320,128]{2,1,0:T(8,128)(2,1)S(1)} %all-to-all-done.3.queries.gathered, f32[8,256]{1,0:T(8,128)S(1)} %get-tuple-element.49.slot_adapters, bf16[256,1024]{1,0:T(8,128)(2,1)S(1)} %bitcast.19, bf16[2048,256]{1,0:T(8,128)(2,1)S(1)} %get-tuple-element.55.keys, ...), custom_call_target="tpu_custom_call" | custom-call | flops 4294967296 | bytes 3145728 | tf_op jit(solution)/shard_map/pallas_call | solution.py:406
  109.2 15.3 %all_to_all.31.partials = bf16[8,272,128]{2,1,0:T(8,128)(2,1)S(1)} all-to-all(bf16[8,272,128]{2,1,0:T(8,128)(2,1)S(1)} %shard_map.131), channel_id=1, replica_groups=mesh['grp'=16,'yh'=4,'yl'=2,'x'=4] {'yl','x'}, dimensions={0} | all-to-all | bytes 1114112 | tf_op jit(solution)/shard_map/all_to_all | solution.py:417
  124.7 17.8 %all_to_all.32.received = bf16[16,32,128]{2,1,0:T(8,128)(2,1)S(1)} all-to-all(bf16[16,32,128]{2,1,0:T(8,128)(2,1)S(1)} %shard_map.132), channel_id=1, replica_groups=mesh['grp'=16,'yh'=4,'yl'=2,'x'=4] {'grp'}, dimensions={0} | all-to-all | bytes 262144 | tf_op jit(solution)/shard_map/all_to_all | solution.py:426
  142.5 0.9 shard_map.133
  (46 shorter events, 2.5 us)
Async XLA Ops:
  0.1 1.0 copy-start.2
  1.1 1.0 copy-start.3
  2.2 0.8 copy-start.12
  3.7 0.7 copy-start.19
  4.3 19.0 %copy-start.6 = (bf16[1152,128]{1,0:T(8,128)(2,1)}, bf16[1152,128]{1,0:T(8,128)(2,1)S(1)}, u32[]{:S(2)}) copy-start(bf16[1152,128]{1,0:T(8,128)(2,1)S(1)} %get-tuple-element.50.refs_0_) | copy-start | bytes 884740
  4.3 19.0 %copy-start.16 = (bf16[1152,128]{1,0:T(8,128)(2,1)}, bf16[1152,128]{1,0:T(8,128)(2,1)S(1)}, u32[]{:S(2)}) copy-start(bf16[1152,128]{1,0:T(8,128)(2,1)S(1)} %get-tuple-element.40) | copy-start | bytes 884740
  4.3 19.0 %copy-start.17 = (bf16[1152,128]{1,0:T(8,128)(2,1)}, bf16[1152,128]{1,0:T(8,128)(2,1)S(1)}, u32[]{:S(2)}) copy-start(bf16[1152,128]{1,0:T(8,128)(2,1)S(1)} %get-tuple-element.39) | copy-start | bytes 884740
  4.3 19.0 %copy-start.18 = (bf16[576,128]{1,0:T(8,128)(2,1)}, bf16[576,128]{1,0:T(8,128)(2,1)S(1)}, u32[]{:S(2)}) copy-start(bf16[576,128]{1,0:T(8,128)(2,1)S(1)} %get-tuple-element.42) | copy-start | bytes 442372
  24.6 20.0 %copy-start.21 = (f32[5120]{0:T(1024)S(1)}, f32[5120]{0:T(1024)}, u32[]{:S(2)}) copy-start(f32[5120]{0:T(1024)} %param.14) | copy-start | bytes 61444
  24.6 20.4 %copy-start = (bf16[16,16,1024]{2,1,0:T(8,128)(2,1)S(1)}, bf16[16,16,1024]{2,1,0:T(8,128)(2,1)}, u32[]{:S(2)}) copy-start(bf16[16,16,1024]{2,1,0:T(8,128)(2,1)} %param.19) | copy-start | bytes 1572868
  24.6 20.4 %copy-start.1 = (bf16[5120,128]{1,0:T(8,128)(2,1)S(1)}, bf16[5120,128]{1,0:T(8,128)(2,1)}, u32[]{:S(2)}) copy-start(bf16[5120,128]{1,0:T(8,128)(2,1)} %query_weight.1) | copy-start | bytes 3932164
  24.6 20.4 %copy-start.5 = (bf16[5120,32]{0,1:T(8,128)(2,1)S(1)}, bf16[5120,32]{0,1:T(8,128)(2,1)}, u32[]{:S(2)}) copy-start(bf16[5120,32]{0,1:T(8,128)(2,1)} %param.16) | copy-start | bytes 983044
  24.6 20.4 %copy-start.13 = (s32[16,128]{1,0:T(8,128)S(1)}, s32[16,128]{1,0:T(8,128)}, u32[]{:S(2)}) copy-start(s32[16,128]{1,0:T(8,128)} %page_slots.1) | copy-start | bytes 24580
  24.6 20.4 %copy-start.14 = (s32[128]{0:T(128)S(1)}, s32[128]{0:T(128)}, u32[]{:S(2)}) copy-start(s32[128]{0:T(128)} %param.23) | copy-start | bytes 1540
  24.7 20.3 %all-to-all-start.1 = ((bf16[4,1280,128]{2,1,0:T(8,128)(2,1)}), bf16[4,1280,128]{2,1,0:T(8,128)(2,1)S(1)}, u32[]{:S(2)}, u32[]{:S(2)}) async-start(bf16[4,1280,128]{2,1,0:T(8,128)(2,1)} %broadcast_in_dim.15), calls=%async_computation.1 | async-start | bytes 2621440 | tf_op jit(solution)/shard_map/all_to_all | solution.py:346
  29.8 25.2 %collective-permute-start = (bf16[1152,128]{1,0:T(8,128)(2,1)}, bf16[1152,128]{1,0:T(8,128)(2,1)}, u32[]{:S(2)}, u32[]{:S(2)}) collective-permute-start(bf16[1152,128]{1,0:T(8,128)(2,1)} %copy-done.17), channel_id=1, source_target_pairs={{0,8},{8,16},{16,24},{24,0},{1,9},{9,17},{17,25},{25,1},{2,10},{10... | collective-permute-start | bytes 884744 | tf_op jit(solution)/shard_map/ppermute | solution.py:300
  31.7 23.3 %collective-permute-start.1 = (bf16[1152,128]{1,0:T(8,128)(2,1)}, bf16[1152,128]{1,0:T(8,128)(2,1)}, u32[]{:S(2)}, u32[]{:S(2)}) collective-permute-start(bf16[1152,128]{1,0:T(8,128)(2,1)} %copy-done.16), channel_id=1, source_target_pairs={{0,24},{8,0},{16,8},{24,16},{1,25},{9,1},{17,9},{25,17},{2,26},{10... | collective-permute-start | bytes 884744 | tf_op jit(solution)/shard_map/ppermute | solution.py:300
  37.2 14.9 %collective-permute-start.2 = (bf16[576,128]{1,0:T(8,128)(2,1)}, bf16[576,128]{1,0:T(8,128)(2,1)}, u32[]{:S(2)}, u32[]{:S(2)}) collective-permute-start(bf16[576,128]{1,0:T(8,128)(2,1)} %copy-done.19), channel_id=1, source_target_pairs={{0,8},{8,16},{16,24},{24,0},{1,9},{9,17},{17,25},{25,1},{2,10},{10... | collective-permute-start | bytes 442376 | tf_op jit(solution)/shard_map/ppermute | solution.py:300
  39.1 15.9 %collective-permute-start.3 = (bf16[576,128]{1,0:T(8,128)(2,1)}, bf16[576,128]{1,0:T(8,128)(2,1)}, u32[]{:S(2)}, u32[]{:S(2)}) collective-permute-start(bf16[576,128]{1,0:T(8,128)(2,1)} %copy-done.18), channel_id=1, source_target_pairs={{0,24},{8,0},{16,8},{24,16},{1,25},{9,1},{17,9},{25,17},{2,26},{10... | collective-permute-start | bytes 442376 | tf_op jit(solution)/shard_map/ppermute | solution.py:300
  45.0 1.0 copy-start.4
  46.1 0.8 copy-start.9
  46.9 0.7 copy-start.15
  50.3 0.6 copy-start.8
  50.9 0.6 copy-start.10
  51.5 0.6 copy-start.20
  52.1 38.9 %copy-start.7 = (bf16[1152,128]{1,0:T(8,128)(2,1)S(1)}, bf16[1152,128]{1,0:T(8,128)(2,1)}, u32[]{:S(2)}) copy-start(bf16[1152,128]{1,0:T(8,128)(2,1)} %copy-done.6) | copy-start | bytes 884740
  55.0 21.8 %all-to-all-start.2 = ((bf16[16,32,128]{2,1,0:T(8,128)(2,1)}), bf16[16,32,128]{2,1,0:T(8,128)(2,1)S(1)}, u32[]{:S(2)}, u32[]{:S(2)}) async-start(bf16[16,32,128]{2,1,0:T(8,128)(2,1)} %copy-done.8), calls=%async_computation.2 | async-start | bytes 262144 | tf_op jit(solution)/shard_map/all_to_all | solution.py:386
  67.2 11.8 %collective-permute-start.5 = (bf16[576,128]{1,0:T(8,128)(2,1)}, bf16[576,128]{1,0:T(8,128)(2,1)S(1)}, u32[]{:S(2)}, u32[]{:S(2)}) collective-permute-start(bf16[576,128]{1,0:T(8,128)(2,1)} %collective-permute-done.2), channel_id=1, source_target_pairs={{0,8},{8,16},{16,24},{24,0},{1,9},{9,17},{17,25},{25,1},{2,10},{10... | collective-permute-start | bytes 442376 | tf_op jit(solution)/shard_map/ppermute | solution.py:300
  71.4 11.3 %collective-permute-start.6 = (bf16[576,128]{1,0:T(8,128)(2,1)}, bf16[576,128]{1,0:T(8,128)(2,1)S(1)}, u32[]{:S(2)}, u32[]{:S(2)}) collective-permute-start(bf16[576,128]{1,0:T(8,128)(2,1)} %collective-permute-done.3), channel_id=1, source_target_pairs={{0,24},{8,0},{16,8},{24,16},{1,25},{9,1},{17,9},{25,17},{2,26},{10... | collective-permute-start | bytes 442376 | tf_op jit(solution)/shard_map/ppermute | solution.py:300
  75.5 1.4 collective-permute-start.4
  82.7 16.9 %all-to-all-start.3 = ((bf16[8,320,128]{2,1,0:T(8,128)(2,1)}), bf16[8,320,128]{2,1,0:T(8,128)(2,1)S(1)}, u32[]{:S(2)}, u32[]{:S(2)}) async-start(bf16[8,320,128]{2,1,0:T(8,128)(2,1)} %get-tuple-element.48), calls=%async_computation.3 | async-start | bytes 1310720 | tf_op jit(solution)/shard_map/all_to_all | solution.py:397
  109.2 33.3 %copy-start.11 = (bf16[256,128]{1,0:T(8,128)(2,1)S(1)}, bf16[256,128]{1,0:T(8,128)(2,1)}, u32[]{:S(2)}) copy-start(bf16[256,128]{1,0:T(8,128)(2,1)} %copy-done.10) | copy-start | bytes 196612

commit v3 on v2

--- a/solution.py
+++ b/solution.py
@@ -17,8 +17,9 @@
 SLOTS = 256
 TILES = SLOTS // LANES
 QUERY_ROWS = HEAD_SIZE + RANK
-MESSAGE_ROWS = TILES * QUERY_ROWS + 32
+MESSAGE_ROWS = TILES * QUERY_ROWS
 RETURN_ROWS = TILES * HEAD_SIZE + 16
+FRESH_ROWS = 32
 PIECE_TOKENS = 512
 PIECES = ((0, 0, 512), (1, 0, 512), (3, 0, 512), (2, 0, 256), (2, 256, 256))
 SCORE_SCALE = HEAD_SIZE**-0.5
@@ -26,6 +27,8 @@
 BF16 = jnp.bfloat16
 VMEM = pl.BlockSpec(memory_space=pltpu.VMEM)
 SMEM = pl.BlockSpec(memory_space=pltpu.SMEM)
+ANY = pl.BlockSpec(memory_space=pl.ANY)
+HBM = pl.BlockSpec(memory_space=pltpu.HBM)
 
 
 def dot(left, right, left_dim, right_dim):
@@ -34,12 +37,12 @@
     )
 
 
-def call(kernel, out_shape, in_specs, scratch=(), flops=0, moved=0, limit=32):
+def call(kernel, out_shape, in_specs, scratch=(), flops=0, moved=0, limit=32, out_specs=None):
     return pl.pallas_call(
         kernel,
         out_shape=out_shape,
         in_specs=in_specs,
-        out_specs=jax.tree.map(lambda _: VMEM, out_shape),
+        out_specs=out_specs or jax.tree.map(lambda _: VMEM, out_shape),
         scratch_shapes=list(scratch),
         compiler_params=pltpu.CompilerParams(vmem_limit_bytes=limit * 1024 * 1024),
         cost_estimate=pl.CostEstimate(flops=flops, bytes_accessed=moved, transcendentals=0),
@@ -62,15 +65,34 @@
     return high, middle, value - high - middle
 
 
-def pack_kernel(place, keys, values, factors, *pieces):
+def pack_kernel(place, keys, values, factors, features, copies, *rest):
+    pieces, sems = rest[:-1], rest[-1]
     own = place[1]
+    moves = []
     for (shift, start, count), piece in zip(PIECES, pieces):
         head = lax.rem(own + shift, Y_HIGH)
         columns = pl.ds(pl.multiple_of(head * HEAD_SIZE, HEAD_SIZE), HEAD_SIZE)
-        piece[0:count, :] = keys[start : start + count, columns]
-        piece[count : 2 * count, :] = values[start : start + count, columns]
+        tokens = pl.ds(start, count)
         first = start // LANES * 2 * RANK
-        piece[2 * count :, :] = factors[first : first + count // LANES * 2 * RANK, :]
+        rows = count // LANES * 2 * RANK
+        moves += [
+            (keys.at[tokens, columns], piece.at[pl.ds(0, count), :]),
+            (values.at[tokens, columns], piece.at[pl.ds(count, count), :]),
+            (factors.at[pl.ds(first, rows), :], piece.at[pl.ds(2 * count, rows), :]),
+        ]
+    moves = [pltpu.make_async_copy(*move, sems.at[i]) for i, move in enumerate(moves)]
+    for move in moves:
+        move.start()
+    mine = features[...]
+    for member in range(Y):
+        copies[member] = mine
+    for move in moves:
+        move.wait()
+
+
+def spread_kernel(features, held_right, held_left, copies):
+    for member in range(X):
+        copies[member] = features[...]
 
 
 def project_kernel(
@@ -78,22 +100,41 @@
     place,
     page_slots,
     features,
-    query_weight,
-    key_value_weight,
-    down,
+    query_weight_far,
+    key_value_weight_far,
+    down_far,
     gain,
-    query_up,
-    key_value_up,
+    query_up_far,
+    key_value_up_far,
     adapters,
     documents,
+    held_right,
+    held_left,
+    held_far_right,
+    held_far_left,
     message,
     fresh,
     queries_t,
     placing,
     normed,
+    query_weight,
     weights,
+    query_up,
+    key_value_up,
     update,
+    sems,
 ):
+    columns = pl.ds(pl.multiple_of(place[0] // X * HEAD_SIZE, HEAD_SIZE), HEAD_SIZE)
+    moves = [
+        (query_weight_far, query_weight),
+        (key_value_weight_far, weights.at[pl.ds(0, FRESH_ROWS), :]),
+        (down_far, weights.at[pl.ds(FRESH_ROWS, 3 * RANK), :]),
+        (query_up_far, query_up),
+        (key_value_up_far.at[:, columns], key_value_up),
+    ]
+    moves = [pltpu.make_async_copy(*move, sems.at[i]) for i, move in enumerate(moves)]
+    for move in moves:
+        move.start()
     device = place[0]
     part = gain.shape[1]
     width = normed.shape[0]
@@ -111,23 +152,22 @@
             t = y * X + x
             block = features[x, y].astype(F32) * scale * gain_t[:, t : t + 1]
             normed[t * part : (t + 1) * part, :] = block.astype(BF16)
-    weights[0:32, :] = key_value_weight[...]
-    weights[32:, :] = down[...]
+    for move in moves:
+        move.wait()
     query_total = dot(query_weight[...], normed[...], 0, 0)
     total = dot(weights[...], normed[...], 1, 0)
 
     adapter = adapters[...]
-    low = total[32:].astype(BF16)
+    low = total[FRESH_ROWS:].astype(BF16)
     query_update = dot(query_up[...], of_adapter(low[0:RANK], adapter), 0, 0)
     queries = (query_total + query_update).astype(BF16)
     queries_t[...] = queries
 
     is_key = device < Y * X // 2
     low_kv = jnp.where(is_key, low[RANK : 2 * RANK], low[2 * RANK :])
-    columns = pl.ds(pl.multiple_of(device // X * HEAD_SIZE, HEAD_SIZE), HEAD_SIZE)
-    update[...] = dot(key_value_up[:, columns], of_adapter(low_kv, adapter), 0, 0)
+    update[...] = dot(key_value_up[...], of_adapter(low_kv, adapter), 0, 0)
     mine = pl.ds(pl.multiple_of(lax.rem(device, X) * 32, 32), 32)
-    fresh[...] = (total[0:32] + update[mine, :]).astype(BF16)
+    fresh[...] = (total[0:FRESH_ROWS] + update[mine, :]).astype(BF16)
 
     document = documents[...]
     target = jnp.zeros_like(document)
@@ -155,7 +195,7 @@
     )
 
 
-def factor_kernel(groups, place, received, fresh, key_value_up, message, slot_adapters):
+def factor_kernel(groups, place, received, key_value_up, message, slot_adapters):
     capacity = SLOTS // groups
     queries = received[:, 0:capacity, :].reshape(SLOTS, HEAD_SIZE)
     queries_t = queries.astype(F32).T.astype(BF16)
@@ -169,14 +209,12 @@
     for a in range(1, 16):
         factors = factors + kept[a * RANK : (a + 1) * RANK]
     factors = factors.astype(BF16)
-    new = fresh[...]
     for member in range(BLOCK):
         for tile in range(TILES):
             lanes = slice(tile * LANES, (tile + 1) * LANES)
             start = tile * QUERY_ROWS
             message[member, start : start + HEAD_SIZE, :] = queries_t[:, lanes]
             message[member, start + HEAD_SIZE : start + QUERY_ROWS, :] = factors[:, lanes]
-        message[member, TILES * QUERY_ROWS :, :] = new
 
 
 def prepare_kernel(*refs):
@@ -203,7 +241,7 @@
 
 
 def attend_kernel(
-    place, queries, slot_adapters, key_value_up, keys, values_t, message, query, scores
+    place, queries, slot_adapters, key_value_up, keys, values_t, fresh, message, query, scores
 ):
     tokens = keys.shape[0]
     depth = 2 * HEAD_SIZE
@@ -245,7 +283,8 @@
             message[head, tile * HEAD_SIZE : (tile + 1) * HEAD_SIZE, :] = result[
                 :, tile * LANES : (tile + 1) * LANES
             ]
-        message[head, TILES * HEAD_SIZE :, :] = stats.astype(BF16)
+        message[head, TILES * HEAD_SIZE : RETURN_ROWS, :] = stats.astype(BF16)
+        message[head, RETURN_ROWS:, :] = fresh[...]
 
     def two_heads(pair, carry):
         first = score_head(2 * pair, 0)
@@ -259,7 +298,7 @@
 
 def merge_kernel(groups, partials, message):
     capacity = SLOTS // groups
-    stats = [partials[member, TILES * HEAD_SIZE :, :].astype(F32) for member in range(BLOCK)]
+    stats = [partials[member, TILES * HEAD_SIZE : RETURN_ROWS, :].astype(F32) for member in range(BLOCK)]
     results, masses = [], []
     for tile in range(TILES):
         first = 3 * tile
@@ -279,13 +318,13 @@
     message[:, capacity:, :] = jnp.concatenate(masses, axis=0).reshape(groups, capacity, LANES)
 
 
-def finish_kernel(groups, received, placing, queries_t, gathered, out):
+def finish_kernel(groups, received, placing, queries_t, partials, out):
     capacity = SLOTS // groups
     place = placing[...]
     shared = dot(received[:, 0:capacity, :].reshape(SLOTS, HEAD_SIZE), place, 0, 0)
     stats = dot(received[:, capacity:, :].reshape(SLOTS, LANES), place, 0, 0)
     log_mass = stats[0:1] + stats[1:2] + stats[2:3]
-    new = gathered[:, TILES * QUERY_ROWS :, :]
+    new = partials[:, RETURN_ROWS:, :]
     key = new[0:X].reshape(HEAD_SIZE, LANES).astype(F32)
     value = new[X:].reshape(HEAD_SIZE, LANES).astype(F32)
     own = jnp.sum(queries_t[...].astype(F32) * key, axis=0, keepdims=True) * SCORE_SCALE
@@ -325,39 +364,52 @@
     query_up = query_up_factors.reshape(-1, HEAD_SIZE)
     key_value_up = key_value_up_factors.reshape(-1, key_value_up_factors.shape[2])
 
-    features = jnp.broadcast_to(residual_input.T[None], (Y, part, rows))
-    pieces = call(
+    piece_shapes = [shape(2 * n + 2 * RANK * n // LANES, HEAD_SIZE) for _, _, n in PIECES]
+    features, own, right, left, far_right, far_left = call(
         pack_kernel,
-        [shape(2 * n + 2 * RANK * n // LANES, HEAD_SIZE) for _, _, n in PIECES],
-        [SMEM, VMEM, VMEM, VMEM],
+        [shape(Y, part, rows)] + piece_shapes,
+        [SMEM, HBM, HBM, HBM, VMEM],
+        [pltpu.SemaphoreType.DMA((3 * len(PIECES),))],
         moved=3 * 1024 * 1024,
+        limit=60,
+        out_specs=[VMEM] + [HBM] * len(PIECES),
     )(
         place,
         paged_base_keys.reshape(PIECE_TOKENS, -1),
         paged_base_values.reshape(PIECE_TOKENS, -1),
         paged_down_factors.transpose(0, 2, 1).reshape(-1, LANES),
-    )
-    features, pieces = lax.optimization_barrier((features, pieces))
-    own, right, left, far_right, far_left = pieces
-    right, left = send(right, 1), send(left, -1)
+        residual_input.T,
+    )
     far_right, far_left = send(far_right, 1), send(far_left, -1)
     features = lax.all_to_all(features, ("yh", "yl"), 0, 0, tiled=True)
-    features = jnp.broadcast_to(features.reshape(1, Y * part, rows), (X, Y * part, rows))
+
+    features = call(
+        spread_kernel,
+        shape(X, Y * part, rows),
+        [VMEM, ANY, ANY],
+        moved=1024 * 1024,
+    )(features.reshape(Y * part, rows), far_right, far_left)
+    far_right, far_left = send(far_right, 1), send(far_left, -1)
+    right, left = send(right, 1), send(left, -1)
     features = lax.all_to_all(features, "x", 0, 0, tiled=True).reshape(X, Y, part, rows)
 
     message, fresh, queries_t, placing = call(
         functools.partial(project_kernel, groups),
         [
             shape(groups, 2 * capacity, HEAD_SIZE),
-            shape(32, rows),
+            shape(FRESH_ROWS, rows),
             shape(HEAD_SIZE, rows),
             shape(SLOTS, rows),
         ],
-        [SMEM, SMEM] + [VMEM] * 9,
+        [SMEM, SMEM, VMEM, HBM, HBM, HBM, VMEM, HBM, HBM, VMEM, VMEM] + [ANY] * 4,
         [
             pltpu.VMEM((width, rows), BF16),
-            pltpu.VMEM((32 + 3 * RANK, width), BF16),
+            pltpu.VMEM((width, HEAD_SIZE), BF16),
+            pltpu.VMEM((FRESH_ROWS + 3 * RANK, width), BF16),
+            pltpu.VMEM(query_up.shape, BF16),
+            pltpu.VMEM((key_value_up.shape[0], HEAD_SIZE), BF16),
             pltpu.VMEM((HEAD_SIZE, rows), F32),
+            pltpu.SemaphoreType.DMA((5,)),
         ],
         flops=2 * width * rows * 256,
         moved=6 * 1024 * 1024,
@@ -373,26 +425,25 @@
         key_value_up,
         adapter_of_row.reshape(1, rows),
         document_of_row.reshape(1, rows),
+        right,
+        left,
+        far_right,
+        far_left,
     )
     fresh = lax.ppermute(
         fresh,
         ("yh", "yl"),
         [(y, 2 * y if y < Y_HIGH else 2 * (y - Y_HIGH) + 1) for y in range(Y)],
     )
-    message, right, left, far_right, far_left = lax.optimization_barrier(
-        (message, right, left, far_right, far_left)
-    )
-    far_right, far_left = send(far_right, 1), send(far_left, -1)
     received = lax.all_to_all(message, "grp", 0, 0, tiled=True)
 
     message, slot_adapters = call(
         functools.partial(factor_kernel, groups),
         [shape(BLOCK, MESSAGE_ROWS, LANES), shape(8, SLOTS, dtype=F32)],
-        [SMEM] + [VMEM] * 3,
+        [SMEM] + [VMEM] * 2,
         flops=2 * 256 * 256 * 128,
         moved=1024 * 1024,
-    )(place, received, fresh, key_value_up)
-    message, far_right, far_left = lax.optimization_barrier((message, far_right, far_left))
+    )(place, received, key_value_up)
     pieces = (own, right, left, far_right, far_left)
     gathered = lax.all_to_all(message, ("yl", "x"), 0, 0, tiled=True)
 
@@ -405,15 +456,15 @@
     )(*pieces)
     message = call(
         attend_kernel,
-        shape(BLOCK, RETURN_ROWS, LANES),
-        [SMEM] + [VMEM] * 5,
+        shape(BLOCK, RETURN_ROWS + FRESH_ROWS, LANES),
+        [SMEM] + [VMEM] * 6,
         [
             pltpu.VMEM((2, 2 * HEAD_SIZE, SLOTS), BF16),
             pltpu.VMEM((2, tokens, SLOTS), F32),
         ],
         flops=4 * SLOTS * BLOCK * tokens * 256,
         moved=3 * 1024 * 1024,
-    )(place, gathered, slot_adapters, key_value_up, keys, values_t)
+    )(place, gathered, slot_adapters, key_value_up, keys, values_t, fresh)
     partials = lax.all_to_all(message, ("yl", "x"), 0, 0, tiled=True)
 
     message = call(
@@ -431,7 +482,7 @@
         [VMEM] * 4,
         flops=2 * SLOTS * rows * 256,
         moved=1024 * 1024,
-    )(received, placing, queries_t, gathered)
+    )(received, placing, queries_t, partials)
 
 
 def solution(mesh):

time: 144 us -> 180 us (1.25)
  Pallas kernels: 17.3 us -> 56.9 us
  waiting for transfers between devices: 14.5 us -> 28.7 us
  starting transfers between devices: 50 us -> 39.5 us
  local copies, waits for them, and re-layouts: 10.1 us -> 4.81 us
  blocking collectives: 51.2 us -> 48.2 us
    pallas_call x2 -> x3, Pallas kernels: 10.3 us -> 49.3 us  [the longest x1 38.5 us: per_device(): call(pack_kernel, [shape(Y, part, rows)] + piece_shapes, [SMEM, HBM, HBM,...]
    all_to_all x1 -> x0, blocking collectives: 18.1 us -> none  [per_device(): features = lax.all_to_all(features, ('yh', 'yl'), 0, 0, tiled=True)]
    all_to_all x1 -> x2, blocking collectives: 17.8 us -> 33.9 us  [per_device(): received = lax.all_to_all(message, 'grp', 0, 0, tiled=True)]
    ppermute x6, waiting for transfers between devices: 7.1 us -> 22 us  [send(): lax.ppermute(value, 'yh', [(i, (i + shift) % Y_HIGH) for i in range(Y_HIG...]
    all_to_all x1, starting transfers between devices: 12.2 us -> 7.66 us  [per_device(): features = lax.all_to_all(features, ('yh', 'yl'), 0, 0, tiled=True)]
    all_to_all x1, starting transfers between devices: 8.28 us -> 4.16 us  [per_device(): gathered = lax.all_to_all(message, ('yl', 'x'), 0, 0, tiled=True)]
    unnamed x44 -> x34, local copies, waits for them, and re-layouts: 7.92 us -> 4.01 us
    broadcast_in_dim x2 -> x0, local copies, waits for them, and re-layouts: 2.11 us -> none  [the longest x1 1.24 us: per_device(): jnp.broadcast_to(features.reshape(1, Y * part, rows), (X, Y * part, rows))]
  transfers between devices with their start and end apart: 10 -> 10, of which waited for: 5 -> 5; matrix products, arithmetic and copies ran while one was open for 0% -> 0% of each run, Pallas kernels for 4% -> 1%
where the time goes in v3:
time: 180 us; the launch traced here: 179 us
  Pallas kernels  56.9 us (32%)
  blocking collectives  48.2 us (27%)
  starting transfers between devices  39.5 us (22%)
  waiting for transfers between devices  28.7 us (16%)
  local copies, waits for them, and re-layouts  4.81 us (3%)
    pallas_call x1, Pallas kernels, per_device(): call(pack_kernel, [shape(Y, part, rows)] + piece_shapes, [SMEM, HBM, HBM,...  38.5 us
    all_to_all x2, blocking collectives, per_device(): received = lax.all_to_all(message, 'grp', 0, 0, tiled=True)  33.9 us
    ppermute x6, starting transfers between devices, send(): lax.ppermute(value, 'yh', [(i, (i + shift) % Y_HIGH) for i in range(Y_HIG...  22.2 us
    ppermute x6, waiting for transfers between devices, send(): lax.ppermute(value, 'yh', [(i, (i + shift) % Y_HIGH) for i in range(Y_HIG...  22 us
    all_to_all x1, blocking collectives, per_device(): partials = lax.all_to_all(message, ('yl', 'x'), 0, 0, tiled=True)  14.3 us
    pallas_call x1, Pallas kernels, per_device(): call(attend_kernel, shape(BLOCK, RETURN_ROWS + FRESH_ROWS, LANES), [SMEM]...  9.56 us
    all_to_all x1, starting transfers between devices, per_device(): features = lax.all_to_all(features, ('yh', 'yl'), 0, 0, tiled=True)  7.66 us
    all_to_all x1, waiting for transfers between devices, per_device(): gathered = lax.all_to_all(message, ('yl', 'x'), 0, 0, tiled=True)  6.74 us
  transfers between devices with their start and end apart: 10, of which 5 were waited for; matrix products, arithmetic and copies ran while one was open for 0% of the time, Pallas kernels for 1%

profile of v3, /device:TPU:1, one launch (start us, length us, event | category | flops | bytes accessed | tf_op | source)
XLA Modules:
  0.0 178.9 jit_solution(15128293667884958573)
XLA Ops:
  0.0 0.6 pad_add_fusion.place
  0.6 38.5 %shard_map.127 = (bf16[8,160,128]{2,1,0:T(8,128)(2,1)}, bf16[1152,128]{1,0:T(8,128)(2,1)}, bf16[1152,128]{1,0:T(8,128)(2,1)}, bf16[1152,128]{1,0:T(8,128)(2,1)},...) custom-call(s32[2]{0:T(128)} %pad_add_fusion.place, bf16[512,512]{1,0:T(8,128)(2,1)} %bitcast.26, ...), custom_call_target="tpu_custom_call" | custom-call | bytes 3145728 | tf_op jit(solution)/shard_map/pallas_call | solution.py:368
  39.1 7.7 %all-to-all-start = ((bf16[8,160,128]{2,1,0:T(8,128)(2,1)}), bf16[8,160,128]{2,1,0:T(8,128)(2,1)S(1)}, u32[]{:S(2)}, u32[]{:S(2)}) async-start(bf16[8,160,128]{2,1,0:T(8,128)(2,1)} %get-tuple-element.19), calls=%async_computation | async-start | bytes 655360 | tf_op jit(solution)/shard_map/all_to_all | solution.py:384
  46.7 4.3 %collective-permute-start = (bf16[576,128]{1,0:T(8,128)(2,1)}, bf16[576,128]{1,0:T(8,128)(2,1)S(1)}, u32[]{:S(2)}, u32[]{:S(2)}) collective-permute-start(bf16[576,128]{1,0:T(8,128)(2,1)} %get-tuple-element.20), channel_id=1, source_target_pairs={{0,8},{8,16},{16,24},{24,0},{1,9},{9,17},{17,25},{25,1},{2,10},{10... | collective-permute-start | bytes 442376 | tf_op jit(solution)/shard_map/ppermute | solution.py:339
  51.0 3.1 %collective-permute-start.1 = (bf16[576,128]{1,0:T(8,128)(2,1)}, bf16[576,128]{1,0:T(8,128)(2,1)S(1)}, u32[]{:S(2)}, u32[]{:S(2)}) collective-permute-start(bf16[576,128]{1,0:T(8,128)(2,1)} %get-tuple-element.21), channel_id=1, source_target_pairs={{0,24},{8,0},{16,8},{24,16},{1,25},{9,1},{17,9},{25,17},{2,26},{10... | collective-permute-start | bytes 442376 | tf_op jit(solution)/shard_map/ppermute | solution.py:339
  54.2 6.8 %collective-permute-done.held_right = bf16[576,128]{1,0:T(8,128)(2,1)S(1)} collective-permute-done((bf16[576,128]{1,0:T(8,128)(2,1)}, bf16[576,128]{1,0:T(8,128)(2,1)S(1)}, u32[]{:S(2)}, u32[]{:S(2)}) %collective-permute-start) | collective-permute-done | bytes 147488 | tf_op jit(solution)/shard_map/ppermute | solution.py:339
  60.9 3.1 %collective-permute-done.1.held_left = bf16[576,128]{1,0:T(8,128)(2,1)S(1)} collective-permute-done((bf16[576,128]{1,0:T(8,128)(2,1)}, bf16[576,128]{1,0:T(8,128)(2,1)S(1)}, u32[]{:S(2)}, u32[]{:S(2)}) %collective-permute-start.1) | collective-permute-done | bytes 147488 | tf_op jit(solution)/shard_map/ppermute | solution.py:339
  64.0 1.2 shard_map.128
  65.2 0.7 copy-done.5
  65.9 0.6 copy-done.6
  66.6 4.2 %all-to-all-start.1 = ((bf16[4,1280,128]{2,1,0:T(8,128)(2,1)}), bf16[4,1280,128]{2,1,0:T(8,128)(2,1)S(1)}, u32[]{:S(2)}, u32[]{:S(2)}) async-start(bf16[4,1280,128]{2,1,0:T(8,128)(2,1)} %shard_map.128), calls=%async_computation.1 | async-start | bytes 2621440 | tf_op jit(solution)/shard_map/all_to_all | solution.py:394
  70.7 4.6 %collective-permute-start.2 = (bf16[1152,128]{1,0:T(8,128)(2,1)}, bf16[1152,128]{1,0:T(8,128)(2,1)S(1)}, u32[]{:S(2)}, u32[]{:S(2)}) collective-permute-start(bf16[1152,128]{1,0:T(8,128)(2,1)} %get-tuple-element.22), channel_id=1, source_target_pairs={{0,8},{8,16},{16,24},{24,0},{1,9},{9,17},{17,25},{25,1},{2,10},{10... | collective-permute-start | bytes 884744 | tf_op jit(solution)/shard_map/ppermute | solution.py:339
  75.4 2.8 %collective-permute-start.3 = (bf16[1152,128]{1,0:T(8,128)(2,1)}, bf16[1152,128]{1,0:T(8,128)(2,1)}, u32[]{:S(2)}, u32[]{:S(2)}) collective-permute-start(bf16[1152,128]{1,0:T(8,128)(2,1)} %get-tuple-element.23), channel_id=1, source_target_pairs={{0,24},{8,0},{16,8},{24,16},{1,25},{9,1},{17,9},{25,17},{2,26},{10... | collective-permute-start | bytes 884744 | tf_op jit(solution)/shard_map/ppermute | solution.py:339
  78.1 3.4 %collective-permute-start.4 = (bf16[576,128]{1,0:T(8,128)(2,1)}, bf16[576,128]{1,0:T(8,128)(2,1)}, u32[]{:S(2)}, u32[]{:S(2)}) collective-permute-start(bf16[576,128]{1,0:T(8,128)(2,1)} %copy-done.5), channel_id=1, source_target_pairs={{0,8},{8,16},{16,24},{24,0},{1,9},{9,17},{17,25},{25,1},{2,10},{10... | collective-permute-start | bytes 442376 | tf_op jit(solution)/shard_map/ppermute | solution.py:339
  81.6 4.0 %collective-permute-start.5 = (bf16[576,128]{1,0:T(8,128)(2,1)}, bf16[576,128]{1,0:T(8,128)(2,1)}, u32[]{:S(2)}, u32[]{:S(2)}) collective-permute-start(bf16[576,128]{1,0:T(8,128)(2,1)} %copy-done.6), channel_id=1, source_target_pairs={{0,24},{8,0},{16,8},{24,16},{1,25},{9,1},{17,9},{25,17},{2,26},{10... | collective-permute-start | bytes 442376 | tf_op jit(solution)/shard_map/ppermute | solution.py:339
  85.6 0.8 reshape.35.gain
  86.4 9.0 %collective-permute-done.3.held_left.refs_2_ = bf16[1152,128]{1,0:T(8,128)(2,1)} collective-permute-done((bf16[1152,128]{1,0:T(8,128)(2,1)}, bf16[1152,128]{1,0:T(8,128)(2,1)}, u32[]{:S(2)}, u32[]{:S(2)}) %collective-permute-start.3) | collective-permute-done | bytes 294944 | tf_op jit(solution)/shard_map/ppermute | solution.py:339
  95.3 3.2 %collective-permute-done.5.held_far_left.refs_4_ = bf16[576,128]{1,0:T(8,128)(2,1)} collective-permute-done((bf16[576,128]{1,0:T(8,128)(2,1)}, bf16[576,128]{1,0:T(8,128)(2,1)}, u32[]{:S(2)}, u32[]{:S(2)}) %collective-permute-start.5) | collective-permute-done | bytes 147488 | tf_op jit(solution)/shard_map/ppermute | solution.py:339
  98.5 1.0 copy-done.2
  99.6 1.0 copy-done.3
  100.5 0.7 copy-done.15
  101.2 3.4 %shard_map.129 = (bf16[16,32,128]{2,1,0:T(8,128)(2,1)S(1)}, bf16[32,128]{1,0:T(8,128)(2,1)S(1)}, bf16[128,128]{1,0:T(8,128)(2,1)S(1)}, bf16[256,128]{1,0:T(8,128)(2,1)S(1)}) custom-call(s32[2]{0:T(128)S(1)} %copy-done.13, s32[16,128]{1,0:T(8,128)S(1)} %copy-done.12, bf16[4,8,160,128]{3,2,1,0:T(8,128)(2,1)S(1)} %bitcast.16, bf16[5120,128]{1,0:T(8,128)(2,1)S(1)} %copy-done.1, ...), custom_call_target="tpu_custom_call" | custom-call | flops 335544320 | bytes 6291456 | tf_op jit(solution)/shard_map/pallas_call | solution.py:396
  104.6 20.4 %all_to_all.30.received = bf16[16,32,128]{2,1,0:T(8,128)(2,1)S(1)} all-to-all(bf16[16,32,128]{2,1,0:T(8,128)(2,1)S(1)} %get-tuple-element.24), channel_id=1, replica_groups=mesh['grp'=16,'yh'=4,'yl'=2,'x'=4] {'grp'}, dimensions={0} | all-to-all | bytes 262144 | tf_op jit(solution)/shard_map/all_to_all | solution.py:438
  125.0 1.6 shard_map.130
  126.6 4.2 %all-to-all-start.3 = ((bf16[8,288,128]{2,1,0:T(8,128)(2,1)}), bf16[8,288,128]{2,1,0:T(8,128)(2,1)S(1)}, u32[]{:S(2)}, u32[]{:S(2)}) async-start(bf16[8,288,128]{2,1,0:T(8,128)(2,1)} %get-tuple-element.25), calls=%async_computation.3 | async-start | bytes 1179648 | tf_op jit(solution)/shard_map/all_to_all | solution.py:448
  130.7 1.3 collective-permute-start.6
  132.1 1.5 shard_map.131
  133.6 6.7 %all-to-all-done.3.queries = bf16[8,288,128]{2,1,0:T(8,128)(2,1)S(1)} async-done(((bf16[8,288,128]{2,1,0:T(8,128)(2,1)}), bf16[8,288,128]{2,1,0:T(8,128)(2,1)S(1)}, u32[]{:S(2)}, u32[]{:S(2)}) %all-to-all-start.3) | async-done | bytes 589856 | tf_op jit(solution)/shard_map/all_to_all | solution.py:448
  140.4 9.6 %shard_map.132 = bf16[8,304,128]{2,1,0:T(8,128)(2,1)S(1)} custom-call(s32[2]{0:T(128)S(1)} %copy-done.13, bf16[8,288,128]{2,1,0:T(8,128)(2,1)S(1)} %all-to-all-done.3.queries, f32[8,256]{1,0:T(8,128)S(1)} %get-tuple-element.26.slot_adapters, bf16[256,1024]{1,0:T(8,128)(2,1)S(1)} %bitcast.19, bf16[2048,256]{1,0:T(8,128)(2,1)S(1)} %get-tuple-element.28.keys, ...), custom_call_target="tpu_custom_call" | custom-call | flops 4294967296 | bytes 3145728 | tf_op jit(solution)/shard_map/pallas_call | solution.py:457
  150.0 14.3 %all_to_all.31.partials = bf16[8,304,128]{2,1,0:T(8,128)(2,1)S(1)} all-to-all(bf16[8,304,128]{2,1,0:T(8,128)(2,1)S(1)} %shard_map.132), channel_id=1, replica_groups=mesh['grp'=16,'yh'=4,'yl'=2,'x'=4] {'yl','x'}, dimensions={0} | all-to-all | bytes 1245184 | tf_op jit(solution)/shard_map/all_to_all | solution.py:468
  164.5 13.5 %all_to_all.32.received = bf16[16,32,128]{2,1,0:T(8,128)(2,1)S(1)} all-to-all(bf16[16,32,128]{2,1,0:T(8,128)(2,1)S(1)} %shard_map.133), channel_id=1, replica_groups=mesh['grp'=16,'yh'=4,'yl'=2,'x'=4] {'grp'}, dimensions={0} | all-to-all | bytes 262144 | tf_op jit(solution)/shard_map/all_to_all | solution.py:477
  178.0 0.9 shard_map.134
  (35 shorter events, 0.3 us)
Async XLA Ops:
  39.1 24.9 %all-to-all-start = ((bf16[8,160,128]{2,1,0:T(8,128)(2,1)}), bf16[8,160,128]{2,1,0:T(8,128)(2,1)S(1)}, u32[]{:S(2)}, u32[]{:S(2)}) async-start(bf16[8,160,128]{2,1,0:T(8,128)(2,1)} %get-tuple-element.19), calls=%async_computation | async-start | bytes 655360 | tf_op jit(solution)/shard_map/all_to_all | solution.py:384
  46.7 14.2 %collective-permute-start = (bf16[576,128]{1,0:T(8,128)(2,1)}, bf16[576,128]{1,0:T(8,128)(2,1)S(1)}, u32[]{:S(2)}, u32[]{:S(2)}) collective-permute-start(bf16[576,128]{1,0:T(8,128)(2,1)} %get-tuple-element.20), channel_id=1, source_target_pairs={{0,8},{8,16},{16,24},{24,0},{1,9},{9,17},{17,25},{25,1},{2,10},{10... | collective-permute-start | bytes 442376 | tf_op jit(solution)/shard_map/ppermute | solution.py:339
  51.0 13.0 %collective-permute-start.1 = (bf16[576,128]{1,0:T(8,128)(2,1)}, bf16[576,128]{1,0:T(8,128)(2,1)S(1)}, u32[]{:S(2)}, u32[]{:S(2)}) collective-permute-start(bf16[576,128]{1,0:T(8,128)(2,1)} %get-tuple-element.21), channel_id=1, source_target_pairs={{0,24},{8,0},{16,8},{24,16},{1,25},{9,1},{17,9},{25,17},{2,26},{10... | collective-permute-start | bytes 442376 | tf_op jit(solution)/shard_map/ppermute | solution.py:339
  65.2 0.7 copy-start.5
  65.9 0.6 copy-start.6
  66.6 31.9 %copy-start = (bf16[16,16,1024]{2,1,0:T(8,128)(2,1)S(1)}, bf16[16,16,1024]{2,1,0:T(8,128)(2,1)}, u32[]{:S(2)}) copy-start(bf16[16,16,1024]{2,1,0:T(8,128)(2,1)} %param.19) | copy-start | bytes 1572868
  66.6 31.9 %copy-start.1 = (bf16[5120,128]{1,0:T(8,128)(2,1)S(1)}, bf16[5120,128]{1,0:T(8,128)(2,1)}, u32[]{:S(2)}) copy-start(bf16[5120,128]{1,0:T(8,128)(2,1)} %query_weight_far.1) | copy-start | bytes 3932164
  66.6 31.9 %copy-start.7 = (bf16[16,16,128]{2,1,0:T(8,128)(2,1)S(1)}, bf16[16,16,128]{2,1,0:T(8,128)(2,1)}, u32[]{:S(2)}) copy-start(bf16[16,16,128]{2,1,0:T(8,128)(2,1)} %param.18) | copy-start | bytes 196612
  66.6 31.9 %copy-start.12 = (s32[16,128]{1,0:T(8,128)S(1)}, s32[16,128]{1,0:T(8,128)}, u32[]{:S(2)}) copy-start(s32[16,128]{1,0:T(8,128)} %page_slots.1) | copy-start | bytes 24580
  66.6 32.0 %copy-start.13 = (s32[2]{0:T(128)S(1)}, s32[2]{0:T(128)}, u32[]{:S(2)}) copy-start(s32[2]{0:T(128)} %pad_add_fusion.place) | copy-start | bytes 28
  66.6 32.0 %copy-start.14 = (s32[128]{0:T(128)S(1)}, s32[128]{0:T(128)}, u32[]{:S(2)}) copy-start(s32[128]{0:T(128)} %param.23) | copy-start | bytes 1540
  66.6 31.9 %all-to-all-start.1 = ((bf16[4,1280,128]{2,1,0:T(8,128)(2,1)}), bf16[4,1280,128]{2,1,0:T(8,128)(2,1)S(1)}, u32[]{:S(2)}, u32[]{:S(2)}) async-start(bf16[4,1280,128]{2,1,0:T(8,128)(2,1)} %shard_map.128), calls=%async_computation.1 | async-start | bytes 2621440 | tf_op jit(solution)/shard_map/all_to_all | solution.py:394
  70.7 15.6 %collective-permute-start.2 = (bf16[1152,128]{1,0:T(8,128)(2,1)}, bf16[1152,128]{1,0:T(8,128)(2,1)S(1)}, u32[]{:S(2)}, u32[]{:S(2)}) collective-permute-start(bf16[1152,128]{1,0:T(8,128)(2,1)} %get-tuple-element.22), channel_id=1, source_target_pairs={{0,8},{8,16},{16,24},{24,0},{1,9},{9,17},{17,25},{25,1},{2,10},{10... | collective-permute-start | bytes 884744 | tf_op jit(solution)/shard_map/ppermute | solution.py:339
  75.4 19.9 %collective-permute-start.3 = (bf16[1152,128]{1,0:T(8,128)(2,1)}, bf16[1152,128]{1,0:T(8,128)(2,1)}, u32[]{:S(2)}, u32[]{:S(2)}) collective-permute-start(bf16[1152,128]{1,0:T(8,128)(2,1)} %get-tuple-element.23), channel_id=1, source_target_pairs={{0,24},{8,0},{16,8},{24,16},{1,25},{9,1},{17,9},{25,17},{2,26},{10... | collective-permute-start | bytes 884744 | tf_op jit(solution)/shard_map/ppermute | solution.py:339
  78.1 17.2 %collective-permute-start.4 = (bf16[576,128]{1,0:T(8,128)(2,1)}, bf16[576,128]{1,0:T(8,128)(2,1)}, u32[]{:S(2)}, u32[]{:S(2)}) collective-permute-start(bf16[576,128]{1,0:T(8,128)(2,1)} %copy-done.5), channel_id=1, source_target_pairs={{0,8},{8,16},{16,24},{24,0},{1,9},{9,17},{17,25},{25,1},{2,10},{10... | collective-permute-start | bytes 442376 | tf_op jit(solution)/shard_map/ppermute | solution.py:339
  81.6 16.9 %collective-permute-start.5 = (bf16[576,128]{1,0:T(8,128)(2,1)}, bf16[576,128]{1,0:T(8,128)(2,1)}, u32[]{:S(2)}, u32[]{:S(2)}) collective-permute-start(bf16[576,128]{1,0:T(8,128)(2,1)} %copy-done.6), channel_id=1, source_target_pairs={{0,24},{8,0},{16,8},{24,16},{1,25},{9,1},{17,9},{25,17},{2,26},{10... | collective-permute-start | bytes 442376 | tf_op jit(solution)/shard_map/ppermute | solution.py:339
  98.5 1.0 copy-start.2
  99.6 1.0 copy-start.3
  100.5 0.7 copy-start.15
  104.6 22.0 %copy-start.8 = (bf16[256,128]{1,0:T(8,128)(2,1)}, bf16[256,128]{1,0:T(8,128)(2,1)S(1)}, u32[]{:S(2)}) copy-start(bf16[256,128]{1,0:T(8,128)(2,1)S(1)} %get-tuple-element.31.placing) | copy-start | bytes 196612
  104.6 22.0 %copy-start.10 = (bf16[128,128]{1,0:T(8,128)(2,1)}, bf16[128,128]{1,0:T(8,128)(2,1)S(1)}, u32[]{:S(2)}) copy-start(bf16[128,128]{1,0:T(8,128)(2,1)S(1)} %get-tuple-element.32.queries_t) | copy-start | bytes 98308
  104.6 22.0 %copy-start.16 = (bf16[32,128]{1,0:T(8,128)(2,1)}, bf16[32,128]{1,0:T(8,128)(2,1)S(1)}, u32[]{:S(2)}) copy-start(bf16[32,128]{1,0:T(8,128)(2,1)S(1)} %get-tuple-element.30) | copy-start | bytes 24580
  104.6 27.5 %copy-start.4 = (bf16[1152,128]{1,0:T(8,128)(2,1)S(1)}, bf16[1152,128]{1,0:T(8,128)(2,1)}, u32[]{:S(2)}) copy-start(bf16[1152,128]{1,0:T(8,128)(2,1)} %get-tuple-element.27.refs_0_) | copy-start | bytes 884740
  126.6 13.8 %all-to-all-start.3 = ((bf16[8,288,128]{2,1,0:T(8,128)(2,1)}), bf16[8,288,128]{2,1,0:T(8,128)(2,1)S(1)}, u32[]{:S(2)}, u32[]{:S(2)}) async-start(bf16[8,288,128]{2,1,0:T(8,128)(2,1)} %get-tuple-element.25), calls=%async_computation.3 | async-start | bytes 1179648 | tf_op jit(solution)/shard_map/all_to_all | solution.py:448
  130.7 2.9 %collective-permute-start.6 = (bf16[32,128]{1,0:T(8,128)(2,1)}, bf16[32,128]{1,0:T(8,128)(2,1)S(1)}, u32[]{:S(2)}, u32[]{:S(2)}) collective-permute-start(bf16[32,128]{1,0:T(8,128)(2,1)} %copy-done.16), channel_id=1, source_target_pairs={{0,0},{4,8},{8,16},{12,24},{16,4},{20,12},{24,20},{28,28},{1,1},{5... | collective-permute-start | bytes 24584 | tf_op jit(solution)/shard_map/ppermute | solution.py:433
  149.9 28.0 %copy-start.9 = (bf16[256,128]{1,0:T(8,128)(2,1)S(1)}, bf16[256,128]{1,0:T(8,128)(2,1)}, u32[]{:S(2)}) copy-start(bf16[256,128]{1,0:T(8,128)(2,1)} %copy-done.8) | copy-start | bytes 196612
  150.0 28.0 %copy-start.11 = (bf16[128,128]{1,0:T(8,128)(2,1)S(1)}, bf16[128,128]{1,0:T(8,128)(2,1)}, u32[]{:S(2)}) copy-start(bf16[128,128]{1,0:T(8,128)(2,1)} %copy-done.10) | copy-start | bytes 98308

commit v4 on v3

--- a/solution.py
+++ b/solution.py
@@ -21,7 +21,8 @@
 RETURN_ROWS = TILES * HEAD_SIZE + 16
 FRESH_ROWS = 32
 PIECE_TOKENS = 512
-PIECES = ((0, 0, 512), (1, 0, 512), (3, 0, 512), (2, 0, 256), (2, 256, 256))
+PIECE_ROWS = 2 * PIECE_TOKENS + 2 * RANK * PIECE_TOKENS // LANES
+SHIFTS = (0, 1, 3, 2)
 SCORE_SCALE = HEAD_SIZE**-0.5
 F32 = jnp.float32
 BF16 = jnp.bfloat16
@@ -65,41 +66,22 @@
     return high, middle, value - high - middle
 
 
-def pack_kernel(place, keys, values, factors, features, copies, *rest):
-    pieces, sems = rest[:-1], rest[-1]
-    own = place[1]
-    moves = []
-    for (shift, start, count), piece in zip(PIECES, pieces):
-        head = lax.rem(own + shift, Y_HIGH)
-        columns = pl.ds(pl.multiple_of(head * HEAD_SIZE, HEAD_SIZE), HEAD_SIZE)
-        tokens = pl.ds(start, count)
-        first = start // LANES * 2 * RANK
-        rows = count // LANES * 2 * RANK
-        moves += [
-            (keys.at[tokens, columns], piece.at[pl.ds(0, count), :]),
-            (values.at[tokens, columns], piece.at[pl.ds(count, count), :]),
-            (factors.at[pl.ds(first, rows), :], piece.at[pl.ds(2 * count, rows), :]),
-        ]
-    moves = [pltpu.make_async_copy(*move, sems.at[i]) for i, move in enumerate(moves)]
-    for move in moves:
-        move.start()
-    mine = features[...]
-    for member in range(Y):
-        copies[member] = mine
-    for move in moves:
-        move.wait()
-
-
-def spread_kernel(features, held_right, held_left, copies):
-    for member in range(X):
-        copies[member] = features[...]
+def pack_kernel(keys, values, factors, message):
+    for head in range(Y_HIGH):
+        columns = slice(head * HEAD_SIZE, (head + 1) * HEAD_SIZE)
+        message[head, 0:PIECE_TOKENS, :] = keys[:, columns]
+        message[head, PIECE_TOKENS : 2 * PIECE_TOKENS, :] = values[:, columns]
+        message[head, 2 * PIECE_TOKENS :, :] = factors[...]
 
 
 def project_kernel(
     groups,
     place,
     page_slots,
-    features,
+    features_0,
+    features_1,
+    features_2,
+    features_3,
     query_weight_far,
     key_value_weight_far,
     down_far,
@@ -108,10 +90,7 @@
     key_value_up_far,
     adapters,
     documents,
-    held_right,
-    held_left,
-    held_far_right,
-    held_far_left,
+    held,
     message,
     fresh,
     queries_t,
@@ -136,22 +115,24 @@
     for move in moves:
         move.start()
     device = place[0]
-    part = gain.shape[1]
+    part = gain.shape[2]
     width = normed.shape[0]
-    rows = features.shape[-1]
+    rows = adapters.shape[1]
+    sources = (features_0, features_1, features_2, features_3)
 
     squares = jnp.zeros((part, rows), F32)
-    for x in range(X):
+    for features in sources:
         for y in range(Y):
-            block = features[x, y].astype(F32)
+            block = features[y].astype(F32)
             squares = squares + block * block
     scale = lax.rsqrt(jnp.sum(squares, axis=0, keepdims=True) / width + 1e-06)
-    gain_t = gain[...].T
-    for x in range(X):
+    for shift, features in zip(SHIFTS, sources):
+        x = lax.rem(device + shift, X)
+        gain_t = gain[x].T
         for y in range(Y):
-            t = y * X + x
-            block = features[x, y].astype(F32) * scale * gain_t[:, t : t + 1]
-            normed[t * part : (t + 1) * part, :] = block.astype(BF16)
+            block = features[y].astype(F32) * scale * gain_t[:, y : y + 1]
+            start = pl.multiple_of((y * X + x) * part, 32)
+            normed[pl.ds(start, part), :] = block.astype(BF16)
     for move in moves:
         move.wait()
     query_total = dot(query_weight[...], normed[...], 0, 0)
@@ -217,27 +198,24 @@
             message[member, start + HEAD_SIZE : start + QUERY_ROWS, :] = factors[:, lanes]
 
 
-def prepare_kernel(*refs):
-    pieces, (keys, values_t) = refs[:-2], refs[-2:]
+def prepare_kernel(pieces, keys, values_t):
     tokens = keys.shape[0]
     ones = lax.broadcasted_iota(jnp.int32, (values_t.shape[0] - QUERY_ROWS, tokens), 0) == 0
     values_t[QUERY_ROWS:, :] = ones.astype(F32).astype(BF16)
-    base = 0
-    for (_, _, count), piece in zip(PIECES, pieces):
-        for page in range(count // LANES):
+    for index in range(Y_HIGH):
+        for page in range(PIECE_TOKENS // LANES):
             start = page * LANES
-            here = slice(base + start, base + start + LANES)
-            row = 2 * count + page * 2 * RANK
-            factors = piece[row : row + 2 * RANK, :]
+            here = slice(index * PIECE_TOKENS + start, index * PIECE_TOKENS + start + LANES)
+            row = 2 * PIECE_TOKENS + page * 2 * RANK
+            factors = pieces[index, row : row + 2 * RANK, :]
             key_factors = jnp.concatenate(
                 [factors[0:RANK].astype(F32), jnp.zeros((LANES - RANK, LANES), F32)], axis=0
             )
-            keys[here, 0:HEAD_SIZE] = piece[start : start + LANES, :]
+            keys[here, 0:HEAD_SIZE] = pieces[index, start : start + LANES, :]
             keys[here, HEAD_SIZE:] = key_factors.T.astype(BF16)
-            value = piece[count + start : count + start + LANES, :]
+            value = pieces[index, PIECE_TOKENS + start : PIECE_TOKENS + start + LANES, :]
             values_t[0:HEAD_SIZE, here] = value.astype(F32).T.astype(BF16)
             values_t[HEAD_SIZE:QUERY_ROWS, here] = factors[RANK:]
-        base += count
 
 
 def attend_kernel(
@@ -333,10 +311,6 @@
     own_weight = jnp.exp(own - peak)
     result = (shared * shared_weight + value * own_weight) / (shared_weight + own_weight)
     out[...] = result.T.astype(BF16)
-
-
-def send(value, shift):
-    return lax.ppermute(value, "yh", [(i, (i + shift) % Y_HIGH) for i in range(Y_HIGH)])
 
 
 def per_device(
@@ -364,34 +338,24 @@
     query_up = query_up_factors.reshape(-1, HEAD_SIZE)
     key_value_up = key_value_up_factors.reshape(-1, key_value_up_factors.shape[2])
 
-    piece_shapes = [shape(2 * n + 2 * RANK * n // LANES, HEAD_SIZE) for _, _, n in PIECES]
-    features, own, right, left, far_right, far_left = call(
+    features = jnp.broadcast_to(residual_input.T[None], (Y, part, rows))
+    features = lax.all_to_all(features, ("yh", "yl"), 0, 0, tiled=True)
+    pieces = call(
         pack_kernel,
-        [shape(Y, part, rows)] + piece_shapes,
-        [SMEM, HBM, HBM, HBM, VMEM],
-        [pltpu.SemaphoreType.DMA((3 * len(PIECES),))],
+        shape(Y_HIGH, PIECE_ROWS, HEAD_SIZE),
+        [VMEM] * 3,
         moved=3 * 1024 * 1024,
-        limit=60,
-        out_specs=[VMEM] + [HBM] * len(PIECES),
     )(
-        place,
         paged_base_keys.reshape(PIECE_TOKENS, -1),
         paged_base_values.reshape(PIECE_TOKENS, -1),
         paged_down_factors.transpose(0, 2, 1).reshape(-1, LANES),
-        residual_input.T,
-    )
-    far_right, far_left = send(far_right, 1), send(far_left, -1)
-    features = lax.all_to_all(features, ("yh", "yl"), 0, 0, tiled=True)
-
-    features = call(
-        spread_kernel,
-        shape(X, Y * part, rows),
-        [VMEM, ANY, ANY],
-        moved=1024 * 1024,
-    )(features.reshape(Y * part, rows), far_right, far_left)
-    far_right, far_left = send(far_right, 1), send(far_left, -1)
-    right, left = send(right, 1), send(left, -1)
-    features = lax.all_to_all(features, "x", 0, 0, tiled=True).reshape(X, Y, part, rows)
+    )
+    features, pieces = lax.optimization_barrier((features, pieces))
+    pieces = lax.all_to_all(pieces, "yh", 0, 0, tiled=True)
+    sources = [
+        lax.ppermute(features, "x", [(i, (i - shift) % X) for i in range(X)]) if shift else features
+        for shift in SHIFTS
+    ]
 
     message, fresh, queries_t, placing = call(
         functools.partial(project_kernel, groups),
@@ -401,7 +365,7 @@
             shape(HEAD_SIZE, rows),
             shape(SLOTS, rows),
         ],
-        [SMEM, SMEM, VMEM, HBM, HBM, HBM, VMEM, HBM, HBM, VMEM, VMEM] + [ANY] * 4,
+        [SMEM, SMEM] + [VMEM] * X + [HBM, HBM, HBM, VMEM, HBM, HBM, VMEM, VMEM, ANY],
         [
             pltpu.VMEM((width, rows), BF16),
             pltpu.VMEM((width, HEAD_SIZE), BF16),
@@ -416,19 +380,16 @@
     )(
         place,
         document_page_slots,
-        features,
+        *sources,
         query_weight,
         key_value_weight.T,
         shared_down_factors.T,
-        input_norm_gain.reshape(Y * X, part),
+        input_norm_gain.reshape(Y, X, part).transpose(1, 0, 2),
         query_up,
         key_value_up,
         adapter_of_row.reshape(1, rows),
         document_of_row.reshape(1, rows),
-        right,
-        left,
-        far_right,
-        far_left,
+        pieces,
     )
     fresh = lax.ppermute(
         fresh,
@@ -444,16 +405,15 @@
         flops=2 * 256 * 256 * 128,
         moved=1024 * 1024,
     )(place, received, key_value_up)
-    pieces = (own, right, left, far_right, far_left)
     gathered = lax.all_to_all(message, ("yl", "x"), 0, 0, tiled=True)
 
     tokens = PIECE_TOKENS * Y_HIGH
     keys, values_t = call(
         prepare_kernel,
         [shape(tokens, 2 * HEAD_SIZE), shape(QUERY_ROWS + 16, tokens)],
-        [VMEM] * len(pieces),
+        [VMEM],
         moved=3 * 1024 * 1024,
-    )(*pieces)
+    )(pieces)
     message = call(
         attend_kernel,
         shape(BLOCK, RETURN_ROWS + FRESH_ROWS, LANES),

time: 180 us -> 136 us (0.76)
  Pallas kernels: 56.9 us -> 17.8 us
  starting transfers between devices: 39.5 us -> 28.9 us
  local copies, waits for them, and re-layouts: 4.81 us -> 8.69 us
    pallas_call x2 -> x1, Pallas kernels: 39.7 us -> 1.24 us  [per_device(): call(pack_kernel, shape(Y_HIGH, PIECE_ROWS, HEAD_SIZE), [VMEM] * 3, moved...]
    ppermute x6 -> x3, waiting for transfers between devices: 22 us -> 7.37 us  [per_device(): lax.ppermute(features, 'x', [(i, (i - shift) % X) for i in range(X)])]
    ppermute x6 -> x3, starting transfers between devices: 22.2 us -> 13 us  [per_device(): lax.ppermute(features, 'x', [(i, (i - shift) % X) for i in range(X)])]
    all_to_all x1, waiting for transfers between devices: 0.01 us -> 7.81 us  [per_device(): pieces = lax.all_to_all(pieces, 'yh', 0, 0, tiled=True)]
    all_to_all x1, waiting for transfers between devices: 0.01 us -> 6.98 us  [per_device(): features = lax.all_to_all(features, ('yh', 'yl'), 0, 0, tiled=True)]
    unnamed x34 -> x32, local copies, waits for them, and re-layouts: 4.01 us -> 7 us
  transfers between devices with their start and end apart: 10 -> 7, of which waited for: 5 -> 4; matrix products, arithmetic and copies ran while one was open for 0% -> 0% of each run, Pallas kernels for 1% -> 1%
where the time goes in v4:
time: 136 us; the launch traced here: 135 us
  blocking collectives  49.6 us (36%)
  waiting for transfers between devices  29.9 us (22%)
  starting transfers between devices  28.9 us (21%)
  Pallas kernels  17.8 us (13%)
  local copies, waits for them, and re-layouts  8.69 us (6%)
    all_to_all x2, blocking collectives, per_device(): received = lax.all_to_all(message, 'grp', 0, 0, tiled=True)  35.4 us
    all_to_all x1, blocking collectives, per_device(): partials = lax.all_to_all(message, ('yl', 'x'), 0, 0, tiled=True)  14.2 us
    ppermute x3, starting transfers between devices, per_device(): lax.ppermute(features, 'x', [(i, (i - shift) % X) for i in range(X)])  13 us
    pallas_call x1, Pallas kernels, per_device(): call(attend_kernel, shape(BLOCK, RETURN_ROWS + FRESH_ROWS, LANES), [SMEM]...  9.5 us
    all_to_all x1, waiting for transfers between devices, per_device(): pieces = lax.all_to_all(pieces, 'yh', 0, 0, tiled=True)  7.81 us
    all_to_all x1, waiting for transfers between devices, per_device(): gathered = lax.all_to_all(message, ('yl', 'x'), 0, 0, tiled=True)  7.7 us
    all_to_all x1, starting transfers between devices, per_device(): features = lax.all_to_all(features, ('yh', 'yl'), 0, 0, tiled=True)  7.65 us
    ppermute x3, waiting for transfers between devices, per_device(): lax.ppermute(features, 'x', [(i, (i - shift) % X) for i in range(X)])  7.37 us
  transfers between devices with their start and end apart: 7, of which 4 were waited for; matrix products, arithmetic and copies ran while one was open for 0% of the time, Pallas kernels for 1%

profile of v4, /device:TPU:1, one launch (start us, length us, event | category | flops | bytes accessed | tf_op | source)
XLA Modules:
  0.0 135.1 jit_solution(7335106166695752782)
XLA Ops:
  0.0 1.6 %broadcast_in_dim.2 = bf16[8,160,128]{2,1,0:T(8,128)(2,1)} broadcast(bf16[160,128]{1,0:T(8,128)(2,1)} %bitcast.29), dimensions={1,2} | broadcast | bytes 368640 | tf_op jit(solution)/shard_map/broadcast_in_dim | solution.py:341
  1.6 7.7 %all-to-all-start = ((bf16[8,160,128]{2,1,0:T(8,128)(2,1)}), bf16[8,160,128]{2,1,0:T(8,128)(2,1)S(1)}, u32[]{:S(2)}, u32[]{:S(2)}) async-start(bf16[8,160,128]{2,1,0:T(8,128)(2,1)} %broadcast_in_dim.2), calls=%async_computation | async-start | bytes 655360 | tf_op jit(solution)/shard_map/all_to_all | solution.py:342
  9.3 1.0 copy-done.3
  10.3 0.8 copy-done.7
  11.1 1.2 shard_map.127
  12.3 7.0 %all-to-all-done.features_0 = bf16[8,160,128]{2,1,0:T(8,128)(2,1)S(1)} async-done(((bf16[8,160,128]{2,1,0:T(8,128)(2,1)}), bf16[8,160,128]{2,1,0:T(8,128)(2,1)S(1)}, u32[]{:S(2)}, u32[]{:S(2)}) %all-to-all-start) | async-done | bytes 327712 | tf_op jit(solution)/shard_map/all_to_all | solution.py:342
  19.3 3.5 %all-to-all-start.1 = ((bf16[4,1152,128]{2,1,0:T(8,128)(2,1)}), bf16[4,1152,128]{2,1,0:T(8,128)(2,1)S(1)}, u32[]{:S(2)}, u32[]{:S(2)}) async-start(bf16[4,1152,128]{2,1,0:T(8,128)(2,1)} %shard_map.127), calls=%async_computation.1 | async-start | bytes 2359296 | tf_op jit(solution)/shard_map/all_to_all | solution.py:354
  22.9 6.5 %collective-permute-start.2 = (bf16[8,160,128]{2,1,0:T(8,128)(2,1)S(1)}, bf16[8,160,128]{2,1,0:T(8,128)(2,1)}, u32[]{:S(2)}, u32[]{:S(2)}) collective-permute-start(bf16[8,160,128]{2,1,0:T(8,128)(2,1)S(1)} %all-to-all-done.features_0), channel_id=1, source_target_pairs={{0,2},{1,3},{2,0},{3,1},{4,6},{5,7},{6,4},{7,5},{8,10},{9,11},{10,... | collective-permute-start | bytes 983048 | tf_op jit(solution)/shard_map/ppermute | solution.py:356
  29.4 2.2 %collective-permute-start.1 = (bf16[8,160,128]{2,1,0:T(8,128)(2,1)S(1)}, bf16[8,160,128]{2,1,0:T(8,128)(2,1)}, u32[]{:S(2)}, u32[]{:S(2)}) collective-permute-start(bf16[8,160,128]{2,1,0:T(8,128)(2,1)S(1)} %all-to-all-done.features_0), channel_id=1, source_target_pairs={{0,1},{1,2},{2,3},{3,0},{4,5},{5,6},{6,7},{7,4},{8,9},{9,10},{10,1... | collective-permute-start | bytes 983048 | tf_op jit(solution)/shard_map/ppermute | solution.py:356
  31.6 4.3 %collective-permute-start = (bf16[8,160,128]{2,1,0:T(8,128)(2,1)S(1)}, bf16[8,160,128]{2,1,0:T(8,128)(2,1)}, u32[]{:S(2)}, u32[]{:S(2)}) collective-permute-start(bf16[8,160,128]{2,1,0:T(8,128)(2,1)S(1)} %all-to-all-done.features_0), channel_id=1, source_target_pairs={{0,3},{1,0},{2,1},{3,2},{4,7},{5,4},{6,5},{7,6},{8,11},{9,8},{10,9... | collective-permute-start | bytes 983048 | tf_op jit(solution)/shard_map/ppermute | solution.py:356
  35.9 0.1 reshape.28
  36.0 0.1 pad_add_fusion.place
  36.1 7.4 %collective-permute-done.1.features_2 = bf16[8,160,128]{2,1,0:T(8,128)(2,1)} collective-permute-done((bf16[8,160,128]{2,1,0:T(8,128)(2,1)S(1)}, bf16[8,160,128]{2,1,0:T(8,128)(2,1)}, u32[]{:S(2)}, u32[]{:S(2)}) %collective-permute-start.1) | collective-permute-done | bytes 327712 | tf_op jit(solution)/shard_map/ppermute | solution.py:356
  43.5 7.8 %all-to-all-done.1.held.pieces = bf16[4,1152,128]{2,1,0:T(8,128)(2,1)S(1)} async-done(((bf16[4,1152,128]{2,1,0:T(8,128)(2,1)}), bf16[4,1152,128]{2,1,0:T(8,128)(2,1)S(1)}, u32[]{:S(2)}, u32[]{:S(2)}) %all-to-all-start.1) | async-done | bytes 1179680 | tf_op jit(solution)/shard_map/all_to_all | solution.py:354
  51.3 1.0 copy-done.4
  52.3 1.0 copy-done.5
  53.3 0.7 copy-done.10
  54.0 3.9 %shard_map.128 = (bf16[16,32,128]{2,1,0:T(8,128)(2,1)S(1)}, bf16[32,128]{1,0:T(8,128)(2,1)S(1)}, bf16[128,128]{1,0:T(8,128)(2,1)S(1)}, bf16[256,128]{1,0:T(8,128)(2,1)S(1)}) custom-call(s32[2]{0:T(128)S(1)} %pad_add_fusion.place, s32[16,128]{1,0:T(8,128)S(1)} %copy-done.8, bf16[8,160,128]{2,1,0:T(8,128)(2,1)S(1)} %all-to-all-done.features_0, ...), custom_call_target="tpu_custom_call" | custom-call | flops 335544320 | bytes 6291456 | tf_op jit(solution)/shard_map/pallas_call | solution.py:360
  57.9 0.6 copy-done.13
  58.5 22.0 %all_to_all.30.received = bf16[16,32,128]{2,1,0:T(8,128)(2,1)S(1)} all-to-all(bf16[16,32,128]{2,1,0:T(8,128)(2,1)S(1)} %get-tuple-element.17), channel_id=1, replica_groups=mesh['grp'=16,'yh'=4,'yl'=2,'x'=4] {'grp'}, dimensions={0} | all-to-all | bytes 262144 | tf_op jit(solution)/shard_map/all_to_all | solution.py:399
  80.4 1.6 %shard_map.129 = (bf16[8,288,128]{2,1,0:T(8,128)(2,1)}, f32[8,256]{1,0:T(8,128)S(1)}) custom-call(s32[2]{0:T(128)S(1)} %pad_add_fusion.place, bf16[16,32,128]{2,1,0:T(8,128)(2,1)S(1)} %all_to_all.30.received, bf16[256,1024]{1,0:T(8,128)(2,1)S(1)} %bitcast.18), custom_call_target="tpu_custom_call" | custom-call | flops 16777216 | bytes 1048576 | tf_op jit(solution)/shard_map/pallas_call | solution.py:401
  82.0 4.0 %all-to-all-start.3 = ((bf16[8,288,128]{2,1,0:T(8,128)(2,1)}), bf16[8,288,128]{2,1,0:T(8,128)(2,1)S(1)}, u32[]{:S(2)}, u32[]{:S(2)}) async-start(bf16[8,288,128]{2,1,0:T(8,128)(2,1)} %get-tuple-element.18), calls=%async_computation.3 | async-start | bytes 1179648 | tf_op jit(solution)/shard_map/all_to_all | solution.py:408
  86.0 0.7 collective-permute-start.3
  86.7 0.4 shard_map.130
  87.1 0.8 copy-done.11
  88.0 7.7 %all-to-all-done.3.queries = bf16[8,288,128]{2,1,0:T(8,128)(2,1)S(1)} async-done(((bf16[8,288,128]{2,1,0:T(8,128)(2,1)}), bf16[8,288,128]{2,1,0:T(8,128)(2,1)S(1)}, u32[]{:S(2)}, u32[]{:S(2)}) %all-to-all-start.3) | async-done | bytes 589856 | tf_op jit(solution)/shard_map/all_to_all | solution.py:408
  95.7 1.1 copy-done.12
  96.8 9.5 %shard_map.131 = bf16[8,304,128]{2,1,0:T(8,128)(2,1)S(1)} custom-call(s32[2]{0:T(128)S(1)} %pad_add_fusion.place, bf16[8,288,128]{2,1,0:T(8,128)(2,1)S(1)} %all-to-all-done.3.queries, f32[8,256]{1,0:T(8,128)S(1)} %get-tuple-element.19.slot_adapters, bf16[256,1024]{1,0:T(8,128)(2,1)S(1)} %bitcast.19, bf16[2048,256]{1,0:T(8,128)(2,1)S(1)} %get-tuple-element.20.keys, ...), custom_call_target="tpu_custom_call" | custom-call | flops 4294967296 | bytes 3145728 | tf_op jit(solution)/shard_map/pallas_call | solution.py:417
  106.3 14.2 %all_to_all.31.partials = bf16[8,304,128]{2,1,0:T(8,128)(2,1)S(1)} all-to-all(bf16[8,304,128]{2,1,0:T(8,128)(2,1)S(1)} %shard_map.131), channel_id=1, replica_groups=mesh['grp'=16,'yh'=4,'yl'=2,'x'=4] {'yl','x'}, dimensions={0} | all-to-all | bytes 1245184 | tf_op jit(solution)/shard_map/all_to_all | solution.py:428
  120.5 0.2 shard_map.132
  120.7 13.5 %all_to_all.32.received = bf16[16,32,128]{2,1,0:T(8,128)(2,1)S(1)} all-to-all(bf16[16,32,128]{2,1,0:T(8,128)(2,1)S(1)} %shard_map.132), channel_id=1, replica_groups=mesh['grp'=16,'yh'=4,'yl'=2,'x'=4] {'grp'}, dimensions={0} | all-to-all | bytes 262144 | tf_op jit(solution)/shard_map/all_to_all | solution.py:437
  134.2 0.9 shard_map.133
  (28 shorter events, 0.1 us)
Async XLA Ops:
  0.0 9.2 %copy-start.2 = (bf16[4,128,512]{2,1,0:T(8,128)(2,1)S(1)}, bf16[4,128,512]{2,1,0:T(8,128)(2,1)}, u32[]{:S(2)}) copy-start(bf16[4,128,512]{2,1,0:T(8,128)(2,1)} %param.20) | copy-start | bytes 1572868
  1.6 17.7 %all-to-all-start = ((bf16[8,160,128]{2,1,0:T(8,128)(2,1)}), bf16[8,160,128]{2,1,0:T(8,128)(2,1)S(1)}, u32[]{:S(2)}, u32[]{:S(2)}) async-start(bf16[8,160,128]{2,1,0:T(8,128)(2,1)} %broadcast_in_dim.2), calls=%async_computation | async-start | bytes 655360 | tf_op jit(solution)/shard_map/all_to_all | solution.py:342
  9.2 1.0 copy-start.3
  10.3 0.8 copy-start.7
  12.3 23.6 %copy-start.15 = (f32[5120]{0:T(1024)S(1)}, f32[5120]{0:T(1024)}, u32[]{:S(2)}) copy-start(f32[5120]{0:T(1024)} %param.14) | copy-start | bytes 61444
  12.3 39.0 %copy-start = (bf16[16,16,1024]{2,1,0:T(8,128)(2,1)S(1)}, bf16[16,16,1024]{2,1,0:T(8,128)(2,1)}, u32[]{:S(2)}) copy-start(bf16[16,16,1024]{2,1,0:T(8,128)(2,1)} %param.19) | copy-start | bytes 1572868
  12.3 39.0 %copy-start.1 = (bf16[5120,128]{1,0:T(8,128)(2,1)S(1)}, bf16[5120,128]{1,0:T(8,128)(2,1)}, u32[]{:S(2)}) copy-start(bf16[5120,128]{1,0:T(8,128)(2,1)} %query_weight_far.1) | copy-start | bytes 3932164
  12.3 39.0 %copy-start.6 = (bf16[16,16,128]{2,1,0:T(8,128)(2,1)S(1)}, bf16[16,16,128]{2,1,0:T(8,128)(2,1)}, u32[]{:S(2)}) copy-start(bf16[16,16,128]{2,1,0:T(8,128)(2,1)} %param.18) | copy-start | bytes 196612
  12.3 39.0 %copy-start.8 = (s32[16,128]{1,0:T(8,128)S(1)}, s32[16,128]{1,0:T(8,128)}, u32[]{:S(2)}) copy-start(s32[16,128]{1,0:T(8,128)} %page_slots.1) | copy-start | bytes 24580
  12.3 39.0 %copy-start.9 = (s32[128]{0:T(128)S(1)}, s32[128]{0:T(128)}, u32[]{:S(2)}) copy-start(s32[128]{0:T(128)} %param.23) | copy-start | bytes 1540
  19.3 31.9 %all-to-all-start.1 = ((bf16[4,1152,128]{2,1,0:T(8,128)(2,1)}), bf16[4,1152,128]{2,1,0:T(8,128)(2,1)S(1)}, u32[]{:S(2)}, u32[]{:S(2)}) async-start(bf16[4,1152,128]{2,1,0:T(8,128)(2,1)} %shard_map.127), calls=%async_computation.1 | async-start | bytes 2359296 | tf_op jit(solution)/shard_map/all_to_all | solution.py:354
  22.9 13.2 %collective-permute-start.2 = (bf16[8,160,128]{2,1,0:T(8,128)(2,1)S(1)}, bf16[8,160,128]{2,1,0:T(8,128)(2,1)}, u32[]{:S(2)}, u32[]{:S(2)}) collective-permute-start(bf16[8,160,128]{2,1,0:T(8,128)(2,1)S(1)} %all-to-all-done.features_0), channel_id=1, source_target_pairs={{0,2},{1,3},{2,0},{3,1},{4,6},{5,7},{6,4},{7,5},{8,10},{9,11},{10,... | collective-permute-start | bytes 983048 | tf_op jit(solution)/shard_map/ppermute | solution.py:356
  29.4 14.1 %collective-permute-start.1 = (bf16[8,160,128]{2,1,0:T(8,128)(2,1)S(1)}, bf16[8,160,128]{2,1,0:T(8,128)(2,1)}, u32[]{:S(2)}, u32[]{:S(2)}) collective-permute-start(bf16[8,160,128]{2,1,0:T(8,128)(2,1)S(1)} %all-to-all-done.features_0), channel_id=1, source_target_pairs={{0,1},{1,2},{2,3},{3,0},{4,5},{5,6},{6,7},{7,4},{8,9},{9,10},{10,1... | collective-permute-start | bytes 983048 | tf_op jit(solution)/shard_map/ppermute | solution.py:356
  31.6 11.9 %collective-permute-start = (bf16[8,160,128]{2,1,0:T(8,128)(2,1)S(1)}, bf16[8,160,128]{2,1,0:T(8,128)(2,1)}, u32[]{:S(2)}, u32[]{:S(2)}) collective-permute-start(bf16[8,160,128]{2,1,0:T(8,128)(2,1)S(1)} %all-to-all-done.features_0), channel_id=1, source_target_pairs={{0,3},{1,0},{2,1},{3,2},{4,7},{5,4},{6,5},{7,6},{8,11},{9,8},{10,9... | collective-permute-start | bytes 983048 | tf_op jit(solution)/shard_map/ppermute | solution.py:356
  51.3 1.0 copy-start.4
  52.3 1.0 copy-start.5
  53.3 0.7 copy-start.10
  57.9 0.6 copy-start.13
  58.5 27.6 %copy-start.14 = (bf16[32,128]{1,0:T(8,128)(2,1)S(1)}, bf16[32,128]{1,0:T(8,128)(2,1)}, u32[]{:S(2)}) copy-start(bf16[32,128]{1,0:T(8,128)(2,1)} %copy-done.13) | copy-start | bytes 24580
  82.0 13.7 %all-to-all-start.3 = ((bf16[8,288,128]{2,1,0:T(8,128)(2,1)}), bf16[8,288,128]{2,1,0:T(8,128)(2,1)S(1)}, u32[]{:S(2)}, u32[]{:S(2)}) async-start(bf16[8,288,128]{2,1,0:T(8,128)(2,1)} %get-tuple-element.18), calls=%async_computation.3 | async-start | bytes 1179648 | tf_op jit(solution)/shard_map/all_to_all | solution.py:408
  86.0 1.9 %collective-permute-start.3 = (bf16[32,128]{1,0:T(8,128)(2,1)S(1)}, bf16[32,128]{1,0:T(8,128)(2,1)S(1)}, u32[]{:S(2)}, u32[]{:S(2)}) collective-permute-start(bf16[32,128]{1,0:T(8,128)(2,1)S(1)} %copy-done.14), channel_id=1, source_target_pairs={{0,0},{4,8},{8,16},{12,24},{16,4},{20,12},{24,20},{28,28},{1,1},{5... | collective-permute-start | bytes 24584 | tf_op jit(solution)/shard_map/ppermute | solution.py:394
  87.1 0.8 copy-start.11
  95.7 1.1 copy-start.12

commit v5 on v4

--- a/solution.py
+++ b/solution.py
@@ -20,6 +20,8 @@
 MESSAGE_ROWS = TILES * QUERY_ROWS
 RETURN_ROWS = TILES * HEAD_SIZE + 16
 FRESH_ROWS = 32
+DEPTH = 2 * HEAD_SIZE
+VALUE_ROWS = QUERY_ROWS + 16
 PIECE_TOKENS = 512
 PIECE_ROWS = 2 * PIECE_TOKENS + 2 * RANK * PIECE_TOKENS // LANES
 SHIFTS = (0, 1, 3, 2)
@@ -29,7 +31,6 @@
 VMEM = pl.BlockSpec(memory_space=pltpu.VMEM)
 SMEM = pl.BlockSpec(memory_space=pltpu.SMEM)
 ANY = pl.BlockSpec(memory_space=pl.ANY)
-HBM = pl.BlockSpec(memory_space=pltpu.HBM)
 
 
 def dot(left, right, left_dim, right_dim):
@@ -74,53 +75,72 @@
         message[head, 2 * PIECE_TOKENS :, :] = factors[...]
 
 
+def plan_kernel(
+    groups,
+    page_slots,
+    query_weight,
+    key_value_weight,
+    down,
+    adapters,
+    documents,
+    weights,
+    placing,
+    slot_adapters,
+):
+    for start in range(0, weights.shape[1], LANES):
+        block = query_weight[start : start + LANES, :].astype(F32).T
+        weights[0:HEAD_SIZE, start : start + LANES] = block.astype(BF16)
+    weights[HEAD_SIZE : HEAD_SIZE + FRESH_ROWS, :] = key_value_weight[...]
+    weights[HEAD_SIZE + FRESH_ROWS :, :] = down[...]
+
+    document = documents[...]
+    rows = document.shape[1]
+    target = jnp.zeros_like(document)
+    for d in range(page_slots.shape[0]):
+        target = jnp.where(document == d, page_slots[d, 0] // page_slots.shape[1], target)
+    capacity = SLOTS // groups
+    group = lax.broadcasted_iota(jnp.int32, (16, rows), 0)
+    match = (group == target).astype(F32)
+    before = (
+        lax.broadcasted_iota(jnp.int32, (rows, rows), 0)
+        < lax.broadcasted_iota(jnp.int32, (rows, rows), 1)
+    ).astype(F32)
+    earlier = dot(match.astype(BF16), before.astype(BF16), 1, 0)
+    position = jnp.sum(earlier * match, axis=0, keepdims=True).astype(jnp.int32)
+    slot = target * capacity + position
+    placed = (lax.broadcasted_iota(jnp.int32, (SLOTS, rows), 0) == slot).astype(F32)
+    placing[...] = placed.astype(BF16)
+    adapter = jnp.sum(placed * adapters[...].astype(F32), axis=1, keepdims=True)
+    slot_adapters[...] = jnp.broadcast_to(adapter, (SLOTS, LANES)).astype(BF16)
+
+
 def project_kernel(
     groups,
     place,
-    page_slots,
     features_0,
     features_1,
     features_2,
     features_3,
-    query_weight_far,
-    key_value_weight_far,
-    down_far,
+    weights,
     gain,
-    query_up_far,
-    key_value_up_far,
+    query_up,
+    key_value_up,
     adapters,
-    documents,
+    placing,
+    slot_adapters,
     held,
     message,
     fresh,
     queries_t,
-    placing,
     normed,
-    query_weight,
-    weights,
-    query_up,
-    key_value_up,
     update,
-    sems,
 ):
-    columns = pl.ds(pl.multiple_of(place[0] // X * HEAD_SIZE, HEAD_SIZE), HEAD_SIZE)
-    moves = [
-        (query_weight_far, query_weight),
-        (key_value_weight_far, weights.at[pl.ds(0, FRESH_ROWS), :]),
-        (down_far, weights.at[pl.ds(FRESH_ROWS, 3 * RANK), :]),
-        (query_up_far, query_up),
-        (key_value_up_far.at[:, columns], key_value_up),
-    ]
-    moves = [pltpu.make_async_copy(*move, sems.at[i]) for i, move in enumerate(moves)]
-    for move in moves:
-        move.start()
     device = place[0]
     part = gain.shape[2]
     width = normed.shape[0]
-    rows = adapters.shape[1]
     sources = (features_0, features_1, features_2, features_3)
 
-    squares = jnp.zeros((part, rows), F32)
+    squares = jnp.zeros((part, normed.shape[1]), F32)
     for features in sources:
         for y in range(Y):
             block = features[y].astype(F32)
@@ -133,47 +153,26 @@
             block = features[y].astype(F32) * scale * gain_t[:, y : y + 1]
             start = pl.multiple_of((y * X + x) * part, 32)
             normed[pl.ds(start, part), :] = block.astype(BF16)
-    for move in moves:
-        move.wait()
-    query_total = dot(query_weight[...], normed[...], 0, 0)
     total = dot(weights[...], normed[...], 1, 0)
 
     adapter = adapters[...]
-    low = total[FRESH_ROWS:].astype(BF16)
+    low = total[HEAD_SIZE + FRESH_ROWS :].astype(BF16)
     query_update = dot(query_up[...], of_adapter(low[0:RANK], adapter), 0, 0)
-    queries = (query_total + query_update).astype(BF16)
+    queries = (total[0:HEAD_SIZE] + query_update).astype(BF16)
     queries_t[...] = queries
 
     is_key = device < Y * X // 2
     low_kv = jnp.where(is_key, low[RANK : 2 * RANK], low[2 * RANK :])
-    update[...] = dot(key_value_up[...], of_adapter(low_kv, adapter), 0, 0)
-    mine = pl.ds(pl.multiple_of(lax.rem(device, X) * 32, 32), 32)
-    fresh[...] = (total[0:FRESH_ROWS] + update[mine, :]).astype(BF16)
-
-    document = documents[...]
-    target = jnp.zeros_like(document)
-    for d in range(page_slots.shape[0]):
-        target = jnp.where(document == d, page_slots[d, 0] // page_slots.shape[1], target)
-    capacity = SLOTS // groups
-    group = lax.broadcasted_iota(jnp.int32, (16, rows), 0)
-    match = (group == target).astype(F32)
-    before = (
-        lax.broadcasted_iota(jnp.int32, (rows, rows), 0)
-        < lax.broadcasted_iota(jnp.int32, (rows, rows), 1)
-    ).astype(F32)
-    earlier = dot(match.astype(BF16), before.astype(BF16), 1, 0)
-    position = jnp.sum(earlier * match, axis=0, keepdims=True).astype(jnp.int32)
-    slot = target * capacity + position
-    place_here = lax.broadcasted_iota(jnp.int32, (SLOTS, rows), 0) == slot
-    placed = place_here.astype(F32)
-    placing[...] = placed.astype(BF16)
-    message[:, 0:capacity, :] = (
-        dot(placed.astype(BF16), queries, 1, 1).astype(BF16).reshape(groups, capacity, HEAD_SIZE)
-    )
-    slot_adapter = jnp.sum(placed * adapter.astype(F32), axis=1, keepdims=True)
-    message[:, capacity:, :] = (
-        jnp.broadcast_to(slot_adapter, (SLOTS, LANES)).astype(BF16).reshape(groups, capacity, LANES)
-    )
+    columns = pl.ds(pl.multiple_of(device // X * HEAD_SIZE, HEAD_SIZE), HEAD_SIZE)
+    update[...] = dot(key_value_up[:, columns], of_adapter(low_kv, adapter), 0, 0)
+    mine = pl.ds(pl.multiple_of(lax.rem(device, X) * FRESH_ROWS, FRESH_ROWS), FRESH_ROWS)
+    new = total[HEAD_SIZE : HEAD_SIZE + FRESH_ROWS] + update[mine, :]
+    fresh[...] = new.astype(BF16)
+
+    capacity = SLOTS // groups
+    placed = dot(placing[...], queries, 1, 1).astype(BF16)
+    message[:, 0:capacity, :] = placed.reshape(groups, capacity, HEAD_SIZE)
+    message[:, capacity:, :] = slot_adapters[...].reshape(groups, capacity, LANES)
 
 
 def factor_kernel(groups, place, received, key_value_up, message, slot_adapters):
@@ -198,57 +197,84 @@
             message[member, start + HEAD_SIZE : start + QUERY_ROWS, :] = factors[:, lanes]
 
 
-def prepare_kernel(pieces, keys, values_t):
-    tokens = keys.shape[0]
-    ones = lax.broadcasted_iota(jnp.int32, (values_t.shape[0] - QUERY_ROWS, tokens), 0) == 0
-    values_t[QUERY_ROWS:, :] = ones.astype(F32).astype(BF16)
+def prepare_kernel(pieces, prepared):
+    tokens = PIECE_TOKENS * Y_HIGH
+    ones = lax.broadcasted_iota(jnp.int32, (VALUE_ROWS - QUERY_ROWS, DEPTH), 0) == 0
     for index in range(Y_HIGH):
         for page in range(PIECE_TOKENS // LANES):
             start = page * LANES
-            here = slice(index * PIECE_TOKENS + start, index * PIECE_TOKENS + start + LANES)
+            token = index * PIECE_TOKENS + start
+            here = slice(token, token + LANES)
             row = 2 * PIECE_TOKENS + page * 2 * RANK
             factors = pieces[index, row : row + 2 * RANK, :]
             key_factors = jnp.concatenate(
                 [factors[0:RANK].astype(F32), jnp.zeros((LANES - RANK, LANES), F32)], axis=0
             )
-            keys[here, 0:HEAD_SIZE] = pieces[index, start : start + LANES, :]
-            keys[here, HEAD_SIZE:] = key_factors.T.astype(BF16)
+            prepared[here, 0:HEAD_SIZE] = pieces[index, start : start + LANES, :]
+            prepared[here, HEAD_SIZE:] = key_factors.T.astype(BF16)
             value = pieces[index, PIECE_TOKENS + start : PIECE_TOKENS + start + LANES, :]
-            values_t[0:HEAD_SIZE, here] = value.astype(F32).T.astype(BF16)
-            values_t[HEAD_SIZE:QUERY_ROWS, here] = factors[RANK:]
+            base = tokens + token // DEPTH * VALUE_ROWS
+            lanes = slice(token % DEPTH, token % DEPTH + LANES)
+            prepared[base : base + HEAD_SIZE, lanes] = value.astype(F32).T.astype(BF16)
+            prepared[base + HEAD_SIZE : base + QUERY_ROWS, lanes] = factors[RANK:]
+            if token % DEPTH == 0:
+                prepared[base + QUERY_ROWS : base + VALUE_ROWS, :] = ones.astype(F32).astype(BF16)
 
 
 def attend_kernel(
-    place, queries, slot_adapters, key_value_up, keys, values_t, fresh, message, query, scores
+    place, queries, slot_adapters, key_value_up, prepared, fresh, message, query, scores, totals, peaks
 ):
-    tokens = keys.shape[0]
-    depth = 2 * HEAD_SIZE
-    value_rows = values_t.shape[0]
-    query[:, QUERY_ROWS:, :] = jnp.zeros((2, depth - QUERY_ROWS, SLOTS), BF16)
-    columns = pl.ds(pl.multiple_of((place[1] + Y_HIGH) * HEAD_SIZE, HEAD_SIZE), HEAD_SIZE)
-    value_up = key_value_up[:, columns]
-    adapters = slot_adapters[0:1, :].astype(jnp.int32)
-    chunk = 512
-
-    def score_head(head, side):
+    tokens = PIECE_TOKENS * Y_HIGH
+    chunk = 1024
+    exponent = SCORE_SCALE * math.log2(math.e)
+    query[:, QUERY_ROWS:, :] = jnp.zeros((2, DEPTH - QUERY_ROWS, SLOTS), BF16)
+
+    def load(head, side):
         for tile in range(TILES):
             query[side, 0:QUERY_ROWS, tile * LANES : (tile + 1) * LANES] = queries[
                 head, tile * QUERY_ROWS : (tile + 1) * QUERY_ROWS, :
             ]
-        highest = None
+
+    def score(side, start, highest):
+        block = dot(prepared[start : start + chunk, :], query[side], 1, 0)
+        scores[side, start : start + chunk, :] = block
+        return jnp.maximum(highest, jnp.max(block.reshape(chunk // 8, 8, SLOTS), axis=0))
+
+    def add(side, start, peak, total):
+        weight = jnp.exp2(scores[side, start : start + chunk, :] * exponent - peak).astype(BF16)
+        for step in range(chunk // DEPTH):
+            base = tokens + (start // DEPTH + step) * VALUE_ROWS
+            values = prepared[base : base + VALUE_ROWS, :]
+            total = total + dot(values, weight[step * DEPTH : (step + 1) * DEPTH], 1, 0)
+        return total
+
+    lowest = jnp.full((8, SLOTS), -jnp.inf, F32)
+
+    def one_head(head, following, side, peak):
+        load(following, 1 - side)
+        highest, total = lowest, jnp.zeros((VALUE_ROWS, SLOTS), F32)
         for start in range(0, tokens, chunk):
-            score = dot(keys[start : start + chunk, :], query[side], 1, 0)
-            scores[side, start : start + chunk, :] = score
-            top = jnp.max(score.reshape(chunk // 8, 8, SLOTS), axis=0)
-            highest = top if highest is None else jnp.maximum(highest, top)
+            highest = score(1 - side, start, highest)
+            total = add(side, start, peak * exponent, total)
+        totals[head] = total
+        peaks[head] = jnp.broadcast_to(peak, (8, SLOTS))
         return jnp.max(highest, axis=0, keepdims=True)
 
-    def sum_head(head, side, peak):
-        total = jnp.zeros((value_rows, SLOTS), F32)
-        for start in range(0, tokens, chunk):
-            shifted = scores[side, start : start + chunk, :] - peak
-            weight = jnp.exp2(shifted * (SCORE_SCALE * math.log2(math.e))).astype(BF16)
-            total = total + dot(values_t[:, start : start + chunk], weight, 1, 0)
+    def two_heads(pair, peak):
+        peak = one_head(2 * pair, 2 * pair + 1, 0, peak)
+        return one_head(2 * pair + 1, jnp.minimum(2 * pair + 2, BLOCK - 1), 1, peak)
+
+    load(0, 0)
+    highest = lowest
+    for start in range(0, tokens, chunk):
+        highest = score(0, start, highest)
+    lax.fori_loop(0, BLOCK // 2, two_heads, jnp.max(highest, axis=0, keepdims=True))
+
+    columns = pl.ds(pl.multiple_of((place[1] + Y_HIGH) * HEAD_SIZE, HEAD_SIZE), HEAD_SIZE)
+    value_up = key_value_up[:, columns]
+    adapters = slot_adapters[0:1, :].astype(jnp.int32)
+    for head in range(BLOCK):
+        total, peak = totals[head], peaks[head, 0:1]
         mass = total[QUERY_ROWS : QUERY_ROWS + 1]
         inverse = 1.0 / mass
         low = (total[HEAD_SIZE:QUERY_ROWS] * inverse).astype(BF16)
@@ -263,15 +289,6 @@
             ]
         message[head, TILES * HEAD_SIZE : RETURN_ROWS, :] = stats.astype(BF16)
         message[head, RETURN_ROWS:, :] = fresh[...]
-
-    def two_heads(pair, carry):
-        first = score_head(2 * pair, 0)
-        second = score_head(2 * pair + 1, 1)
-        sum_head(2 * pair, 0, first)
-        sum_head(2 * pair + 1, 1, second)
-        return carry
-
-    lax.fori_loop(0, BLOCK // 2, two_heads, 0)
 
 
 def merge_kernel(groups, partials, message):
@@ -357,38 +374,42 @@
         for shift in SHIFTS
     ]
 
-    message, fresh, queries_t, placing = call(
+    columns = HEAD_SIZE + FRESH_ROWS + 3 * RANK
+    adapters = adapter_of_row.reshape(1, rows)
+    weights, placing, row_adapters = call(
+        functools.partial(plan_kernel, groups),
+        [shape(columns, width), shape(SLOTS, rows), shape(SLOTS, LANES)],
+        [SMEM] + [VMEM] * 5,
+        moved=5 * 1024 * 1024,
+    )(
+        document_page_slots,
+        query_weight,
+        key_value_weight.T,
+        shared_down_factors.T,
+        adapters,
+        document_of_row.reshape(1, rows),
+    )
+    message, fresh, queries_t = call(
         functools.partial(project_kernel, groups),
         [
             shape(groups, 2 * capacity, HEAD_SIZE),
             shape(FRESH_ROWS, rows),
             shape(HEAD_SIZE, rows),
-            shape(SLOTS, rows),
         ],
-        [SMEM, SMEM] + [VMEM] * X + [HBM, HBM, HBM, VMEM, HBM, HBM, VMEM, VMEM, ANY],
-        [
-            pltpu.VMEM((width, rows), BF16),
-            pltpu.VMEM((width, HEAD_SIZE), BF16),
-            pltpu.VMEM((FRESH_ROWS + 3 * RANK, width), BF16),
-            pltpu.VMEM(query_up.shape, BF16),
-            pltpu.VMEM((key_value_up.shape[0], HEAD_SIZE), BF16),
-            pltpu.VMEM((HEAD_SIZE, rows), F32),
-            pltpu.SemaphoreType.DMA((5,)),
-        ],
+        [SMEM] + [VMEM] * (X + 7) + [ANY],
+        [pltpu.VMEM((width, rows), BF16), pltpu.VMEM((HEAD_SIZE, rows), F32)],
         flops=2 * width * rows * 256,
-        moved=6 * 1024 * 1024,
+        moved=4 * 1024 * 1024,
     )(
         place,
-        document_page_slots,
         *sources,
-        query_weight,
-        key_value_weight.T,
-        shared_down_factors.T,
+        weights,
         input_norm_gain.reshape(Y, X, part).transpose(1, 0, 2),
         query_up,
         key_value_up,
-        adapter_of_row.reshape(1, rows),
-        document_of_row.reshape(1, rows),
+        adapters,
+        placing,
+        row_adapters,
         pieces,
     )
     fresh = lax.ppermute(
@@ -408,23 +429,25 @@
     gathered = lax.all_to_all(message, ("yl", "x"), 0, 0, tiled=True)
 
     tokens = PIECE_TOKENS * Y_HIGH
-    keys, values_t = call(
+    prepared = call(
         prepare_kernel,
-        [shape(tokens, 2 * HEAD_SIZE), shape(QUERY_ROWS + 16, tokens)],
+        shape(tokens + tokens // DEPTH * VALUE_ROWS, DEPTH),
         [VMEM],
         moved=3 * 1024 * 1024,
     )(pieces)
     message = call(
         attend_kernel,
         shape(BLOCK, RETURN_ROWS + FRESH_ROWS, LANES),
-        [SMEM] + [VMEM] * 6,
+        [SMEM] + [VMEM] * 5,
         [
-            pltpu.VMEM((2, 2 * HEAD_SIZE, SLOTS), BF16),
+            pltpu.VMEM((2, DEPTH, SLOTS), BF16),
             pltpu.VMEM((2, tokens, SLOTS), F32),
+            pltpu.VMEM((BLOCK, VALUE_ROWS, SLOTS), F32),
+            pltpu.VMEM((BLOCK, 8, SLOTS), F32),
         ],
         flops=4 * SLOTS * BLOCK * tokens * 256,
         moved=3 * 1024 * 1024,
-    )(place, gathered, slot_adapters, key_value_up, keys, values_t, fresh)
+    )(place, gathered, slot_adapters, key_value_up, prepared, fresh)
     partials = lax.all_to_all(message, ("yl", "x"), 0, 0, tiled=True)
 
     message = call(

time: 136 us -> 129 us (0.949)
  waiting for transfers between devices: 29.9 us -> 27.1 us
  Pallas kernels: 17.8 us -> 15.4 us
    pallas_call x1, Pallas kernels: 9.5 us -> 6.59 us  [per_device(): call(attend_kernel, shape(BLOCK, RETURN_ROWS + FRESH_ROWS, LANES), [SMEM]...]
    ppermute x3, waiting for transfers between devices: 7.37 us -> 5.79 us  [per_device(): lax.ppermute(features, 'x', [(i, (i - shift) % X) for i in range(X)])]
    all_to_all x1, waiting for transfers between devices: 7.81 us -> 6.45 us  [per_device(): pieces = lax.all_to_all(pieces, 'yh', 0, 0, tiled=True)]
  transfers between devices with their start and end apart: 7 -> 7, of which waited for: 4 -> 5; matrix products, arithmetic and copies ran while one was open for 0% -> 0% of each run, Pallas kernels for 1% -> 2%
where the time goes in v5:
time: 129 us; the launch traced here: 128 us
  blocking collectives  49 us (38%)
  starting transfers between devices  28.7 us (22%)
  waiting for transfers between devices  27.1 us (21%)
  Pallas kernels  15.4 us (12%)
  local copies, waits for them, and re-layouts  7.92 us (6%)
    all_to_all x2, blocking collectives, per_device(): received = lax.all_to_all(message, 'grp', 0, 0, tiled=True)  34.7 us
    all_to_all x1, blocking collectives, per_device(): partials = lax.all_to_all(message, ('yl', 'x'), 0, 0, tiled=True)  14.2 us
    ppermute x3, starting transfers between devices, per_device(): lax.ppermute(features, 'x', [(i, (i - shift) % X) for i in range(X)])  11.8 us
    all_to_all x1, waiting for transfers between devices, per_device(): gathered = lax.all_to_all(message, ('yl', 'x'), 0, 0, tiled=True)  7.69 us
    all_to_all x1, starting transfers between devices, per_device(): features = lax.all_to_all(features, ('yh', 'yl'), 0, 0, tiled=True)  7.65 us
    all_to_all x1, waiting for transfers between devices, per_device(): features = lax.all_to_all(features, ('yh', 'yl'), 0, 0, tiled=True)  7.18 us
    pallas_call x1, Pallas kernels, per_device(): call(attend_kernel, shape(BLOCK, RETURN_ROWS + FRESH_ROWS, LANES), [SMEM]...  6.59 us
    all_to_all x1, waiting for transfers between devices, per_device(): pieces = lax.all_to_all(pieces, 'yh', 0, 0, tiled=True)  6.45 us
  transfers between devices with their start and end apart: 7, of which 5 were waited for; matrix products, arithmetic and copies ran while one was open for 0% of the time, Pallas kernels for 2%

profile of v5, /device:TPU:1, one launch (start us, length us, event | category | flops | bytes accessed | tf_op | source)
XLA Modules:
  0.0 128.4 jit_solution(16445186251650177068)
XLA Ops:
  0.0 1.6 %broadcast_in_dim.2 = bf16[8,160,128]{2,1,0:T(8,128)(2,1)} broadcast(bf16[160,128]{1,0:T(8,128)(2,1)} %bitcast.30), dimensions={1,2} | broadcast | bytes 368640 | tf_op jit(solution)/shard_map/broadcast_in_dim | solution.py:358
  1.6 7.7 %all-to-all-start = ((bf16[8,160,128]{2,1,0:T(8,128)(2,1)}), bf16[8,160,128]{2,1,0:T(8,128)(2,1)}, u32[]{:S(2)}, u32[]{:S(2)}) async-start(bf16[8,160,128]{2,1,0:T(8,128)(2,1)} %broadcast_in_dim.2), calls=%async_computation | async-start | bytes 655360 | tf_op jit(solution)/shard_map/all_to_all | solution.py:359
  9.3 1.0 copy-done.4
  10.3 0.8 copy-done.8
  11.1 1.2 shard_map.127
  12.3 7.2 %all-to-all-done.features_0 = bf16[8,160,128]{2,1,0:T(8,128)(2,1)} async-done(((bf16[8,160,128]{2,1,0:T(8,128)(2,1)}), bf16[8,160,128]{2,1,0:T(8,128)(2,1)}, u32[]{:S(2)}, u32[]{:S(2)}) %all-to-all-start) | async-done | bytes 327712 | tf_op jit(solution)/shard_map/all_to_all | solution.py:359
  19.5 3.5 %all-to-all-start.1 = ((bf16[4,1152,128]{2,1,0:T(8,128)(2,1)}), bf16[4,1152,128]{2,1,0:T(8,128)(2,1)S(1)}, u32[]{:S(2)}, u32[]{:S(2)}) async-start(bf16[4,1152,128]{2,1,0:T(8,128)(2,1)} %shard_map.127), calls=%async_computation.1 | async-start | bytes 2359296 | tf_op jit(solution)/shard_map/all_to_all | solution.py:371
  23.1 6.3 %collective-permute-start = (bf16[8,160,128]{2,1,0:T(8,128)(2,1)}, bf16[8,160,128]{2,1,0:T(8,128)(2,1)}, u32[]{:S(2)}, u32[]{:S(2)}) collective-permute-start(bf16[8,160,128]{2,1,0:T(8,128)(2,1)} %all-to-all-done.features_0), channel_id=1, source_target_pairs={{0,3},{1,0},{2,1},{3,2},{4,7},{5,4},{6,5},{7,6},{8,11},{9,8},{10,9... | collective-permute-start | bytes 983048 | tf_op jit(solution)/shard_map/ppermute | solution.py:373
  29.4 1.9 %collective-permute-start.1 = (bf16[8,160,128]{2,1,0:T(8,128)(2,1)}, bf16[8,160,128]{2,1,0:T(8,128)(2,1)}, u32[]{:S(2)}, u32[]{:S(2)}) collective-permute-start(bf16[8,160,128]{2,1,0:T(8,128)(2,1)} %all-to-all-done.features_0), channel_id=1, source_target_pairs={{0,1},{1,2},{2,3},{3,0},{4,5},{5,6},{6,7},{7,4},{8,9},{9,10},{10,1... | collective-permute-start | bytes 983048 | tf_op jit(solution)/shard_map/ppermute | solution.py:373
  31.3 3.6 %collective-permute-start.2 = (bf16[8,160,128]{2,1,0:T(8,128)(2,1)}, bf16[8,160,128]{2,1,0:T(8,128)(2,1)}, u32[]{:S(2)}, u32[]{:S(2)}) collective-permute-start(bf16[8,160,128]{2,1,0:T(8,128)(2,1)} %all-to-all-done.features_0), channel_id=1, source_target_pairs={{0,2},{1,3},{2,0},{3,1},{4,6},{5,7},{6,4},{7,5},{8,10},{9,11},{10,... | collective-permute-start | bytes 983048 | tf_op jit(solution)/shard_map/ppermute | solution.py:373
  35.0 0.1 reshape.30
  35.1 1.3 %copy-done.2 = bf16[5120,128]{1,0:T(8,128)(2,1)S(1)} copy-done((bf16[5120,128]{1,0:T(8,128)(2,1)S(1)}, bf16[5120,128]{1,0:T(8,128)(2,1)}, u32[]{:S(2)}) %copy-start.2) | copy-done | bytes 1310744
  36.4 1.0 copy-done.5
  37.5 1.0 copy-done.6
  38.4 1.2 shard_map.128
  39.6 0.1 pad_add_fusion.place
  39.7 0.8 collective-permute-done.1.features_2
  40.5 5.0 %collective-permute-done.2.features_3 = bf16[8,160,128]{2,1,0:T(8,128)(2,1)} collective-permute-done((bf16[8,160,128]{2,1,0:T(8,128)(2,1)}, bf16[8,160,128]{2,1,0:T(8,128)(2,1)}, u32[]{:S(2)}, u32[]{:S(2)}) %collective-permute-start.2) | collective-permute-done | bytes 327712 | tf_op jit(solution)/shard_map/ppermute | solution.py:373
  45.5 6.4 %all-to-all-done.1.held.pieces = bf16[4,1152,128]{2,1,0:T(8,128)(2,1)S(1)} async-done(((bf16[4,1152,128]{2,1,0:T(8,128)(2,1)}), bf16[4,1152,128]{2,1,0:T(8,128)(2,1)S(1)}, u32[]{:S(2)}, u32[]{:S(2)}) %all-to-all-start.1) | async-done | bytes 1179680 | tf_op jit(solution)/shard_map/all_to_all | solution.py:371
  51.9 1.0 copy-done
  53.0 3.2 %shard_map.129 = (bf16[16,32,128]{2,1,0:T(8,128)(2,1)S(1)}, bf16[32,128]{1,0:T(8,128)(2,1)S(1)}, bf16[128,128]{1,0:T(8,128)(2,1)S(1)}) custom-call(s32[2]{0:T(128)S(1)} %pad_add_fusion.place, bf16[8,160,128]{2,1,0:T(8,128)(2,1)} %all-to-all-done.features_0, bf16[8,160,128]{2,1,0:T(8,128)(2,1)} %collective-permute-done.features_1, ...), custom_call_target="tpu_custom_call" | custom-call | flops 335544320 | bytes 4194304 | tf_op jit(solution)/shard_map/pallas_call | solution.py:392
  56.2 21.3 %all_to_all.30.received = bf16[16,32,128]{2,1,0:T(8,128)(2,1)S(1)} all-to-all(bf16[16,32,128]{2,1,0:T(8,128)(2,1)S(1)} %get-tuple-element.20), channel_id=1, replica_groups=mesh['grp'=16,'yh'=4,'yl'=2,'x'=4] {'grp'}, dimensions={0} | all-to-all | bytes 262144 | tf_op jit(solution)/shard_map/all_to_all | solution.py:420
  77.5 1.6 %shard_map.130 = (bf16[8,288,128]{2,1,0:T(8,128)(2,1)}, f32[8,256]{1,0:T(8,128)S(1)}) custom-call(s32[2]{0:T(128)S(1)} %pad_add_fusion.place, bf16[16,32,128]{2,1,0:T(8,128)(2,1)S(1)} %all_to_all.30.received, bf16[256,1024]{1,0:T(8,128)(2,1)S(1)} %bitcast.18), custom_call_target="tpu_custom_call" | custom-call | flops 16777216 | bytes 1048576 | tf_op jit(solution)/shard_map/pallas_call | solution.py:422
  79.1 4.2 %all-to-all-start.3 = ((bf16[8,288,128]{2,1,0:T(8,128)(2,1)}), bf16[8,288,128]{2,1,0:T(8,128)(2,1)}, u32[]{:S(2)}, u32[]{:S(2)}) async-start(bf16[8,288,128]{2,1,0:T(8,128)(2,1)} %get-tuple-element.21), calls=%async_computation.3 | async-start | bytes 1179648 | tf_op jit(solution)/shard_map/all_to_all | solution.py:429
  83.3 1.5 %collective-permute-start.3 = (bf16[32,128]{1,0:T(8,128)(2,1)}, bf16[32,128]{1,0:T(8,128)(2,1)S(1)}, u32[]{:S(2)}, u32[]{:S(2)}) collective-permute-start(bf16[32,128]{1,0:T(8,128)(2,1)} %copy-done.14), channel_id=1, source_target_pairs={{0,0},{4,8},{8,16},{12,24},{16,4},{20,12},{24,20},{28,28},{1,1},{5... | collective-permute-start | bytes 24584 | tf_op jit(solution)/shard_map/ppermute | solution.py:415
  84.8 0.4 shard_map.131.prepared
  85.3 7.7 %all-to-all-done.3.queries = bf16[8,288,128]{2,1,0:T(8,128)(2,1)} async-done(((bf16[8,288,128]{2,1,0:T(8,128)(2,1)}), bf16[8,288,128]{2,1,0:T(8,128)(2,1)}, u32[]{:S(2)}, u32[]{:S(2)}) %all-to-all-start.3) | async-done | bytes 589856 | tf_op jit(solution)/shard_map/all_to_all | solution.py:429
  93.0 6.6 %shard_map.132 = bf16[8,304,128]{2,1,0:T(8,128)(2,1)S(1)} custom-call(s32[2]{0:T(128)S(1)} %pad_add_fusion.place, bf16[8,288,128]{2,1,0:T(8,128)(2,1)} %all-to-all-done.3.queries, f32[8,256]{1,0:T(8,128)S(1)} %get-tuple-element.22.slot_adapters, bf16[256,1024]{1,0:T(8,128)(2,1)S(1)} %bitcast.19, bf16[3328,256]{1,0:T(8,128)(2,1)S(1)} %shard_map.131.prepared, ...), custom_call_target="tpu_custom_call" | custom-call | flops 4294967296 | bytes 3145728 | tf_op jit(solution)/shard_map/pallas_call | solution.py:438
  99.6 14.2 %all_to_all.31.partials = bf16[8,304,128]{2,1,0:T(8,128)(2,1)S(1)} all-to-all(bf16[8,304,128]{2,1,0:T(8,128)(2,1)S(1)} %shard_map.132), channel_id=1, replica_groups=mesh['grp'=16,'yh'=4,'yl'=2,'x'=4] {'yl','x'}, dimensions={0} | all-to-all | bytes 1245184 | tf_op jit(solution)/shard_map/all_to_all | solution.py:451
  113.8 0.2 shard_map.133
  114.0 13.4 %all_to_all.32.received = bf16[16,32,128]{2,1,0:T(8,128)(2,1)S(1)} all-to-all(bf16[16,32,128]{2,1,0:T(8,128)(2,1)S(1)} %shard_map.133), channel_id=1, replica_groups=mesh['grp'=16,'yh'=4,'yl'=2,'x'=4] {'grp'}, dimensions={0} | all-to-all | bytes 262144 | tf_op jit(solution)/shard_map/all_to_all | solution.py:460
  127.4 0.9 shard_map.134
  (29 shorter events, 0.1 us)
Async XLA Ops:
  0.0 9.3 %copy-start.3 = (bf16[4,128,512]{2,1,0:T(8,128)(2,1)S(1)}, bf16[4,128,512]{2,1,0:T(8,128)(2,1)}, u32[]{:S(2)}) copy-start(bf16[4,128,512]{2,1,0:T(8,128)(2,1)} %param.20) | copy-start | bytes 1572868
  1.6 17.9 %all-to-all-start = ((bf16[8,160,128]{2,1,0:T(8,128)(2,1)}), bf16[8,160,128]{2,1,0:T(8,128)(2,1)}, u32[]{:S(2)}, u32[]{:S(2)}) async-start(bf16[8,160,128]{2,1,0:T(8,128)(2,1)} %broadcast_in_dim.2), calls=%async_computation | async-start | bytes 655360 | tf_op jit(solution)/shard_map/all_to_all | solution.py:359
  9.3 1.0 copy-start.4
  10.3 0.8 copy-start.8
  12.3 22.6 %copy-start.15 = (f32[5120]{0:T(1024)S(1)}, f32[5120]{0:T(1024)}, u32[]{:S(2)}) copy-start(f32[5120]{0:T(1024)} %param.14) | copy-start | bytes 61444
  12.3 22.7 %copy-start.11 = (s32[16,128]{1,0:T(8,128)S(1)}, s32[16,128]{1,0:T(8,128)}, u32[]{:S(2)}) copy-start(s32[16,128]{1,0:T(8,128)} %page_slots.1) | copy-start | bytes 24580
  12.3 22.8 %copy-start.12 = (s32[128]{0:T(128)S(1)}, s32[128]{0:T(128)}, u32[]{:S(2)}) copy-start(s32[128]{0:T(128)} %param.23) | copy-start | bytes 1540
  12.3 22.8 %copy-start.13 = (s32[128,1]{0,1:T(1,128)S(1)}, s32[128,1]{0,1:T(1,128)}, u32[]{:S(2)}) copy-start(s32[128,1]{0,1:T(1,128)} %param.24) | copy-start | bytes 1540
  19.5 32.4 %all-to-all-start.1 = ((bf16[4,1152,128]{2,1,0:T(8,128)(2,1)}), bf16[4,1152,128]{2,1,0:T(8,128)(2,1)S(1)}, u32[]{:S(2)}, u32[]{:S(2)}) async-start(bf16[4,1152,128]{2,1,0:T(8,128)(2,1)} %shard_map.127), calls=%async_computation.1 | async-start | bytes 2359296 | tf_op jit(solution)/shard_map/all_to_all | solution.py:371
  23.1 28.9 %copy-start.7 = (bf16[16,16,128]{2,1,0:T(8,128)(2,1)S(1)}, bf16[16,16,128]{2,1,0:T(8,128)(2,1)}, u32[]{:S(2)}) copy-start(bf16[16,16,128]{2,1,0:T(8,128)(2,1)} %param.18) | copy-start | bytes 196612
  23.1 16.6 %collective-permute-start = (bf16[8,160,128]{2,1,0:T(8,128)(2,1)}, bf16[8,160,128]{2,1,0:T(8,128)(2,1)}, u32[]{:S(2)}, u32[]{:S(2)}) collective-permute-start(bf16[8,160,128]{2,1,0:T(8,128)(2,1)} %all-to-all-done.features_0), channel_id=1, source_target_pairs={{0,3},{1,0},{2,1},{3,2},{4,7},{5,4},{6,5},{7,6},{8,11},{9,8},{10,9... | collective-permute-start | bytes 983048 | tf_op jit(solution)/shard_map/ppermute | solution.py:373
  29.4 11.1 %collective-permute-start.1 = (bf16[8,160,128]{2,1,0:T(8,128)(2,1)}, bf16[8,160,128]{2,1,0:T(8,128)(2,1)}, u32[]{:S(2)}, u32[]{:S(2)}) collective-permute-start(bf16[8,160,128]{2,1,0:T(8,128)(2,1)} %all-to-all-done.features_0), channel_id=1, source_target_pairs={{0,1},{1,2},{2,3},{3,0},{4,5},{5,6},{6,7},{7,4},{8,9},{9,10},{10,1... | collective-permute-start | bytes 983048 | tf_op jit(solution)/shard_map/ppermute | solution.py:373
  31.3 14.2 %collective-permute-start.2 = (bf16[8,160,128]{2,1,0:T(8,128)(2,1)}, bf16[8,160,128]{2,1,0:T(8,128)(2,1)}, u32[]{:S(2)}, u32[]{:S(2)}) collective-permute-start(bf16[8,160,128]{2,1,0:T(8,128)(2,1)} %all-to-all-done.features_0), channel_id=1, source_target_pairs={{0,2},{1,3},{2,0},{3,1},{4,6},{5,7},{6,4},{7,5},{8,10},{9,11},{10,... | collective-permute-start | bytes 983048 | tf_op jit(solution)/shard_map/ppermute | solution.py:373
  35.1 1.3 %copy-start.2 = (bf16[5120,128]{1,0:T(8,128)(2,1)S(1)}, bf16[5120,128]{1,0:T(8,128)(2,1)}, u32[]{:S(2)}) copy-start(bf16[5120,128]{1,0:T(8,128)(2,1)} %query_weight.1) | copy-start | bytes 3932164
  36.4 1.0 copy-start.5
  37.5 1.0 copy-start.6
  51.9 1.0 copy-start
  56.2 22.9 %copy-start.9 = (bf16[128,128]{1,0:T(8,128)(2,1)}, bf16[128,128]{1,0:T(8,128)(2,1)S(1)}, u32[]{:S(2)}) copy-start(bf16[128,128]{1,0:T(8,128)(2,1)S(1)} %get-tuple-element.24.queries_t) | copy-start | bytes 98308
  56.2 22.9 %copy-start.14 = (bf16[32,128]{1,0:T(8,128)(2,1)}, bf16[32,128]{1,0:T(8,128)(2,1)S(1)}, u32[]{:S(2)}) copy-start(bf16[32,128]{1,0:T(8,128)(2,1)S(1)} %get-tuple-element.23) | copy-start | bytes 24580
  79.1 13.8 %all-to-all-start.3 = ((bf16[8,288,128]{2,1,0:T(8,128)(2,1)}), bf16[8,288,128]{2,1,0:T(8,128)(2,1)}, u32[]{:S(2)}, u32[]{:S(2)}) async-start(bf16[8,288,128]{2,1,0:T(8,128)(2,1)} %get-tuple-element.21), calls=%async_computation.3 | async-start | bytes 1179648 | tf_op jit(solution)/shard_map/all_to_all | solution.py:429
  83.3 9.6 %copy-start.1 = (bf16[16,16,1024]{2,1,0:T(8,128)(2,1)S(1)}, bf16[16,16,1024]{2,1,0:T(8,128)(2,1)}, u32[]{:S(2)}) copy-start(bf16[16,16,1024]{2,1,0:T(8,128)(2,1)} %param.19) | copy-start | bytes 1572868
  83.3 1.9 %collective-permute-start.3 = (bf16[32,128]{1,0:T(8,128)(2,1)}, bf16[32,128]{1,0:T(8,128)(2,1)S(1)}, u32[]{:S(2)}, u32[]{:S(2)}) collective-permute-start(bf16[32,128]{1,0:T(8,128)(2,1)} %copy-done.14), channel_id=1, source_target_pairs={{0,0},{4,8},{8,16},{12,24},{16,4},{20,12},{24,20},{28,28},{1,1},{5... | collective-permute-start | bytes 24584 | tf_op jit(solution)/shard_map/ppermute | solution.py:415
  99.6 27.9 %copy-start.10 = (bf16[128,128]{1,0:T(8,128)(2,1)S(1)}, bf16[128,128]{1,0:T(8,128)(2,1)}, u32[]{:S(2)}) copy-start(bf16[128,128]{1,0:T(8,128)(2,1)} %copy-done.9) | copy-start | bytes 98308

commit v6 on v5

--- a/solution.py
+++ b/solution.py
@@ -22,6 +22,7 @@
 FRESH_ROWS = 32
 DEPTH = 2 * HEAD_SIZE
 VALUE_ROWS = QUERY_ROWS + 16
+OWN_UP, KEY_UP, VALUE_UP, QUERY_UP, PLACING = range(5)
 PIECE_TOKENS = 512
 PIECE_ROWS = 2 * PIECE_TOKENS + 2 * RANK * PIECE_TOKENS // LANES
 SHIFTS = (0, 1, 3, 2)
@@ -39,7 +40,7 @@
     )
 
 
-def call(kernel, out_shape, in_specs, scratch=(), flops=0, moved=0, limit=32, out_specs=None):
+def call(kernel, out_shape, in_specs, scratch=(), flops=0, moved=0, limit=16, out_specs=None):
     return pl.pallas_call(
         kernel,
         out_shape=out_shape,
@@ -77,21 +78,26 @@
 
 def plan_kernel(
     groups,
+    place,
     page_slots,
     query_weight,
     key_value_weight,
     down,
-    adapters,
+    query_up,
+    key_value_up,
     documents,
     weights,
-    placing,
-    slot_adapters,
+    smalls,
 ):
     for start in range(0, weights.shape[1], LANES):
         block = query_weight[start : start + LANES, :].astype(F32).T
         weights[0:HEAD_SIZE, start : start + LANES] = block.astype(BF16)
     weights[HEAD_SIZE : HEAD_SIZE + FRESH_ROWS, :] = key_value_weight[...]
     weights[HEAD_SIZE + FRESH_ROWS :, :] = down[...]
+    for index, head in enumerate((place[0] // X, place[1], place[1] + Y_HIGH)):
+        columns = pl.ds(pl.multiple_of(head * HEAD_SIZE, HEAD_SIZE), HEAD_SIZE)
+        smalls[index] = key_value_up[:, columns]
+    smalls[QUERY_UP] = query_up[...]
 
     document = documents[...]
     rows = document.shape[1]
@@ -109,9 +115,7 @@
     position = jnp.sum(earlier * match, axis=0, keepdims=True).astype(jnp.int32)
     slot = target * capacity + position
     placed = (lax.broadcasted_iota(jnp.int32, (SLOTS, rows), 0) == slot).astype(F32)
-    placing[...] = placed.astype(BF16)
-    adapter = jnp.sum(placed * adapters[...].astype(F32), axis=1, keepdims=True)
-    slot_adapters[...] = jnp.broadcast_to(adapter, (SLOTS, LANES)).astype(BF16)
+    smalls[PLACING] = placed.astype(BF16)
 
 
 def project_kernel(
@@ -123,12 +127,8 @@
     features_3,
     weights,
     gain,
-    query_up,
-    key_value_up,
+    smalls,
     adapters,
-    placing,
-    slot_adapters,
-    held,
     message,
     fresh,
     queries_t,
@@ -157,43 +157,45 @@
 
     adapter = adapters[...]
     low = total[HEAD_SIZE + FRESH_ROWS :].astype(BF16)
-    query_update = dot(query_up[...], of_adapter(low[0:RANK], adapter), 0, 0)
+    query_update = dot(smalls[QUERY_UP], of_adapter(low[0:RANK], adapter), 0, 0)
     queries = (total[0:HEAD_SIZE] + query_update).astype(BF16)
     queries_t[...] = queries
 
     is_key = device < Y * X // 2
     low_kv = jnp.where(is_key, low[RANK : 2 * RANK], low[2 * RANK :])
-    columns = pl.ds(pl.multiple_of(device // X * HEAD_SIZE, HEAD_SIZE), HEAD_SIZE)
-    update[...] = dot(key_value_up[:, columns], of_adapter(low_kv, adapter), 0, 0)
+    update[...] = dot(smalls[OWN_UP], of_adapter(low_kv, adapter), 0, 0)
     mine = pl.ds(pl.multiple_of(lax.rem(device, X) * FRESH_ROWS, FRESH_ROWS), FRESH_ROWS)
     new = total[HEAD_SIZE : HEAD_SIZE + FRESH_ROWS] + update[mine, :]
     fresh[...] = new.astype(BF16)
 
-    capacity = SLOTS // groups
-    placed = dot(placing[...], queries, 1, 1).astype(BF16)
-    message[:, 0:capacity, :] = placed.reshape(groups, capacity, HEAD_SIZE)
-    message[:, capacity:, :] = slot_adapters[...].reshape(groups, capacity, LANES)
-
-
-def factor_kernel(groups, place, received, key_value_up, message, slot_adapters):
-    capacity = SLOTS // groups
-    queries = received[:, 0:capacity, :].reshape(SLOTS, HEAD_SIZE)
-    queries_t = queries.astype(F32).T.astype(BF16)
-    adapters = received[:, capacity:, :].reshape(SLOTS, LANES).astype(F32).T[0:1]
-    slot_adapters[...] = jnp.broadcast_to(adapters, slot_adapters.shape)
-    columns = pl.ds(pl.multiple_of(place[1] * HEAD_SIZE, HEAD_SIZE), HEAD_SIZE)
-    every = dot(key_value_up[:, columns], queries, 1, 1)
-    adapter = (lax.broadcasted_iota(jnp.int32, every.shape, 0) // RANK).astype(F32)
-    kept = jnp.where(adapter == adapters, every, 0.0)
+    every = dot(smalls[KEY_UP], queries, 1, 0)
+    of_row = lax.broadcasted_iota(jnp.int32, every.shape, 0) // RANK == adapter
+    kept = jnp.where(of_row, every, 0.0)
     factors = kept[0:RANK]
     for a in range(1, 16):
         factors = factors + kept[a * RANK : (a + 1) * RANK]
-    factors = factors.astype(BF16)
+    rest = jnp.zeros((HEAD_SIZE - RANK - 1, factors.shape[1]), F32)
+    beside = jnp.concatenate([factors, adapter.astype(F32), rest], axis=0).astype(BF16)
+
+    capacity = SLOTS // groups
+    place_rows = smalls[PLACING]
+    placed = dot(place_rows, queries, 1, 1).astype(BF16)
+    message[:, 0:capacity, :] = placed.reshape(groups, capacity, HEAD_SIZE)
+    placed = dot(place_rows, beside, 1, 1).astype(BF16)
+    message[:, capacity:, :] = placed.reshape(groups, capacity, LANES)
+
+
+def turn_kernel(groups, received, message, slot_adapters):
+    capacity = SLOTS // groups
+    queries = received[:, 0:capacity, :].reshape(SLOTS, HEAD_SIZE).astype(F32).T.astype(BF16)
+    beside = received[:, capacity:, :].reshape(SLOTS, LANES).astype(F32).T
+    slot_adapters[...] = jnp.broadcast_to(beside[RANK : RANK + 1], slot_adapters.shape)
+    factors = beside[0:RANK].astype(BF16)
     for member in range(BLOCK):
         for tile in range(TILES):
             lanes = slice(tile * LANES, (tile + 1) * LANES)
             start = tile * QUERY_ROWS
-            message[member, start : start + HEAD_SIZE, :] = queries_t[:, lanes]
+            message[member, start : start + HEAD_SIZE, :] = queries[:, lanes]
             message[member, start + HEAD_SIZE : start + QUERY_ROWS, :] = factors[:, lanes]
 
 
@@ -222,7 +224,7 @@
 
 
 def attend_kernel(
-    place, queries, slot_adapters, key_value_up, prepared, fresh, message, query, scores, totals, peaks
+    queries, slot_adapters, smalls, prepared, fresh, message, query, scores, totals, peaks
 ):
     tokens = PIECE_TOKENS * Y_HIGH
     chunk = 1024
@@ -270,8 +272,7 @@
         highest = score(0, start, highest)
     lax.fori_loop(0, BLOCK // 2, two_heads, jnp.max(highest, axis=0, keepdims=True))
 
-    columns = pl.ds(pl.multiple_of((place[1] + Y_HIGH) * HEAD_SIZE, HEAD_SIZE), HEAD_SIZE)
-    value_up = key_value_up[:, columns]
+    value_up = smalls[VALUE_UP]
     adapters = slot_adapters[0:1, :].astype(jnp.int32)
     for head in range(BLOCK):
         total, peak = totals[head], peaks[head, 0:1]
@@ -313,9 +314,9 @@
     message[:, capacity:, :] = jnp.concatenate(masses, axis=0).reshape(groups, capacity, LANES)
 
 
-def finish_kernel(groups, received, placing, queries_t, partials, out):
-    capacity = SLOTS // groups
-    place = placing[...]
+def finish_kernel(groups, received, smalls, queries_t, partials, out):
+    capacity = SLOTS // groups
+    place = smalls[PLACING]
     shared = dot(received[:, 0:capacity, :].reshape(SLOTS, HEAD_SIZE), place, 0, 0)
     stats = dot(received[:, capacity:, :].reshape(SLOTS, LANES), place, 0, 0)
     log_mass = stats[0:1] + stats[1:2] + stats[2:3]
@@ -375,18 +376,19 @@
     ]
 
     columns = HEAD_SIZE + FRESH_ROWS + 3 * RANK
-    adapters = adapter_of_row.reshape(1, rows)
-    weights, placing, row_adapters = call(
+    weights, smalls = call(
         functools.partial(plan_kernel, groups),
-        [shape(columns, width), shape(SLOTS, rows), shape(SLOTS, LANES)],
-        [SMEM] + [VMEM] * 5,
+        [shape(columns, width), shape(5, SLOTS, LANES)],
+        [SMEM, SMEM] + [VMEM] * 6,
         moved=5 * 1024 * 1024,
     )(
+        place,
         document_page_slots,
         query_weight,
         key_value_weight.T,
         shared_down_factors.T,
-        adapters,
+        query_up,
+        key_value_up,
         document_of_row.reshape(1, rows),
     )
     message, fresh, queries_t = call(
@@ -396,7 +398,7 @@
             shape(FRESH_ROWS, rows),
             shape(HEAD_SIZE, rows),
         ],
-        [SMEM] + [VMEM] * (X + 7) + [ANY],
+        [SMEM] + [VMEM] * (X + 4),
         [pltpu.VMEM((width, rows), BF16), pltpu.VMEM((HEAD_SIZE, rows), F32)],
         flops=2 * width * rows * 256,
         moved=4 * 1024 * 1024,
@@ -405,27 +407,23 @@
         *sources,
         weights,
         input_norm_gain.reshape(Y, X, part).transpose(1, 0, 2),
-        query_up,
-        key_value_up,
-        adapters,
-        placing,
-        row_adapters,
-        pieces,
+        smalls,
+        adapter_of_row.reshape(1, rows),
     )
     fresh = lax.ppermute(
         fresh,
         ("yh", "yl"),
         [(y, 2 * y if y < Y_HIGH else 2 * (y - Y_HIGH) + 1) for y in range(Y)],
     )
+    message, pieces = lax.optimization_barrier((message, pieces))
     received = lax.all_to_all(message, "grp", 0, 0, tiled=True)
 
     message, slot_adapters = call(
-        functools.partial(factor_kernel, groups),
+        functools.partial(turn_kernel, groups),
         [shape(BLOCK, MESSAGE_ROWS, LANES), shape(8, SLOTS, dtype=F32)],
-        [SMEM] + [VMEM] * 2,
-        flops=2 * 256 * 256 * 128,
+        [VMEM],
         moved=1024 * 1024,
-    )(place, received, key_value_up)
+    )(received)
     gathered = lax.all_to_all(message, ("yl", "x"), 0, 0, tiled=True)
 
     tokens = PIECE_TOKENS * Y_HIGH
@@ -438,7 +436,7 @@
     message = call(
         attend_kernel,
         shape(BLOCK, RETURN_ROWS + FRESH_ROWS, LANES),
-        [SMEM] + [VMEM] * 5,
+        [VMEM] * 5,
         [
             pltpu.VMEM((2, DEPTH, SLOTS), BF16),
             pltpu.VMEM((2, tokens, SLOTS), F32),
@@ -447,7 +445,8 @@
         ],
         flops=4 * SLOTS * BLOCK * tokens * 256,
         moved=3 * 1024 * 1024,
-    )(place, gathered, slot_adapters, key_value_up, prepared, fresh)
+        limit=24,
+    )(gathered, slot_adapters, smalls, prepared, fresh)
     partials = lax.all_to_all(message, ("yl", "x"), 0, 0, tiled=True)
 
     message = call(
@@ -465,7 +464,7 @@
         [VMEM] * 4,
         flops=2 * SLOTS * rows * 256,
         moved=1024 * 1024,
-    )(received, placing, queries_t, partials)
+    )(received, smalls, queries_t, partials)
 
 
 def solution(mesh):

time: 129 us -> 124 us (0.961)
  waiting for transfers between devices: 27.1 us -> 23.3 us
  local copies, waits for them, and re-layouts: 7.92 us -> 6.42 us
    ppermute x3, waiting for transfers between devices: 5.79 us -> 3.25 us  [per_device(): lax.ppermute(features, 'x', [(i, (i - shift) % X) for i in range(X)])]
    all_to_all x1, waiting for transfers between devices: 6.45 us -> 4.5 us  [per_device(): pieces = lax.all_to_all(pieces, 'yh', 0, 0, tiled=True)]
    unnamed x32 -> x24, local copies, waits for them, and re-layouts: 6.2 us -> 4.73 us
  transfers between devices with their start and end apart: 7 -> 7, of which waited for: 5 -> 4; matrix products, arithmetic and copies ran while one was open for 0% -> 0% of each run, Pallas kernels for 2% -> 5%
where the time goes in v6:
time: 124 us; the launch traced here: 123 us
  blocking collectives  49.5 us (40%)
  starting transfers between devices  29 us (23%)
  waiting for transfers between devices  23.3 us (19%)
  Pallas kernels  14.8 us (12%)
  local copies, waits for them, and re-layouts  6.42 us (5%)
    all_to_all x2, blocking collectives, per_device(): received = lax.all_to_all(message, 'grp', 0, 0, tiled=True)  35.3 us
    all_to_all x1, blocking collectives, per_device(): partials = lax.all_to_all(message, ('yl', 'x'), 0, 0, tiled=True)  14.2 us
    ppermute x3, starting transfers between devices, per_device(): lax.ppermute(features, 'x', [(i, (i - shift) % X) for i in range(X)])  13 us
    all_to_all x1, waiting for transfers between devices, per_device(): gathered = lax.all_to_all(message, ('yl', 'x'), 0, 0, tiled=True)  8.56 us
    all_to_all x1, starting transfers between devices, per_device(): features = lax.all_to_all(features, ('yh', 'yl'), 0, 0, tiled=True)  7.65 us
    all_to_all x1, waiting for transfers between devices, per_device(): features = lax.all_to_all(features, ('yh', 'yl'), 0, 0, tiled=True)  7.01 us
    pallas_call x1, Pallas kernels, per_device(): call(attend_kernel, shape(BLOCK, RETURN_ROWS + FRESH_ROWS, LANES), [VMEM]...  6.59 us
    unnamed x24, local copies, waits for them, and re-layouts  4.73 us
  transfers between devices with their start and end apart: 7, of which 4 were waited for; matrix products, arithmetic and copies ran while one was open for 0% of the time, Pallas kernels for 5%

profile of v6, /device:TPU:1, one launch (start us, length us, event | category | flops | bytes accessed | tf_op | source)
XLA Modules:
  0.0 123.3 jit_solution(17044430837499085235)
XLA Ops:
  0.0 1.6 %broadcast_in_dim.2 = bf16[8,160,128]{2,1,0:T(8,128)(2,1)} broadcast(bf16[160,128]{1,0:T(8,128)(2,1)} %bitcast.27), dimensions={1,2} | broadcast | bytes 368640 | tf_op jit(solution)/shard_map/broadcast_in_dim | solution.py:359
  1.6 7.7 %all-to-all-start = ((bf16[8,160,128]{2,1,0:T(8,128)(2,1)}), bf16[8,160,128]{2,1,0:T(8,128)(2,1)S(1)}, u32[]{:S(2)}, u32[]{:S(2)}) async-start(bf16[8,160,128]{2,1,0:T(8,128)(2,1)} %broadcast_in_dim.2), calls=%async_computation | async-start | bytes 655360 | tf_op jit(solution)/shard_map/all_to_all | solution.py:360
  9.3 0.0 copy-start.2
  9.3 1.0 copy-done.2
  10.3 0.8 copy-done.7
  11.1 1.2 shard_map.127
  12.3 7.0 %all-to-all-done.features_0 = bf16[8,160,128]{2,1,0:T(8,128)(2,1)S(1)} async-done(((bf16[8,160,128]{2,1,0:T(8,128)(2,1)}), bf16[8,160,128]{2,1,0:T(8,128)(2,1)S(1)}, u32[]{:S(2)}, u32[]{:S(2)}) %all-to-all-start) | async-done | bytes 327712 | tf_op jit(solution)/shard_map/all_to_all | solution.py:360
  19.3 3.5 %all-to-all-start.1 = ((bf16[4,1152,128]{2,1,0:T(8,128)(2,1)}), bf16[4,1152,128]{2,1,0:T(8,128)(2,1)S(1)}, u32[]{:S(2)}, u32[]{:S(2)}) async-start(bf16[4,1152,128]{2,1,0:T(8,128)(2,1)} %shard_map.127), calls=%async_computation.1 | async-start | bytes 2359296 | tf_op jit(solution)/shard_map/all_to_all | solution.py:372
  22.9 6.5 %collective-permute-start.2 = (bf16[8,160,128]{2,1,0:T(8,128)(2,1)S(1)}, bf16[8,160,128]{2,1,0:T(8,128)(2,1)}, u32[]{:S(2)}, u32[]{:S(2)}) collective-permute-start(bf16[8,160,128]{2,1,0:T(8,128)(2,1)S(1)} %all-to-all-done.features_0), channel_id=1, source_target_pairs={{0,2},{1,3},{2,0},{3,1},{4,6},{5,7},{6,4},{7,5},{8,10},{9,11},{10,... | collective-permute-start | bytes 983048 | tf_op jit(solution)/shard_map/ppermute | solution.py:374
  29.4 2.2 %collective-permute-start.1 = (bf16[8,160,128]{2,1,0:T(8,128)(2,1)S(1)}, bf16[8,160,128]{2,1,0:T(8,128)(2,1)}, u32[]{:S(2)}, u32[]{:S(2)}) collective-permute-start(bf16[8,160,128]{2,1,0:T(8,128)(2,1)S(1)} %all-to-all-done.features_0), channel_id=1, source_target_pairs={{0,1},{1,2},{2,3},{3,0},{4,5},{5,6},{6,7},{7,4},{8,9},{9,10},{10,1... | collective-permute-start | bytes 983048 | tf_op jit(solution)/shard_map/ppermute | solution.py:374
  31.6 4.3 %collective-permute-start = (bf16[8,160,128]{2,1,0:T(8,128)(2,1)S(1)}, bf16[8,160,128]{2,1,0:T(8,128)(2,1)}, u32[]{:S(2)}, u32[]{:S(2)}) collective-permute-start(bf16[8,160,128]{2,1,0:T(8,128)(2,1)S(1)} %all-to-all-done.features_0), channel_id=1, source_target_pairs={{0,3},{1,0},{2,1},{3,2},{4,7},{5,4},{6,5},{7,6},{8,11},{9,8},{10,9... | collective-permute-start | bytes 983048 | tf_op jit(solution)/shard_map/ppermute | solution.py:374
  35.9 0.1 reshape.31
  36.0 0.1 pad_add_fusion.place
  36.1 0.0 copy-start.3
  36.1 1.0 copy-done.3
  37.2 1.0 copy-done.4
  38.2 0.8 copy-done.6
  39.0 1.2 shard_map.128
  40.2 3.2 %collective-permute-done.1.features_2 = bf16[8,160,128]{2,1,0:T(8,128)(2,1)} collective-permute-done((bf16[8,160,128]{2,1,0:T(8,128)(2,1)S(1)}, bf16[8,160,128]{2,1,0:T(8,128)(2,1)}, u32[]{:S(2)}, u32[]{:S(2)}) %collective-permute-start.1) | collective-permute-done | bytes 327712 | tf_op jit(solution)/shard_map/ppermute | solution.py:374
  43.5 3.3 %shard_map.129 = (bf16[16,32,128]{2,1,0:T(8,128)(2,1)S(1)}, bf16[32,128]{1,0:T(8,128)(2,1)S(1)}, bf16[128,128]{1,0:T(8,128)(2,1)S(1)}) custom-call(s32[2]{0:T(128)S(1)} %pad_add_fusion.place, bf16[8,160,128]{2,1,0:T(8,128)(2,1)S(1)} %all-to-all-done.features_0, bf16[8,160,128]{2,1,0:T(8,128)(2,1)} %collective-permute-done.features_1, ...), custom_call_target="tpu_custom_call" | custom-call | flops 335544320 | bytes 4194304 | tf_op jit(solution)/shard_map/pallas_call | solution.py:394
  46.8 4.5 %all-to-all-done.1.pieces = bf16[4,1152,128]{2,1,0:T(8,128)(2,1)S(1)} async-done(((bf16[4,1152,128]{2,1,0:T(8,128)(2,1)}), bf16[4,1152,128]{2,1,0:T(8,128)(2,1)S(1)}, u32[]{:S(2)}, u32[]{:S(2)}) %all-to-all-start.1) | async-done | bytes 1179680 | tf_op jit(solution)/shard_map/all_to_all | solution.py:372
  51.3 21.8 %all_to_all.30.received = bf16[16,32,128]{2,1,0:T(8,128)(2,1)S(1)} all-to-all(bf16[16,32,128]{2,1,0:T(8,128)(2,1)S(1)} %get-tuple-element.21), channel_id=1, replica_groups=mesh['grp'=16,'yh'=4,'yl'=2,'x'=4] {'grp'}, dimensions={0} | all-to-all | bytes 262144 | tf_op jit(solution)/shard_map/all_to_all | solution.py:419
  73.1 0.9 shard_map.130
  74.0 4.2 %all-to-all-start.3 = ((bf16[8,288,128]{2,1,0:T(8,128)(2,1)}), bf16[8,288,128]{2,1,0:T(8,128)(2,1)}, u32[]{:S(2)}, u32[]{:S(2)}) async-start(bf16[8,288,128]{2,1,0:T(8,128)(2,1)} %get-tuple-element.22), calls=%async_computation.3 | async-start | bytes 1179648 | tf_op jit(solution)/shard_map/all_to_all | solution.py:427
  78.2 0.7 collective-permute-start.3
  78.9 0.4 shard_map.131.prepared
  79.3 8.6 %all-to-all-done.3.queries = bf16[8,288,128]{2,1,0:T(8,128)(2,1)} async-done(((bf16[8,288,128]{2,1,0:T(8,128)(2,1)}), bf16[8,288,128]{2,1,0:T(8,128)(2,1)}, u32[]{:S(2)}, u32[]{:S(2)}) %all-to-all-start.3) | async-done | bytes 589856 | tf_op jit(solution)/shard_map/all_to_all | solution.py:427
  87.9 6.6 %shard_map.132 = bf16[8,304,128]{2,1,0:T(8,128)(2,1)S(1)} custom-call(bf16[8,288,128]{2,1,0:T(8,128)(2,1)} %all-to-all-done.3.queries, f32[8,256]{1,0:T(8,128)S(1)} %get-tuple-element.23.slot_adapters, bf16[5,256,128]{2,1,0:T(8,128)(2,1)S(1)} %get-tuple-element.18.smalls, bf16[3328,256]{1,0:T(8,128)(2,1)S(1)} %shard_map.131.prepared, ...), custom_call_target="tpu_custom_call" | custom-call | flops 4294967296 | bytes 3145728 | tf_op jit(solution)/shard_map/pallas_call | solution.py:436
  94.5 14.2 %all_to_all.31.partials = bf16[8,304,128]{2,1,0:T(8,128)(2,1)S(1)} all-to-all(bf16[8,304,128]{2,1,0:T(8,128)(2,1)S(1)} %shard_map.132), channel_id=1, replica_groups=mesh['grp'=16,'yh'=4,'yl'=2,'x'=4] {'yl','x'}, dimensions={0} | all-to-all | bytes 1245184 | tf_op jit(solution)/shard_map/all_to_all | solution.py:450
  108.7 0.2 shard_map.133
  108.9 13.5 %all_to_all.32.received = bf16[16,32,128]{2,1,0:T(8,128)(2,1)S(1)} all-to-all(bf16[16,32,128]{2,1,0:T(8,128)(2,1)S(1)} %shard_map.133), channel_id=1, replica_groups=mesh['grp'=16,'yh'=4,'yl'=2,'x'=4] {'grp'}, dimensions={0} | all-to-all | bytes 262144 | tf_op jit(solution)/shard_map/all_to_all | solution.py:459
  122.4 0.9 shard_map.134
  (21 shorter events, 0.0 us)
Async XLA Ops:
  0.0 9.3 %copy-start.1 = (bf16[4,128,512]{2,1,0:T(8,128)(2,1)S(1)}, bf16[4,128,512]{2,1,0:T(8,128)(2,1)}, u32[]{:S(2)}) copy-start(bf16[4,128,512]{2,1,0:T(8,128)(2,1)} %param.20) | copy-start | bytes 1572868
  1.6 17.7 %all-to-all-start = ((bf16[8,160,128]{2,1,0:T(8,128)(2,1)}), bf16[8,160,128]{2,1,0:T(8,128)(2,1)S(1)}, u32[]{:S(2)}, u32[]{:S(2)}) async-start(bf16[8,160,128]{2,1,0:T(8,128)(2,1)} %broadcast_in_dim.2), calls=%async_computation | async-start | bytes 655360 | tf_op jit(solution)/shard_map/all_to_all | solution.py:360
  9.3 1.0 copy-start.2
  10.3 0.8 copy-start.7
  12.3 23.6 %copy-start.11 = (f32[5120]{0:T(1024)S(1)}, f32[5120]{0:T(1024)}, u32[]{:S(2)}) copy-start(f32[5120]{0:T(1024)} %param.14) | copy-start | bytes 61444
  12.3 23.8 %copy-start = (bf16[5120,128]{1,0:T(8,128)(2,1)S(1)}, bf16[5120,128]{1,0:T(8,128)(2,1)}, u32[]{:S(2)}) copy-start(bf16[5120,128]{1,0:T(8,128)(2,1)} %query_weight.1) | copy-start | bytes 3932164
  12.3 23.8 %copy-start.5 = (bf16[5120,32]{0,1:T(8,128)(2,1)S(1)}, bf16[5120,32]{0,1:T(8,128)(2,1)}, u32[]{:S(2)}) copy-start(bf16[5120,32]{0,1:T(8,128)(2,1)} %param.16) | copy-start | bytes 983044
  12.3 23.8 %copy-start.8 = (s32[16,128]{1,0:T(8,128)S(1)}, s32[16,128]{1,0:T(8,128)}, u32[]{:S(2)}) copy-start(s32[16,128]{1,0:T(8,128)} %page_slots.1) | copy-start | bytes 24580
  12.3 23.8 %copy-start.9 = (s32[128,1]{0,1:T(1,128)S(1)}, s32[128,1]{0,1:T(1,128)}, u32[]{:S(2)}) copy-start(s32[128,1]{0,1:T(1,128)} %param.24) | copy-start | bytes 1540
  19.3 31.9 %all-to-all-start.1 = ((bf16[4,1152,128]{2,1,0:T(8,128)(2,1)}), bf16[4,1152,128]{2,1,0:T(8,128)(2,1)S(1)}, u32[]{:S(2)}, u32[]{:S(2)}) async-start(bf16[4,1152,128]{2,1,0:T(8,128)(2,1)} %shard_map.127), calls=%async_computation.1 | async-start | bytes 2359296 | tf_op jit(solution)/shard_map/all_to_all | solution.py:372
  22.9 17.3 %collective-permute-start.2 = (bf16[8,160,128]{2,1,0:T(8,128)(2,1)S(1)}, bf16[8,160,128]{2,1,0:T(8,128)(2,1)}, u32[]{:S(2)}, u32[]{:S(2)}) collective-permute-start(bf16[8,160,128]{2,1,0:T(8,128)(2,1)S(1)} %all-to-all-done.features_0), channel_id=1, source_target_pairs={{0,2},{1,3},{2,0},{3,1},{4,6},{5,7},{6,4},{7,5},{8,10},{9,11},{10,... | collective-permute-start | bytes 983048 | tf_op jit(solution)/shard_map/ppermute | solution.py:374
  29.4 14.1 %collective-permute-start.1 = (bf16[8,160,128]{2,1,0:T(8,128)(2,1)S(1)}, bf16[8,160,128]{2,1,0:T(8,128)(2,1)}, u32[]{:S(2)}, u32[]{:S(2)}) collective-permute-start(bf16[8,160,128]{2,1,0:T(8,128)(2,1)S(1)} %all-to-all-done.features_0), channel_id=1, source_target_pairs={{0,1},{1,2},{2,3},{3,0},{4,5},{5,6},{6,7},{7,4},{8,9},{9,10},{10,1... | collective-permute-start | bytes 983048 | tf_op jit(solution)/shard_map/ppermute | solution.py:374
  31.6 11.9 %collective-permute-start = (bf16[8,160,128]{2,1,0:T(8,128)(2,1)S(1)}, bf16[8,160,128]{2,1,0:T(8,128)(2,1)}, u32[]{:S(2)}, u32[]{:S(2)}) collective-permute-start(bf16[8,160,128]{2,1,0:T(8,128)(2,1)S(1)} %all-to-all-done.features_0), channel_id=1, source_target_pairs={{0,3},{1,0},{2,1},{3,2},{4,7},{5,4},{6,5},{7,6},{8,11},{9,8},{10,9... | collective-permute-start | bytes 983048 | tf_op jit(solution)/shard_map/ppermute | solution.py:374
  36.1 1.0 copy-start.3
  37.1 1.0 copy-start.4
  38.2 0.8 copy-start.6
  39.0 4.4 %copy-start.10 = (s32[128]{0:T(128)S(1)}, s32[128]{0:T(128)}, u32[]{:S(2)}) copy-start(s32[128]{0:T(128)} %param.23) | copy-start | bytes 1540
  74.0 13.9 %all-to-all-start.3 = ((bf16[8,288,128]{2,1,0:T(8,128)(2,1)}), bf16[8,288,128]{2,1,0:T(8,128)(2,1)}, u32[]{:S(2)}, u32[]{:S(2)}) async-start(bf16[8,288,128]{2,1,0:T(8,128)(2,1)} %get-tuple-element.22), calls=%async_computation.3 | async-start | bytes 1179648 | tf_op jit(solution)/shard_map/all_to_all | solution.py:427
  78.2 1.1 collective-permute-start.3

commit v7 on v6

--- a/solution.py
+++ b/solution.py
@@ -68,19 +68,30 @@
     return high, middle, value - high - middle
 
 
-def pack_kernel(keys, values, factors, message):
-    for head in range(Y_HIGH):
-        columns = slice(head * HEAD_SIZE, (head + 1) * HEAD_SIZE)
-        message[head, 0:PIECE_TOKENS, :] = keys[:, columns]
-        message[head, PIECE_TOKENS : 2 * PIECE_TOKENS, :] = values[:, columns]
-        message[head, 2 * PIECE_TOKENS :, :] = factors[...]
+def fetch(pairs, sems):
+    moves = [pltpu.make_async_copy(*pair, sems.at[i]) for i, pair in enumerate(pairs)]
+    for move in moves:
+        move.start()
+    for move in moves:
+        move.wait()
+
+
+def pack_kernel(place, keys_far, values_far, factors_far, *refs):
+    pieces, (keys, values, factors, sems) = refs[:Y_HIGH], refs[Y_HIGH:]
+    fetch([(keys_far, keys), (values_far, values), (factors_far, factors)], sems)
+    for shift, piece in zip(SHIFTS, pieces):
+        head = lax.rem(place[1] + shift, Y_HIGH)
+        columns = pl.ds(pl.multiple_of(head * HEAD_SIZE, HEAD_SIZE), HEAD_SIZE)
+        piece[0:PIECE_TOKENS, :] = keys[:, columns]
+        piece[PIECE_TOKENS : 2 * PIECE_TOKENS, :] = values[:, columns]
+        piece[2 * PIECE_TOKENS :, :] = factors[...]
 
 
 def plan_kernel(
     groups,
     place,
     page_slots,
-    query_weight,
+    query_weight_far,
     key_value_weight,
     down,
     query_up,
@@ -88,16 +99,22 @@
     documents,
     weights,
     smalls,
+    query_weight,
+    sems,
 ):
+    pairs = [
+        (query_weight_far, query_weight),
+        (key_value_weight, weights.at[pl.ds(HEAD_SIZE, FRESH_ROWS), :]),
+        (down, weights.at[pl.ds(HEAD_SIZE + FRESH_ROWS, 3 * RANK), :]),
+        (query_up, smalls.at[QUERY_UP]),
+    ]
+    for index, head in enumerate((place[0] // X, place[1], place[1] + Y_HIGH)):
+        columns = pl.ds(pl.multiple_of(head * HEAD_SIZE, HEAD_SIZE), HEAD_SIZE)
+        pairs.append((key_value_up.at[:, columns], smalls.at[index]))
+    fetch(pairs, sems)
     for start in range(0, weights.shape[1], LANES):
         block = query_weight[start : start + LANES, :].astype(F32).T
         weights[0:HEAD_SIZE, start : start + LANES] = block.astype(BF16)
-    weights[HEAD_SIZE : HEAD_SIZE + FRESH_ROWS, :] = key_value_weight[...]
-    weights[HEAD_SIZE + FRESH_ROWS :, :] = down[...]
-    for index, head in enumerate((place[0] // X, place[1], place[1] + Y_HIGH)):
-        columns = pl.ds(pl.multiple_of(head * HEAD_SIZE, HEAD_SIZE), HEAD_SIZE)
-        smalls[index] = key_value_up[:, columns]
-    smalls[QUERY_UP] = query_up[...]
 
     document = documents[...]
     rows = document.shape[1]
@@ -121,10 +138,7 @@
 def project_kernel(
     groups,
     place,
-    features_0,
-    features_1,
-    features_2,
-    features_3,
+    sources,
     weights,
     gain,
     smalls,
@@ -138,20 +152,17 @@
     device = place[0]
     part = gain.shape[2]
     width = normed.shape[0]
-    sources = (features_0, features_1, features_2, features_3)
-
     squares = jnp.zeros((part, normed.shape[1]), F32)
-    for features in sources:
+    for x in range(X):
         for y in range(Y):
-            block = features[y].astype(F32)
+            block = sources[x, y].astype(F32)
             squares = squares + block * block
     scale = lax.rsqrt(jnp.sum(squares, axis=0, keepdims=True) / width + 1e-06)
-    for shift, features in zip(SHIFTS, sources):
-        x = lax.rem(device + shift, X)
+    for x in range(X):
         gain_t = gain[x].T
         for y in range(Y):
-            block = features[y].astype(F32) * scale * gain_t[:, y : y + 1]
-            start = pl.multiple_of((y * X + x) * part, 32)
+            block = sources[x, y].astype(F32) * scale * gain_t[:, y : y + 1]
+            start = (y * X + x) * part
             normed[pl.ds(start, part), :] = block.astype(BF16)
     total = dot(weights[...], normed[...], 1, 0)
 
@@ -199,22 +210,22 @@
             message[member, start + HEAD_SIZE : start + QUERY_ROWS, :] = factors[:, lanes]
 
 
-def prepare_kernel(pieces, prepared):
+def prepare_kernel(piece_0, piece_1, piece_2, piece_3, prepared):
     tokens = PIECE_TOKENS * Y_HIGH
     ones = lax.broadcasted_iota(jnp.int32, (VALUE_ROWS - QUERY_ROWS, DEPTH), 0) == 0
-    for index in range(Y_HIGH):
+    for index, piece in enumerate((piece_0, piece_1, piece_2, piece_3)):
         for page in range(PIECE_TOKENS // LANES):
             start = page * LANES
             token = index * PIECE_TOKENS + start
             here = slice(token, token + LANES)
             row = 2 * PIECE_TOKENS + page * 2 * RANK
-            factors = pieces[index, row : row + 2 * RANK, :]
+            factors = piece[row : row + 2 * RANK, :]
             key_factors = jnp.concatenate(
                 [factors[0:RANK].astype(F32), jnp.zeros((LANES - RANK, LANES), F32)], axis=0
             )
-            prepared[here, 0:HEAD_SIZE] = pieces[index, start : start + LANES, :]
+            prepared[here, 0:HEAD_SIZE] = piece[start : start + LANES, :]
             prepared[here, HEAD_SIZE:] = key_factors.T.astype(BF16)
-            value = pieces[index, PIECE_TOKENS + start : PIECE_TOKENS + start + LANES, :]
+            value = piece[PIECE_TOKENS + start : PIECE_TOKENS + start + LANES, :]
             base = tokens + token // DEPTH * VALUE_ROWS
             lanes = slice(token % DEPTH, token % DEPTH + LANES)
             prepared[base : base + HEAD_SIZE, lanes] = value.astype(F32).T.astype(BF16)
@@ -360,27 +371,30 @@
     features = lax.all_to_all(features, ("yh", "yl"), 0, 0, tiled=True)
     pieces = call(
         pack_kernel,
-        shape(Y_HIGH, PIECE_ROWS, HEAD_SIZE),
-        [VMEM] * 3,
+        [shape(PIECE_ROWS, HEAD_SIZE)] * Y_HIGH,
+        [SMEM] + [ANY] * 3,
+        [
+            pltpu.VMEM((PIECE_TOKENS, Y_HIGH * HEAD_SIZE), BF16),
+            pltpu.VMEM((PIECE_TOKENS, Y_HIGH * HEAD_SIZE), BF16),
+            pltpu.VMEM((PIECE_ROWS - 2 * PIECE_TOKENS, LANES), BF16),
+            pltpu.SemaphoreType.DMA((3,)),
+        ],
         moved=3 * 1024 * 1024,
+        limit=60,
     )(
+        place,
         paged_base_keys.reshape(PIECE_TOKENS, -1),
         paged_base_values.reshape(PIECE_TOKENS, -1),
         paged_down_factors.transpose(0, 2, 1).reshape(-1, LANES),
     )
-    features, pieces = lax.optimization_barrier((features, pieces))
-    pieces = lax.all_to_all(pieces, "yh", 0, 0, tiled=True)
-    sources = [
-        lax.ppermute(features, "x", [(i, (i - shift) % X) for i in range(X)]) if shift else features
-        for shift in SHIFTS
-    ]
-
     columns = HEAD_SIZE + FRESH_ROWS + 3 * RANK
     weights, smalls = call(
         functools.partial(plan_kernel, groups),
         [shape(columns, width), shape(5, SLOTS, LANES)],
-        [SMEM, SMEM] + [VMEM] * 6,
+        [SMEM, SMEM] + [ANY] * 5 + [VMEM],
+        [pltpu.VMEM((width, HEAD_SIZE), BF16), pltpu.SemaphoreType.DMA((7,))],
         moved=5 * 1024 * 1024,
+        limit=60,
     )(
         place,
         document_page_slots,
@@ -391,6 +405,16 @@
         key_value_up,
         document_of_row.reshape(1, rows),
     )
+    features, pieces, weights, smalls = lax.optimization_barrier(
+        (features, pieces, weights, smalls)
+    )
+    pieces = [
+        lax.ppermute(piece, "yh", [(i, (i + shift) % Y_HIGH) for i in range(Y_HIGH)]) if shift else piece
+        for shift, piece in zip(SHIFTS, pieces)
+    ]
+    features = jnp.broadcast_to(features.reshape(1, Y, part, rows), (X, Y, part, rows))
+    features = lax.all_to_all(features, "x", 0, 0, tiled=True)
+
     message, fresh, queries_t = call(
         functools.partial(project_kernel, groups),
         [
@@ -398,13 +422,13 @@
             shape(FRESH_ROWS, rows),
             shape(HEAD_SIZE, rows),
         ],
-        [SMEM] + [VMEM] * (X + 4),
+        [SMEM] + [VMEM] * 5,
         [pltpu.VMEM((width, rows), BF16), pltpu.VMEM((HEAD_SIZE, rows), F32)],
         flops=2 * width * rows * 256,
         moved=4 * 1024 * 1024,
     )(
         place,
-        *sources,
+        features,
         weights,
         input_norm_gain.reshape(Y, X, part).transpose(1, 0, 2),
         smalls,
@@ -415,7 +439,6 @@
         ("yh", "yl"),
         [(y, 2 * y if y < Y_HIGH else 2 * (y - Y_HIGH) + 1) for y in range(Y)],
     )
-    message, pieces = lax.optimization_barrier((message, pieces))
     received = lax.all_to_all(message, "grp", 0, 0, tiled=True)
 
     message, slot_adapters = call(
@@ -424,15 +447,16 @@
         [VMEM],
         moved=1024 * 1024,
     )(received)
+    message, pieces = lax.optimization_barrier((message, pieces))
     gathered = lax.all_to_all(message, ("yl", "x"), 0, 0, tiled=True)
 
     tokens = PIECE_TOKENS * Y_HIGH
     prepared = call(
         prepare_kernel,
         shape(tokens + tokens // DEPTH * VALUE_ROWS, DEPTH),
-        [VMEM],
+        [VMEM] * 4,
         moved=3 * 1024 * 1024,
-    )(pieces)
+    )(*pieces)
     message = call(
         attend_kernel,
         shape(BLOCK, RETURN_ROWS + FRESH_ROWS, LANES),

time: 124 us -> 118 us (0.952)
  waiting for transfers between devices: 23.3 us -> 14.3 us
  Pallas kernels: 14.8 us -> 19.4 us
  local copies, waits for them, and re-layouts: 6.42 us -> 3.9 us
    all_to_all x1, waiting for transfers between devices: 7.01 us -> 2.02 us  [per_device(): features = lax.all_to_all(features, ('yh', 'yl'), 0, 0, tiled=True)]
    unnamed x24 -> x14, local copies, waits for them, and re-layouts: 4.73 us -> 0.99 us
    ppermute x3, waiting for transfers between devices: 3.25 us -> 0.01 us  [per_device(): lax.ppermute(piece, 'yh', [(i, (i + shift) % Y_HIGH) for i in range(Y_HIG...]
    pallas_call x1, Pallas kernels: 1.18 us -> 4.31 us  [per_device(): call(functools.partial(plan_kernel, groups), [shape(columns, width), shap...]
    all_to_all x1, starting transfers between devices: 3.53 us -> 6 us  [per_device(): features = lax.all_to_all(features, 'x', 0, 0, tiled=True)]
    ppermute x3, starting transfers between devices: 13 us -> 10.8 us  [per_device(): lax.ppermute(piece, 'yh', [(i, (i + shift) % Y_HIGH) for i in range(Y_HIG...]
    pallas_call x1, Pallas kernels: 1.22 us -> 3.13 us  [per_device(): call(pack_kernel, [shape(PIECE_ROWS, HEAD_SIZE)] * Y_HIGH, [SMEM] + [ANY]...]
    broadcast_in_dim x0 -> x1, local copies, waits for them, and re-layouts: none -> 1.27 us  [per_device(): jnp.broadcast_to(features.reshape(1, Y, part, rows), (X, Y, part, rows))]
  transfers between devices with their start and end apart: 7 -> 7, of which waited for: 4 -> 3; matrix products, arithmetic and copies ran while one was open for 0% -> 1% of each run, Pallas kernels for 5% -> 11%
where the time goes in v7:
time: 118 us; the launch traced here: 117 us
  blocking collectives  49.9 us (42%)
  starting transfers between devices  28.8 us (24%)
  Pallas kernels  19.4 us (16%)
  waiting for transfers between devices  14.3 us (12%)
  local copies, waits for them, and re-layouts  3.9 us (3%)
    all_to_all x2, blocking collectives, per_device(): received = lax.all_to_all(message, 'grp', 0, 0, tiled=True)  36.3 us
    all_to_all x1, blocking collectives, per_device(): partials = lax.all_to_all(message, ('yl', 'x'), 0, 0, tiled=True)  13.6 us
    ppermute x3, starting transfers between devices, per_device(): lax.ppermute(piece, 'yh', [(i, (i + shift) % Y_HIGH) for i in range(Y_HIG...  10.8 us
    all_to_all x1, waiting for transfers between devices, per_device(): gathered = lax.all_to_all(message, ('yl', 'x'), 0, 0, tiled=True)  7.72 us
    all_to_all x1, starting transfers between devices, per_device(): features = lax.all_to_all(features, ('yh', 'yl'), 0, 0, tiled=True)  7.65 us
    all_to_all x1, starting transfers between devices, per_device(): features = lax.all_to_all(features, 'x', 0, 0, tiled=True)  6 us
    pallas_call x1, Pallas kernels, per_device(): call(attend_kernel, shape(BLOCK, RETURN_ROWS + FRESH_ROWS, LANES), [VMEM]...  5.82 us
    all_to_all x1, waiting for transfers between devices, per_device(): features = lax.all_to_all(features, 'x', 0, 0, tiled=True)  4.53 us
  transfers between devices with their start and end apart: 7, of which 3 were waited for; matrix products, arithmetic and copies ran while one was open for 1% of the time, Pallas kernels for 11%

profile of v7, /device:TPU:1, one launch (start us, length us, event | category | flops | bytes accessed | tf_op | source)
XLA Modules:
  0.0 117.0 jit_solution(8332518371771868609)
XLA Ops:
  0.0 1.5 %broadcast_in_dim.4 = bf16[8,160,128]{2,1,0:T(8,128)(2,1)} broadcast(bf16[160,128]{1,0:T(8,128)(2,1)} %bitcast.25), dimensions={1,2} | broadcast | bytes 368640 | tf_op jit(solution)/shard_map/broadcast_in_dim | solution.py:370
  1.5 7.7 %all-to-all-start = ((bf16[8,160,128]{2,1,0:T(8,128)(2,1)}), bf16[8,160,128]{2,1,0:T(8,128)(2,1)S(1)}, u32[]{:S(2)}, u32[]{:S(2)}) async-start(bf16[8,160,128]{2,1,0:T(8,128)(2,1)} %broadcast_in_dim.4), calls=%async_computation | async-start | bytes 655360 | tf_op jit(solution)/shard_map/all_to_all | solution.py:371
  9.2 0.6 pad_add_fusion.place
  9.8 3.1 %shard_map.127 = (bf16[1152,128]{1,0:T(8,128)(2,1)}, bf16[1152,128]{1,0:T(8,128)(2,1)}, bf16[1152,128]{1,0:T(8,128)(2,1)}, bf16[1152,128]{1,0:T(8,128)(2,1)}) custom-call(s32[2]{0:T(128)} %pad_add_fusion.place, bf16[512,512]{1,0:T(8,128)(2,1)} %bitcast.20, bf16[512,512]{1,0:T(8,128)(2,1)} %bitcast.21, bf16[128,128]{1,0:T(8,128)(2,1)} %bitcast.26), custom_call_target="tpu_custom_call" | custom-call | bytes 3145728 | tf_op jit(solution)/shard_map/pallas_call | solution.py:372
  12.9 4.3 %shard_map.128 = (bf16[208,5120]{1,0:T(8,128)(2,1)}, bf16[5,256,128]{2,1,0:T(8,128)(2,1)}) custom-call(s32[2]{0:T(128)} %pad_add_fusion.place, s32[16,128]{1,0:T(8,128)} %page_slots.1, bf16[5120,128]{1,0:T(8,128)(2,1)} %query_weight_far.1, bf16[32,5120]{1,0:T(8,128)(2,1)} %bitcast.23, bf16[48,5120]{1,0:T(8,128)(2,1)} %bitcast.22, bf16[256,128]{1,0:T(8,128)(2,1)} %bitcast.24, ...), custom_call_target="tpu_custom_call" | custom-call | bytes 5242880 | tf_op jit(solution)/shard_map/pallas_call | solution.py:391
  17.2 2.0 %all-to-all-done = bf16[8,160,128]{2,1,0:T(8,128)(2,1)S(1)} async-done(((bf16[8,160,128]{2,1,0:T(8,128)(2,1)}), bf16[8,160,128]{2,1,0:T(8,128)(2,1)S(1)}, u32[]{:S(2)}, u32[]{:S(2)}) %all-to-all-start) | async-done | bytes 327712 | tf_op jit(solution)/shard_map/all_to_all | solution.py:371
  19.3 1.3 %broadcast_in_dim.5 = bf16[4,8,160,128]{3,2,1,0:T(8,128)(2,1)} broadcast(bf16[8,160,128]{2,1,0:T(8,128)(2,1)S(1)} %all-to-all-done), dimensions={1,2,3} | broadcast | bytes 1638400 | tf_op jit(solution)/shard_map/broadcast_in_dim | solution.py:415
  20.6 6.0 %all-to-all-start.1 = ((bf16[4,8,160,128]{3,2,1,0:T(8,128)(2,1)}), bf16[4,8,160,128]{3,2,1,0:T(8,128)(2,1)S(1)}, u32[]{:S(2)}, u32[]{:S(2)}) async-start(bf16[4,8,160,128]{3,2,1,0:T(8,128)(2,1)} %broadcast_in_dim.5), calls=%async_computation.1 | async-start | bytes 2621440 | tf_op jit(solution)/shard_map/all_to_all | solution.py:416
  26.6 1.9 %collective-permute-start = (bf16[1152,128]{1,0:T(8,128)(2,1)}, bf16[1152,128]{1,0:T(8,128)(2,1)}, u32[]{:S(2)}, u32[]{:S(2)}) collective-permute-start(bf16[1152,128]{1,0:T(8,128)(2,1)} %get-tuple-element.40), channel_id=1, source_target_pairs={{0,8},{8,16},{16,24},{24,0},{1,9},{9,17},{17,25},{25,1},{2,10},{10... | collective-permute-start | bytes 884744 | tf_op jit(solution)/shard_map/ppermute | solution.py:412
  28.5 5.5 %collective-permute-start.1 = (bf16[1152,128]{1,0:T(8,128)(2,1)}, bf16[1152,128]{1,0:T(8,128)(2,1)}, u32[]{:S(2)}, u32[]{:S(2)}) collective-permute-start(bf16[1152,128]{1,0:T(8,128)(2,1)} %get-tuple-element.41), channel_id=1, source_target_pairs={{0,24},{8,0},{16,8},{24,16},{1,25},{9,1},{17,9},{25,17},{2,26},{10... | collective-permute-start | bytes 884744 | tf_op jit(solution)/shard_map/ppermute | solution.py:412
  34.0 3.4 %collective-permute-start.2 = (bf16[1152,128]{1,0:T(8,128)(2,1)}, bf16[1152,128]{1,0:T(8,128)(2,1)}, u32[]{:S(2)}, u32[]{:S(2)}) collective-permute-start(bf16[1152,128]{1,0:T(8,128)(2,1)} %get-tuple-element.42), channel_id=1, source_target_pairs={{0,16},{8,24},{16,0},{24,8},{1,17},{9,25},{17,1},{25,9},{2,18},{10... | collective-permute-start | bytes 884744 | tf_op jit(solution)/shard_map/ppermute | solution.py:412
  37.4 0.0 copy-done.6
  37.4 0.1 reshape.33
  37.5 4.5 %all-to-all-done.1.sources = bf16[4,8,160,128]{3,2,1,0:T(8,128)(2,1)S(1)} async-done(((bf16[4,8,160,128]{3,2,1,0:T(8,128)(2,1)}), bf16[4,8,160,128]{3,2,1,0:T(8,128)(2,1)S(1)}, u32[]{:S(2)}, u32[]{:S(2)}) %all-to-all-start.1) | async-done | bytes 1310752 | tf_op jit(solution)/shard_map/all_to_all | solution.py:416
  42.0 0.0 copy-done
  42.0 1.0 copy-done.1
  43.0 2.5 %shard_map.129 = (bf16[16,32,128]{2,1,0:T(8,128)(2,1)S(1)}, bf16[32,128]{1,0:T(8,128)(2,1)S(1)}, bf16[128,128]{1,0:T(8,128)(2,1)S(1)}) custom-call(s32[2]{0:T(128)S(1)} %copy-done.4, bf16[4,8,160,128]{3,2,1,0:T(8,128)(2,1)S(1)} %all-to-all-done.1.sources, bf16[208,5120]{1,0:T(8,128)(2,1)S(1)} %copy-done, f32[4,8,160]{2,1,0:T(8,128)S(1)} %bitcast.17, ...), custom_call_target="tpu_custom_call" | custom-call | flops 335544320 | bytes 4194304 | tf_op jit(solution)/shard_map/pallas_call | solution.py:418
  45.5 22.8 %all_to_all.30.received = bf16[16,32,128]{2,1,0:T(8,128)(2,1)S(1)} all-to-all(bf16[16,32,128]{2,1,0:T(8,128)(2,1)S(1)} %get-tuple-element.37), channel_id=1, replica_groups=mesh['grp'=16,'yh'=4,'yl'=2,'x'=4] {'grp'}, dimensions={0} | all-to-all | bytes 262144 | tf_op jit(solution)/shard_map/all_to_all | solution.py:442
  68.3 0.9 shard_map.130
  69.3 0.0 collective-permute-done.piece_1
  69.3 0.0 collective-permute-done.1.piece_2
  69.3 0.0 collective-permute-done.2.piece_3
  69.3 3.5 %all-to-all-start.3 = ((bf16[8,288,128]{2,1,0:T(8,128)(2,1)}), bf16[8,288,128]{2,1,0:T(8,128)(2,1)S(1)}, u32[]{:S(2)}, u32[]{:S(2)}) async-start(bf16[8,288,128]{2,1,0:T(8,128)(2,1)} %get-tuple-element.43), calls=%async_computation.3 | async-start | bytes 1179648 | tf_op jit(solution)/shard_map/all_to_all | solution.py:451
  72.9 0.8 collective-permute-start.3
  73.7 1.6 %shard_map.131.prepared = bf16[3328,256]{1,0:T(8,128)(2,1)S(1)} custom-call(bf16[1152,128]{1,0:T(8,128)(2,1)S(1)} %copy-done.3, bf16[1152,128]{1,0:T(8,128)(2,1)} %collective-permute-done.piece_1, bf16[1152,128]{1,0:T(8,128)(2,1)} %collective-permute-done.1.piece_2, bf16[1152,128]{1,0:T(8,128)(2,1)} %collective-permute-done.2.piece_3), custom_call_target="tpu_custom_call" | custom-call | bytes 3145728 | tf_op jit(solution)/shard_map/pallas_call | solution.py:454
  75.3 0.0 collective-permute-done.3.fresh
  75.3 7.7 %all-to-all-done.3.queries = bf16[8,288,128]{2,1,0:T(8,128)(2,1)S(1)} async-done(((bf16[8,288,128]{2,1,0:T(8,128)(2,1)}), bf16[8,288,128]{2,1,0:T(8,128)(2,1)S(1)}, u32[]{:S(2)}, u32[]{:S(2)}) %all-to-all-start.3) | async-done | bytes 589856 | tf_op jit(solution)/shard_map/all_to_all | solution.py:451
  83.0 5.8 %shard_map.132 = bf16[8,304,128]{2,1,0:T(8,128)(2,1)S(1)} custom-call(bf16[8,288,128]{2,1,0:T(8,128)(2,1)S(1)} %all-to-all-done.3.queries, f32[8,256]{1,0:T(8,128)S(1)} %get-tuple-element.44.slot_adapters, bf16[5,256,128]{2,1,0:T(8,128)(2,1)S(1)} %copy-done.2, bf16[3328,256]{1,0:T(8,128)(2,1)S(1)} %shard_map.131.prepared, ...), custom_call_target="tpu_custom_call" | custom-call | flops 4294967296 | bytes 3145728 | tf_op jit(solution)/shard_map/pallas_call | solution.py:460
  88.8 13.6 %all_to_all.31.partials = bf16[8,304,128]{2,1,0:T(8,128)(2,1)S(1)} all-to-all(bf16[8,304,128]{2,1,0:T(8,128)(2,1)S(1)} %shard_map.132), channel_id=1, replica_groups=mesh['grp'=16,'yh'=4,'yl'=2,'x'=4] {'yl','x'}, dimensions={0} | all-to-all | bytes 1245184 | tf_op jit(solution)/shard_map/all_to_all | solution.py:474
  102.5 0.2 shard_map.133
  102.7 13.4 %all_to_all.32.received = bf16[16,32,128]{2,1,0:T(8,128)(2,1)S(1)} all-to-all(bf16[16,32,128]{2,1,0:T(8,128)(2,1)S(1)} %shard_map.133), channel_id=1, replica_groups=mesh['grp'=16,'yh'=4,'yl'=2,'x'=4] {'grp'}, dimensions={0} | all-to-all | bytes 262144 | tf_op jit(solution)/shard_map/all_to_all | solution.py:483
  116.1 0.9 shard_map.134
  (12 shorter events, 0.0 us)
Async XLA Ops:
  1.5 17.7 %all-to-all-start = ((bf16[8,160,128]{2,1,0:T(8,128)(2,1)}), bf16[8,160,128]{2,1,0:T(8,128)(2,1)S(1)}, u32[]{:S(2)}, u32[]{:S(2)}) async-start(bf16[8,160,128]{2,1,0:T(8,128)(2,1)} %broadcast_in_dim.4), calls=%async_computation | async-start | bytes 655360 | tf_op jit(solution)/shard_map/all_to_all | solution.py:371
  20.5 16.8 %copy-start.6 = (f32[5120]{0:T(1024)S(1)}, f32[5120]{0:T(1024)}, u32[]{:S(2)}) copy-start(f32[5120]{0:T(1024)} %param.14) | copy-start | bytes 61444
  20.5 21.5 %copy-start = (bf16[208,5120]{1,0:T(8,128)(2,1)S(1)}, bf16[208,5120]{1,0:T(8,128)(2,1)}, u32[]{:S(2)}) copy-start(bf16[208,5120]{1,0:T(8,128)(2,1)} %get-tuple-element.35.weights) | copy-start | bytes 6389764
  20.5 21.5 %copy-start.4 = (s32[2]{0:T(128)S(1)}, s32[2]{0:T(128)}, u32[]{:S(2)}) copy-start(s32[2]{0:T(128)} %pad_add_fusion.place) | copy-start | bytes 28
  20.5 21.5 %copy-start.5 = (s32[128]{0:T(128)S(1)}, s32[128]{0:T(128)}, u32[]{:S(2)}) copy-start(s32[128]{0:T(128)} %param.23) | copy-start | bytes 1540
  20.6 21.4 %all-to-all-start.1 = ((bf16[4,8,160,128]{3,2,1,0:T(8,128)(2,1)}), bf16[4,8,160,128]{3,2,1,0:T(8,128)(2,1)S(1)}, u32[]{:S(2)}, u32[]{:S(2)}) async-start(bf16[4,8,160,128]{3,2,1,0:T(8,128)(2,1)} %broadcast_in_dim.5), calls=%async_computation.1 | async-start | bytes 2621440 | tf_op jit(solution)/shard_map/all_to_all | solution.py:416
  26.6 42.7 %collective-permute-start = (bf16[1152,128]{1,0:T(8,128)(2,1)}, bf16[1152,128]{1,0:T(8,128)(2,1)}, u32[]{:S(2)}, u32[]{:S(2)}) collective-permute-start(bf16[1152,128]{1,0:T(8,128)(2,1)} %get-tuple-element.40), channel_id=1, source_target_pairs={{0,8},{8,16},{16,24},{24,0},{1,9},{9,17},{17,25},{25,1},{2,10},{10... | collective-permute-start | bytes 884744 | tf_op jit(solution)/shard_map/ppermute | solution.py:412
  28.5 40.8 %collective-permute-start.1 = (bf16[1152,128]{1,0:T(8,128)(2,1)}, bf16[1152,128]{1,0:T(8,128)(2,1)}, u32[]{:S(2)}, u32[]{:S(2)}) collective-permute-start(bf16[1152,128]{1,0:T(8,128)(2,1)} %get-tuple-element.41), channel_id=1, source_target_pairs={{0,24},{8,0},{16,8},{24,16},{1,25},{9,1},{17,9},{25,17},{2,26},{10... | collective-permute-start | bytes 884744 | tf_op jit(solution)/shard_map/ppermute | solution.py:412
  34.0 35.3 %collective-permute-start.2 = (bf16[1152,128]{1,0:T(8,128)(2,1)}, bf16[1152,128]{1,0:T(8,128)(2,1)}, u32[]{:S(2)}, u32[]{:S(2)}) collective-permute-start(bf16[1152,128]{1,0:T(8,128)(2,1)} %get-tuple-element.42), channel_id=1, source_target_pairs={{0,16},{8,24},{16,0},{24,8},{1,17},{9,25},{17,1},{25,9},{2,18},{10... | collective-permute-start | bytes 884744 | tf_op jit(solution)/shard_map/ppermute | solution.py:412
  42.0 1.0 copy-start.1
  45.5 28.2 %copy-start.3 = (bf16[1152,128]{1,0:T(8,128)(2,1)S(1)}, bf16[1152,128]{1,0:T(8,128)(2,1)}, u32[]{:S(2)}) copy-start(bf16[1152,128]{1,0:T(8,128)(2,1)} %get-tuple-element.45.piece_0) | copy-start | bytes 884740
  69.3 13.7 %all-to-all-start.3 = ((bf16[8,288,128]{2,1,0:T(8,128)(2,1)}), bf16[8,288,128]{2,1,0:T(8,128)(2,1)S(1)}, u32[]{:S(2)}, u32[]{:S(2)}) async-start(bf16[8,288,128]{2,1,0:T(8,128)(2,1)} %get-tuple-element.43), calls=%async_computation.3 | async-start | bytes 1179648 | tf_op jit(solution)/shard_map/all_to_all | solution.py:451
  72.8 10.2 %copy-start.2 = (bf16[5,256,128]{2,1,0:T(8,128)(2,1)S(1)}, bf16[5,256,128]{2,1,0:T(8,128)(2,1)}, u32[]{:S(2)}) copy-start(bf16[5,256,128]{2,1,0:T(8,128)(2,1)} %get-tuple-element.36.smalls) | copy-start | bytes 983044
  72.9 2.4 %collective-permute-start.3 = (bf16[32,128]{1,0:T(8,128)(2,1)S(1)}, bf16[32,128]{1,0:T(8,128)(2,1)S(1)}, u32[]{:S(2)}, u32[]{:S(2)}) collective-permute-start(bf16[32,128]{1,0:T(8,128)(2,1)S(1)} %get-tuple-element.49), channel_id=1, source_target_pairs={{0,0},{4,8},{8,16},{12,24},{16,4},{20,12},{24,20},{28,28},{1,1},{5... | collective-permute-start | bytes 24584 | tf_op jit(solution)/shard_map/ppermute | solution.py:437

commit v8 on v7

--- a/solution.py
+++ b/solution.py
@@ -122,6 +122,7 @@
     for d in range(page_slots.shape[0]):
         target = jnp.where(document == d, page_slots[d, 0] // page_slots.shape[1], target)
     capacity = SLOTS // groups
+    target = target % 2 * (groups // 2) + target // 2
     group = lax.broadcasted_iota(jnp.int32, (16, rows), 0)
     match = (group == target).astype(F32)
     before = (
@@ -357,7 +358,7 @@
     document_of_row,
     document_page_slots,
 ):
-    groups = lax.axis_size("grp")
+    groups = lax.axis_size("z") * lax.axis_size("core")
     capacity = SLOTS // groups
     rows, part = residual_input.shape
     width = part * Y * X
@@ -439,7 +440,7 @@
         ("yh", "yl"),
         [(y, 2 * y if y < Y_HIGH else 2 * (y - Y_HIGH) + 1) for y in range(Y)],
     )
-    received = lax.all_to_all(message, "grp", 0, 0, tiled=True)
+    received = lax.all_to_all(message, ("core", "z"), 0, 0, tiled=True)
 
     message, slot_adapters = call(
         functools.partial(turn_kernel, groups),
@@ -480,7 +481,7 @@
         flops=SLOTS * HEAD_SIZE * 16,
         moved=1024 * 1024,
     )(partials)
-    received = lax.all_to_all(message, "grp", 0, 0, tiled=True)
+    received = lax.all_to_all(message, ("core", "z"), 0, 0, tiled=True)
 
     return call(
         functools.partial(finish_kernel, groups),
@@ -494,24 +495,25 @@
 def solution(mesh):
     groups = mesh.devices.shape[0]
     split = Mesh(
-        mesh.devices.reshape(groups, Y_HIGH, Y_LOW, X), ("grp", "yh", "yl", "x")
+        mesh.devices.reshape(groups // 2, 2, Y_HIGH, Y_LOW, X), ("z", "core", "yh", "yl", "x")
     )
     tp = ("yh", "yl", "x")
+    grp = ("z", "core")
     in_specs = (
-        P("grp", tp),
+        P(grp, tp),
         P(),
         P(None, tp),
         P(None, tp),
         P(),
         P(None, None, tp),
         P(),
-        P(("grp",) + tp, None, None),
-        P(("grp",) + tp, None, None),
-        P(("grp",) + tp, None, None),
-        P("grp"),
-        P("grp", None),
+        P(grp + tp, None, None),
+        P(grp + tp, None, None),
+        P(grp + tp, None, None),
+        P(grp),
+        P(grp, None),
         P(),
     )
     return jax.shard_map(
-        per_device, mesh=split, in_specs=in_specs, out_specs=P("grp", tp), check_vma=False
-    )
+        per_device, mesh=split, in_specs=in_specs, out_specs=P(grp, tp), check_vma=False
+    )

time: 118 us -> 116 us (0.983)
  waiting for transfers between devices: 14.3 us -> 12.1 us
    all_to_all x1, waiting for transfers between devices: 7.72 us -> 5.52 us  [per_device(): gathered = lax.all_to_all(message, ('yl', 'x'), 0, 0, tiled=True)]
where the time goes in v8:
time: 116 us; the launch traced here: 115 us
  blocking collectives  50.1 us (43%)
  starting transfers between devices  28.8 us (25%)
  Pallas kernels  19.4 us (17%)
  waiting for transfers between devices  12.1 us (10%)
  local copies, waits for them, and re-layouts  3.9 us (3%)
    all_to_all x2, blocking collectives, per_device(): received = lax.all_to_all(message, ('core', 'z'), 0, 0, tiled=True)  35.9 us
    all_to_all x1, blocking collectives, per_device(): partials = lax.all_to_all(message, ('yl', 'x'), 0, 0, tiled=True)  14.2 us
    ppermute x3, starting transfers between devices, per_device(): lax.ppermute(piece, 'yh', [(i, (i + shift) % Y_HIGH) for i in range(Y_HIG...  10.8 us
    all_to_all x1, starting transfers between devices, per_device(): features = lax.all_to_all(features, ('yh', 'yl'), 0, 0, tiled=True)  7.65 us
    all_to_all x1, starting transfers between devices, per_device(): features = lax.all_to_all(features, 'x', 0, 0, tiled=True)  6 us
    pallas_call x1, Pallas kernels, per_device(): call(attend_kernel, shape(BLOCK, RETURN_ROWS + FRESH_ROWS, LANES), [VMEM]...  5.81 us
    all_to_all x1, waiting for transfers between devices, per_device(): gathered = lax.all_to_all(message, ('yl', 'x'), 0, 0, tiled=True)  5.52 us
    all_to_all x1, waiting for transfers between devices, per_device(): features = lax.all_to_all(features, 'x', 0, 0, tiled=True)  4.53 us
  transfers between devices with their start and end apart: 7, of which 3 were waited for; matrix products, arithmetic and copies ran while one was open for 1% of the time, Pallas kernels for 11%

profile of v8, /device:TPU:1, one launch (start us, length us, event | category | flops | bytes accessed | tf_op | source)
XLA Modules:
  0.0 115.0 jit_solution(9275122779525581133)
XLA Ops:
  0.0 1.5 %broadcast_in_dim.4 = bf16[8,160,128]{2,1,0:T(8,128)(2,1)} broadcast(bf16[160,128]{1,0:T(8,128)(2,1)} %bitcast.25), dimensions={1,2} | broadcast | bytes 368640 | tf_op jit(solution)/shard_map/broadcast_in_dim | solution.py:371
  1.5 7.7 %all-to-all-start = ((bf16[8,160,128]{2,1,0:T(8,128)(2,1)}), bf16[8,160,128]{2,1,0:T(8,128)(2,1)S(1)}, u32[]{:S(2)}, u32[]{:S(2)}) async-start(bf16[8,160,128]{2,1,0:T(8,128)(2,1)} %broadcast_in_dim.4), calls=%async_computation | async-start | bytes 655360 | tf_op jit(solution)/shard_map/all_to_all | solution.py:372
  9.2 0.6 pad_add_fusion.place
  9.8 3.1 %shard_map.127 = (bf16[1152,128]{1,0:T(8,128)(2,1)}, bf16[1152,128]{1,0:T(8,128)(2,1)}, bf16[1152,128]{1,0:T(8,128)(2,1)}, bf16[1152,128]{1,0:T(8,128)(2,1)}) custom-call(s32[2]{0:T(128)} %pad_add_fusion.place, bf16[512,512]{1,0:T(8,128)(2,1)} %bitcast.20, bf16[512,512]{1,0:T(8,128)(2,1)} %bitcast.21, bf16[128,128]{1,0:T(8,128)(2,1)} %bitcast.26), custom_call_target="tpu_custom_call" | custom-call | bytes 3145728 | tf_op jit(solution)/shard_map/pallas_call | solution.py:373
  12.9 4.3 %shard_map.128 = (bf16[208,5120]{1,0:T(8,128)(2,1)}, bf16[5,256,128]{2,1,0:T(8,128)(2,1)}) custom-call(s32[2]{0:T(128)} %pad_add_fusion.place, s32[16,128]{1,0:T(8,128)} %page_slots.1, bf16[5120,128]{1,0:T(8,128)(2,1)} %query_weight_far.1, bf16[32,5120]{1,0:T(8,128)(2,1)} %bitcast.23, bf16[48,5120]{1,0:T(8,128)(2,1)} %bitcast.22, bf16[256,128]{1,0:T(8,128)(2,1)} %bitcast.24, ...), custom_call_target="tpu_custom_call" | custom-call | bytes 5242880 | tf_op jit(solution)/shard_map/pallas_call | solution.py:392
  17.3 2.0 %all-to-all-done = bf16[8,160,128]{2,1,0:T(8,128)(2,1)S(1)} async-done(((bf16[8,160,128]{2,1,0:T(8,128)(2,1)}), bf16[8,160,128]{2,1,0:T(8,128)(2,1)S(1)}, u32[]{:S(2)}, u32[]{:S(2)}) %all-to-all-start) | async-done | bytes 327712 | tf_op jit(solution)/shard_map/all_to_all | solution.py:372
  19.3 1.3 %broadcast_in_dim.5 = bf16[4,8,160,128]{3,2,1,0:T(8,128)(2,1)} broadcast(bf16[8,160,128]{2,1,0:T(8,128)(2,1)S(1)} %all-to-all-done), dimensions={1,2,3} | broadcast | bytes 1638400 | tf_op jit(solution)/shard_map/broadcast_in_dim | solution.py:416
  20.6 6.0 %all-to-all-start.1 = ((bf16[4,8,160,128]{3,2,1,0:T(8,128)(2,1)}), bf16[4,8,160,128]{3,2,1,0:T(8,128)(2,1)S(1)}, u32[]{:S(2)}, u32[]{:S(2)}) async-start(bf16[4,8,160,128]{3,2,1,0:T(8,128)(2,1)} %broadcast_in_dim.5), calls=%async_computation.1 | async-start | bytes 2621440 | tf_op jit(solution)/shard_map/all_to_all | solution.py:417
  26.6 1.9 %collective-permute-start = (bf16[1152,128]{1,0:T(8,128)(2,1)}, bf16[1152,128]{1,0:T(8,128)(2,1)}, u32[]{:S(2)}, u32[]{:S(2)}) collective-permute-start(bf16[1152,128]{1,0:T(8,128)(2,1)} %get-tuple-element.40), channel_id=1, source_target_pairs={{0,8},{8,16},{16,24},{24,0},{1,9},{9,17},{17,25},{25,1},{2,10},{10... | collective-permute-start | bytes 884744 | tf_op jit(solution)/shard_map/ppermute | solution.py:413
  28.5 5.5 %collective-permute-start.1 = (bf16[1152,128]{1,0:T(8,128)(2,1)}, bf16[1152,128]{1,0:T(8,128)(2,1)}, u32[]{:S(2)}, u32[]{:S(2)}) collective-permute-start(bf16[1152,128]{1,0:T(8,128)(2,1)} %get-tuple-element.41), channel_id=1, source_target_pairs={{0,24},{8,0},{16,8},{24,16},{1,25},{9,1},{17,9},{25,17},{2,26},{10... | collective-permute-start | bytes 884744 | tf_op jit(solution)/shard_map/ppermute | solution.py:413
  34.0 3.4 %collective-permute-start.2 = (bf16[1152,128]{1,0:T(8,128)(2,1)}, bf16[1152,128]{1,0:T(8,128)(2,1)}, u32[]{:S(2)}, u32[]{:S(2)}) collective-permute-start(bf16[1152,128]{1,0:T(8,128)(2,1)} %get-tuple-element.42), channel_id=1, source_target_pairs={{0,16},{8,24},{16,0},{24,8},{1,17},{9,25},{17,1},{25,9},{2,18},{10... | collective-permute-start | bytes 884744 | tf_op jit(solution)/shard_map/ppermute | solution.py:413
  37.4 0.1 reshape.33
  37.5 4.5 %all-to-all-done.1.sources = bf16[4,8,160,128]{3,2,1,0:T(8,128)(2,1)S(1)} async-done(((bf16[4,8,160,128]{3,2,1,0:T(8,128)(2,1)}), bf16[4,8,160,128]{3,2,1,0:T(8,128)(2,1)S(1)}, u32[]{:S(2)}, u32[]{:S(2)}) %all-to-all-start.1) | async-done | bytes 1310752 | tf_op jit(solution)/shard_map/all_to_all | solution.py:417
  42.0 0.0 copy-done
  42.0 0.0 copy-done.5
  42.0 1.0 copy-done.1
  43.0 2.5 %shard_map.129 = (bf16[16,32,128]{2,1,0:T(8,128)(2,1)S(1)}, bf16[32,128]{1,0:T(8,128)(2,1)S(1)}, bf16[128,128]{1,0:T(8,128)(2,1)S(1)}) custom-call(s32[2]{0:T(128)S(1)} %copy-done.4, bf16[4,8,160,128]{3,2,1,0:T(8,128)(2,1)S(1)} %all-to-all-done.1.sources, bf16[208,5120]{1,0:T(8,128)(2,1)S(1)} %copy-done, f32[4,8,160]{2,1,0:T(8,128)S(1)} %bitcast.17, ...), custom_call_target="tpu_custom_call" | custom-call | flops 335544320 | bytes 4194304 | tf_op jit(solution)/shard_map/pallas_call | solution.py:419
  45.5 21.0 %all_to_all.30.received = bf16[16,32,128]{2,1,0:T(8,128)(2,1)S(1)} all-to-all(bf16[16,32,128]{2,1,0:T(8,128)(2,1)S(1)} %get-tuple-element.37), channel_id=1, replica_groups=mesh['z'=8,'core'=2,'yh'=4,'yl'=2,'x'=4] {'core','z'}, dimensions={0} | all-to-all | bytes 262144 | tf_op jit(solution)/shard_map/all_to_all | solution.py:443
  66.5 0.9 shard_map.130
  67.4 0.0 collective-permute-done.piece_1
  67.4 0.0 collective-permute-done.1.piece_2
  67.4 0.0 collective-permute-done.2.piece_3
  67.4 3.5 %all-to-all-start.3 = ((bf16[8,288,128]{2,1,0:T(8,128)(2,1)}), bf16[8,288,128]{2,1,0:T(8,128)(2,1)S(1)}, u32[]{:S(2)}, u32[]{:S(2)}) async-start(bf16[8,288,128]{2,1,0:T(8,128)(2,1)} %get-tuple-element.43), calls=%async_computation.3 | async-start | bytes 1179648 | tf_op jit(solution)/shard_map/all_to_all | solution.py:452
  71.0 0.8 collective-permute-start.3
  71.8 1.6 %shard_map.131.prepared = bf16[3328,256]{1,0:T(8,128)(2,1)S(1)} custom-call(bf16[1152,128]{1,0:T(8,128)(2,1)S(1)} %copy-done.3, bf16[1152,128]{1,0:T(8,128)(2,1)} %collective-permute-done.piece_1, bf16[1152,128]{1,0:T(8,128)(2,1)} %collective-permute-done.1.piece_2, bf16[1152,128]{1,0:T(8,128)(2,1)} %collective-permute-done.2.piece_3), custom_call_target="tpu_custom_call" | custom-call | bytes 3145728 | tf_op jit(solution)/shard_map/pallas_call | solution.py:455
  73.4 0.0 collective-permute-done.3.fresh
  73.4 5.5 %all-to-all-done.3.queries = bf16[8,288,128]{2,1,0:T(8,128)(2,1)S(1)} async-done(((bf16[8,288,128]{2,1,0:T(8,128)(2,1)}), bf16[8,288,128]{2,1,0:T(8,128)(2,1)S(1)}, u32[]{:S(2)}, u32[]{:S(2)}) %all-to-all-start.3) | async-done | bytes 589856 | tf_op jit(solution)/shard_map/all_to_all | solution.py:452
  79.0 5.8 %shard_map.132 = bf16[8,304,128]{2,1,0:T(8,128)(2,1)S(1)} custom-call(bf16[8,288,128]{2,1,0:T(8,128)(2,1)S(1)} %all-to-all-done.3.queries, f32[8,256]{1,0:T(8,128)S(1)} %get-tuple-element.44.slot_adapters, bf16[5,256,128]{2,1,0:T(8,128)(2,1)S(1)} %copy-done.2, bf16[3328,256]{1,0:T(8,128)(2,1)S(1)} %shard_map.131.prepared, ...), custom_call_target="tpu_custom_call" | custom-call | flops 4294967296 | bytes 3145728 | tf_op jit(solution)/shard_map/pallas_call | solution.py:461
  84.8 14.2 %all_to_all.31.partials = bf16[8,304,128]{2,1,0:T(8,128)(2,1)S(1)} all-to-all(bf16[8,304,128]{2,1,0:T(8,128)(2,1)S(1)} %shard_map.132), channel_id=1, replica_groups=mesh['z'=8,'core'=2,'yh'=4,'yl'=2,'x'=4] {'yl','x'}, dimensions={0} | all-to-all | bytes 1245184 | tf_op jit(solution)/shard_map/all_to_all | solution.py:475
  98.9 0.2 shard_map.133
  99.2 14.9 %all_to_all.32.received = bf16[16,32,128]{2,1,0:T(8,128)(2,1)S(1)} all-to-all(bf16[16,32,128]{2,1,0:T(8,128)(2,1)S(1)} %shard_map.133), channel_id=1, replica_groups=mesh['z'=8,'core'=2,'yh'=4,'yl'=2,'x'=4] {'core','z'}, dimensions={0} | all-to-all | bytes 262144 | tf_op jit(solution)/shard_map/all_to_all | solution.py:484
  114.1 0.9 shard_map.134
  (12 shorter events, 0.0 us)
Async XLA Ops:
  1.5 17.7 %all-to-all-start = ((bf16[8,160,128]{2,1,0:T(8,128)(2,1)}), bf16[8,160,128]{2,1,0:T(8,128)(2,1)S(1)}, u32[]{:S(2)}, u32[]{:S(2)}) async-start(bf16[8,160,128]{2,1,0:T(8,128)(2,1)} %broadcast_in_dim.4), calls=%async_computation | async-start | bytes 655360 | tf_op jit(solution)/shard_map/all_to_all | solution.py:372
  20.5 16.8 %copy-start.6 = (f32[5120]{0:T(1024)S(1)}, f32[5120]{0:T(1024)}, u32[]{:S(2)}) copy-start(f32[5120]{0:T(1024)} %param.14) | copy-start | bytes 61444
  20.5 21.5 %copy-start = (bf16[208,5120]{1,0:T(8,128)(2,1)S(1)}, bf16[208,5120]{1,0:T(8,128)(2,1)}, u32[]{:S(2)}) copy-start(bf16[208,5120]{1,0:T(8,128)(2,1)} %get-tuple-element.35.weights) | copy-start | bytes 6389764
  20.5 21.5 %copy-start.4 = (s32[2]{0:T(128)S(1)}, s32[2]{0:T(128)}, u32[]{:S(2)}) copy-start(s32[2]{0:T(128)} %pad_add_fusion.place) | copy-start | bytes 28
  20.5 21.5 %copy-start.5 = (s32[128]{0:T(128)S(1)}, s32[128]{0:T(128)}, u32[]{:S(2)}) copy-start(s32[128]{0:T(128)} %param.23) | copy-start | bytes 1540
  20.6 21.4 %all-to-all-start.1 = ((bf16[4,8,160,128]{3,2,1,0:T(8,128)(2,1)}), bf16[4,8,160,128]{3,2,1,0:T(8,128)(2,1)S(1)}, u32[]{:S(2)}, u32[]{:S(2)}) async-start(bf16[4,8,160,128]{3,2,1,0:T(8,128)(2,1)} %broadcast_in_dim.5), calls=%async_computation.1 | async-start | bytes 2621440 | tf_op jit(solution)/shard_map/all_to_all | solution.py:417
  26.6 40.9 %collective-permute-start = (bf16[1152,128]{1,0:T(8,128)(2,1)}, bf16[1152,128]{1,0:T(8,128)(2,1)}, u32[]{:S(2)}, u32[]{:S(2)}) collective-permute-start(bf16[1152,128]{1,0:T(8,128)(2,1)} %get-tuple-element.40), channel_id=1, source_target_pairs={{0,8},{8,16},{16,24},{24,0},{1,9},{9,17},{17,25},{25,1},{2,10},{10... | collective-permute-start | bytes 884744 | tf_op jit(solution)/shard_map/ppermute | solution.py:413
  28.5 38.9 %collective-permute-start.1 = (bf16[1152,128]{1,0:T(8,128)(2,1)}, bf16[1152,128]{1,0:T(8,128)(2,1)}, u32[]{:S(2)}, u32[]{:S(2)}) collective-permute-start(bf16[1152,128]{1,0:T(8,128)(2,1)} %get-tuple-element.41), channel_id=1, source_target_pairs={{0,24},{8,0},{16,8},{24,16},{1,25},{9,1},{17,9},{25,17},{2,26},{10... | collective-permute-start | bytes 884744 | tf_op jit(solution)/shard_map/ppermute | solution.py:413
  34.0 33.5 %collective-permute-start.2 = (bf16[1152,128]{1,0:T(8,128)(2,1)}, bf16[1152,128]{1,0:T(8,128)(2,1)}, u32[]{:S(2)}, u32[]{:S(2)}) collective-permute-start(bf16[1152,128]{1,0:T(8,128)(2,1)} %get-tuple-element.42), channel_id=1, source_target_pairs={{0,16},{8,24},{16,0},{24,8},{1,17},{9,25},{17,1},{25,9},{2,18},{10... | collective-permute-start | bytes 884744 | tf_op jit(solution)/shard_map/ppermute | solution.py:413
  42.0 1.0 copy-start.1
  45.5 26.3 %copy-start.3 = (bf16[1152,128]{1,0:T(8,128)(2,1)S(1)}, bf16[1152,128]{1,0:T(8,128)(2,1)}, u32[]{:S(2)}) copy-start(bf16[1152,128]{1,0:T(8,128)(2,1)} %get-tuple-element.45.piece_0) | copy-start | bytes 884740
  67.4 11.5 %all-to-all-start.3 = ((bf16[8,288,128]{2,1,0:T(8,128)(2,1)}), bf16[8,288,128]{2,1,0:T(8,128)(2,1)S(1)}, u32[]{:S(2)}, u32[]{:S(2)}) async-start(bf16[8,288,128]{2,1,0:T(8,128)(2,1)} %get-tuple-element.43), calls=%async_computation.3 | async-start | bytes 1179648 | tf_op jit(solution)/shard_map/all_to_all | solution.py:452
  71.0 8.0 %copy-start.2 = (bf16[5,256,128]{2,1,0:T(8,128)(2,1)S(1)}, bf16[5,256,128]{2,1,0:T(8,128)(2,1)}, u32[]{:S(2)}) copy-start(bf16[5,256,128]{2,1,0:T(8,128)(2,1)} %get-tuple-element.36.smalls) | copy-start | bytes 983044
  71.0 2.4 %collective-permute-start.3 = (bf16[32,128]{1,0:T(8,128)(2,1)S(1)}, bf16[32,128]{1,0:T(8,128)(2,1)S(1)}, u32[]{:S(2)}, u32[]{:S(2)}) collective-permute-start(bf16[32,128]{1,0:T(8,128)(2,1)S(1)} %get-tuple-element.49), channel_id=1, source_target_pairs={{0,0},{4,8},{8,16},{12,24},{16,4},{20,12},{24,20},{28,28},{1,1},{5... | collective-permute-start | bytes 24584 | tf_op jit(solution)/shard_map/ppermute | solution.py:438

commit v9 on v8

--- a/solution.py
+++ b/solution.py
@@ -142,14 +142,18 @@
     sources,
     weights,
     gain,
-    smalls,
+    smalls_far,
     adapters,
     message,
     fresh,
     queries_t,
     normed,
     update,
+    smalls,
+    sems,
 ):
+    load = pltpu.make_async_copy(smalls_far, smalls, sems.at[0])
+    load.start()
     device = place[0]
     part = gain.shape[2]
     width = normed.shape[0]
@@ -166,6 +170,7 @@
             start = (y * X + x) * part
             normed[pl.ds(start, part), :] = block.astype(BF16)
     total = dot(weights[...], normed[...], 1, 0)
+    load.wait()
 
     adapter = adapters[...]
     low = total[HEAD_SIZE + FRESH_ROWS :].astype(BF16)
@@ -423,8 +428,13 @@
             shape(FRESH_ROWS, rows),
             shape(HEAD_SIZE, rows),
         ],
-        [SMEM] + [VMEM] * 5,
-        [pltpu.VMEM((width, rows), BF16), pltpu.VMEM((HEAD_SIZE, rows), F32)],
+        [SMEM, VMEM, VMEM, VMEM, ANY, VMEM],
+        [
+            pltpu.VMEM((width, rows), BF16),
+            pltpu.VMEM((HEAD_SIZE, rows), F32),
+            pltpu.VMEM((5, SLOTS, LANES), BF16),
+            pltpu.SemaphoreType.DMA((1,)),
+        ],
         flops=2 * width * rows * 256,
         moved=4 * 1024 * 1024,
     )(

time: 116 us -> 116 us (level)
  no operation moved by 1% of the time
where the time goes in v9:
time: 116 us; the launch traced here: 115 us
  blocking collectives  50 us (43%)
  starting transfers between devices  28.8 us (25%)
  Pallas kernels  19.5 us (17%)
  waiting for transfers between devices  12.1 us (10%)
  local copies, waits for them, and re-layouts  3.9 us (3%)
    all_to_all x2, blocking collectives, per_device(): received = lax.all_to_all(message, ('core', 'z'), 0, 0, tiled=True)  35.8 us
    all_to_all x1, blocking collectives, per_device(): partials = lax.all_to_all(message, ('yl', 'x'), 0, 0, tiled=True)  14.2 us
    ppermute x3, starting transfers between devices, per_device(): lax.ppermute(piece, 'yh', [(i, (i + shift) % Y_HIGH) for i in range(Y_HIG...  10.8 us
    all_to_all x1, starting transfers between devices, per_device(): features = lax.all_to_all(features, ('yh', 'yl'), 0, 0, tiled=True)  7.65 us
    all_to_all x1, starting transfers between devices, per_device(): features = lax.all_to_all(features, 'x', 0, 0, tiled=True)  6 us
    pallas_call x1, Pallas kernels, per_device(): call(attend_kernel, shape(BLOCK, RETURN_ROWS + FRESH_ROWS, LANES), [VMEM]...  5.81 us
    all_to_all x1, waiting for transfers between devices, per_device(): gathered = lax.all_to_all(message, ('yl', 'x'), 0, 0, tiled=True)  5.52 us
    all_to_all x1, waiting for transfers between devices, per_device(): features = lax.all_to_all(features, 'x', 0, 0, tiled=True)  4.53 us
  transfers between devices with their start and end apart: 7, of which 3 were waited for; matrix products, arithmetic and copies ran while one was open for 1% of the time, Pallas kernels for 11%

profile of v9, /device:TPU:1, one launch (start us, length us, event | category | flops | bytes accessed | tf_op | source)
XLA Modules:
  0.0 115.0 jit_solution(13499252770889000834)
XLA Ops:
  0.0 1.5 %broadcast_in_dim.4 = bf16[8,160,128]{2,1,0:T(8,128)(2,1)} broadcast(bf16[160,128]{1,0:T(8,128)(2,1)} %bitcast.25), dimensions={1,2} | broadcast | bytes 368640 | tf_op jit(solution)/shard_map/broadcast_in_dim | solution.py:376
  1.5 7.7 %all-to-all-start = ((bf16[8,160,128]{2,1,0:T(8,128)(2,1)}), bf16[8,160,128]{2,1,0:T(8,128)(2,1)S(1)}, u32[]{:S(2)}, u32[]{:S(2)}) async-start(bf16[8,160,128]{2,1,0:T(8,128)(2,1)} %broadcast_in_dim.4), calls=%async_computation | async-start | bytes 655360 | tf_op jit(solution)/shard_map/all_to_all | solution.py:377
  9.2 0.6 pad_add_fusion.place
  9.8 3.1 %shard_map.127 = (bf16[1152,128]{1,0:T(8,128)(2,1)}, bf16[1152,128]{1,0:T(8,128)(2,1)}, bf16[1152,128]{1,0:T(8,128)(2,1)}, bf16[1152,128]{1,0:T(8,128)(2,1)}) custom-call(s32[2]{0:T(128)} %pad_add_fusion.place, bf16[512,512]{1,0:T(8,128)(2,1)} %bitcast.20, bf16[512,512]{1,0:T(8,128)(2,1)} %bitcast.21, bf16[128,128]{1,0:T(8,128)(2,1)} %bitcast.26), custom_call_target="tpu_custom_call" | custom-call | bytes 3145728 | tf_op jit(solution)/shard_map/pallas_call | solution.py:378
  12.9 4.3 %shard_map.128 = (bf16[208,5120]{1,0:T(8,128)(2,1)}, bf16[5,256,128]{2,1,0:T(8,128)(2,1)}) custom-call(s32[2]{0:T(128)} %pad_add_fusion.place, s32[16,128]{1,0:T(8,128)} %page_slots.1, bf16[5120,128]{1,0:T(8,128)(2,1)} %query_weight_far.1, bf16[32,5120]{1,0:T(8,128)(2,1)} %bitcast.23, bf16[48,5120]{1,0:T(8,128)(2,1)} %bitcast.22, bf16[256,128]{1,0:T(8,128)(2,1)} %bitcast.24, ...), custom_call_target="tpu_custom_call" | custom-call | bytes 5242880 | tf_op jit(solution)/shard_map/pallas_call | solution.py:397
  17.3 2.0 %all-to-all-done = bf16[8,160,128]{2,1,0:T(8,128)(2,1)S(1)} async-done(((bf16[8,160,128]{2,1,0:T(8,128)(2,1)}), bf16[8,160,128]{2,1,0:T(8,128)(2,1)S(1)}, u32[]{:S(2)}, u32[]{:S(2)}) %all-to-all-start) | async-done | bytes 327712 | tf_op jit(solution)/shard_map/all_to_all | solution.py:377
  19.3 1.3 %broadcast_in_dim.5 = bf16[4,8,160,128]{3,2,1,0:T(8,128)(2,1)} broadcast(bf16[8,160,128]{2,1,0:T(8,128)(2,1)S(1)} %all-to-all-done), dimensions={1,2,3} | broadcast | bytes 1638400 | tf_op jit(solution)/shard_map/broadcast_in_dim | solution.py:421
  20.6 6.0 %all-to-all-start.1 = ((bf16[4,8,160,128]{3,2,1,0:T(8,128)(2,1)}), bf16[4,8,160,128]{3,2,1,0:T(8,128)(2,1)S(1)}, u32[]{:S(2)}, u32[]{:S(2)}) async-start(bf16[4,8,160,128]{3,2,1,0:T(8,128)(2,1)} %broadcast_in_dim.5), calls=%async_computation.1 | async-start | bytes 2621440 | tf_op jit(solution)/shard_map/all_to_all | solution.py:422
  26.6 1.9 %collective-permute-start = (bf16[1152,128]{1,0:T(8,128)(2,1)}, bf16[1152,128]{1,0:T(8,128)(2,1)}, u32[]{:S(2)}, u32[]{:S(2)}) collective-permute-start(bf16[1152,128]{1,0:T(8,128)(2,1)} %get-tuple-element.40), channel_id=1, source_target_pairs={{0,8},{8,16},{16,24},{24,0},{1,9},{9,17},{17,25},{25,1},{2,10},{10... | collective-permute-start | bytes 884744 | tf_op jit(solution)/shard_map/ppermute | solution.py:418
  28.5 5.5 %collective-permute-start.1 = (bf16[1152,128]{1,0:T(8,128)(2,1)}, bf16[1152,128]{1,0:T(8,128)(2,1)}, u32[]{:S(2)}, u32[]{:S(2)}) collective-permute-start(bf16[1152,128]{1,0:T(8,128)(2,1)} %get-tuple-element.41), channel_id=1, source_target_pairs={{0,24},{8,0},{16,8},{24,16},{1,25},{9,1},{17,9},{25,17},{2,26},{10... | collective-permute-start | bytes 884744 | tf_op jit(solution)/shard_map/ppermute | solution.py:418
  34.0 3.4 %collective-permute-start.2 = (bf16[1152,128]{1,0:T(8,128)(2,1)}, bf16[1152,128]{1,0:T(8,128)(2,1)}, u32[]{:S(2)}, u32[]{:S(2)}) collective-permute-start(bf16[1152,128]{1,0:T(8,128)(2,1)} %get-tuple-element.42), channel_id=1, source_target_pairs={{0,16},{8,24},{16,0},{24,8},{1,17},{9,25},{17,1},{25,9},{2,18},{10... | collective-permute-start | bytes 884744 | tf_op jit(solution)/shard_map/ppermute | solution.py:418
  37.4 0.1 reshape.33
  37.5 4.5 %all-to-all-done.1.sources = bf16[4,8,160,128]{3,2,1,0:T(8,128)(2,1)S(1)} async-done(((bf16[4,8,160,128]{3,2,1,0:T(8,128)(2,1)}), bf16[4,8,160,128]{3,2,1,0:T(8,128)(2,1)S(1)}, u32[]{:S(2)}, u32[]{:S(2)}) %all-to-all-start.1) | async-done | bytes 1310752 | tf_op jit(solution)/shard_map/all_to_all | solution.py:422
  42.0 0.0 copy-done
  42.0 0.0 copy-done.5
  42.0 1.0 copy-done.1
  43.0 2.6 %shard_map.129 = (bf16[16,32,128]{2,1,0:T(8,128)(2,1)S(1)}, bf16[32,128]{1,0:T(8,128)(2,1)S(1)}, bf16[128,128]{1,0:T(8,128)(2,1)S(1)}) custom-call(s32[2]{0:T(128)S(1)} %copy-done.4, bf16[4,8,160,128]{3,2,1,0:T(8,128)(2,1)S(1)} %all-to-all-done.1.sources, bf16[208,5120]{1,0:T(8,128)(2,1)S(1)} %copy-done, f32[4,8,160]{2,1,0:T(8,128)S(1)} %bitcast.17, ...), custom_call_target="tpu_custom_call" | custom-call | flops 335544320 | bytes 4194304 | tf_op jit(solution)/shard_map/pallas_call | solution.py:424
  45.6 21.0 %all_to_all.30.received = bf16[16,32,128]{2,1,0:T(8,128)(2,1)S(1)} all-to-all(bf16[16,32,128]{2,1,0:T(8,128)(2,1)S(1)} %get-tuple-element.37), channel_id=1, replica_groups=mesh['z'=8,'core'=2,'yh'=4,'yl'=2,'x'=4] {'core','z'}, dimensions={0} | all-to-all | bytes 262144 | tf_op jit(solution)/shard_map/all_to_all | solution.py:453
  66.5 0.9 shard_map.130
  67.5 0.0 collective-permute-done.piece_1
  67.5 0.0 collective-permute-done.1.piece_2
  67.5 0.0 collective-permute-done.2.piece_3
  67.5 3.5 %all-to-all-start.3 = ((bf16[8,288,128]{2,1,0:T(8,128)(2,1)}), bf16[8,288,128]{2,1,0:T(8,128)(2,1)S(1)}, u32[]{:S(2)}, u32[]{:S(2)}) async-start(bf16[8,288,128]{2,1,0:T(8,128)(2,1)} %get-tuple-element.43), calls=%async_computation.3 | async-start | bytes 1179648 | tf_op jit(solution)/shard_map/all_to_all | solution.py:462
  71.1 0.8 collective-permute-start.3
  71.9 1.6 %shard_map.131.prepared = bf16[3328,256]{1,0:T(8,128)(2,1)S(1)} custom-call(bf16[1152,128]{1,0:T(8,128)(2,1)S(1)} %copy-done.3, bf16[1152,128]{1,0:T(8,128)(2,1)} %collective-permute-done.piece_1, bf16[1152,128]{1,0:T(8,128)(2,1)} %collective-permute-done.1.piece_2, bf16[1152,128]{1,0:T(8,128)(2,1)} %collective-permute-done.2.piece_3), custom_call_target="tpu_custom_call" | custom-call | bytes 3145728 | tf_op jit(solution)/shard_map/pallas_call | solution.py:465
  73.5 0.0 collective-permute-done.3.fresh
  73.5 5.5 %all-to-all-done.3.queries = bf16[8,288,128]{2,1,0:T(8,128)(2,1)S(1)} async-done(((bf16[8,288,128]{2,1,0:T(8,128)(2,1)}), bf16[8,288,128]{2,1,0:T(8,128)(2,1)S(1)}, u32[]{:S(2)}, u32[]{:S(2)}) %all-to-all-start.3) | async-done | bytes 589856 | tf_op jit(solution)/shard_map/all_to_all | solution.py:462
  79.0 5.8 %shard_map.132 = bf16[8,304,128]{2,1,0:T(8,128)(2,1)S(1)} custom-call(bf16[8,288,128]{2,1,0:T(8,128)(2,1)S(1)} %all-to-all-done.3.queries, f32[8,256]{1,0:T(8,128)S(1)} %get-tuple-element.44.slot_adapters, bf16[5,256,128]{2,1,0:T(8,128)(2,1)S(1)} %copy-done.2, bf16[3328,256]{1,0:T(8,128)(2,1)S(1)} %shard_map.131.prepared, ...), custom_call_target="tpu_custom_call" | custom-call | flops 4294967296 | bytes 3145728 | tf_op jit(solution)/shard_map/pallas_call | solution.py:471
  84.9 14.2 %all_to_all.31.partials = bf16[8,304,128]{2,1,0:T(8,128)(2,1)S(1)} all-to-all(bf16[8,304,128]{2,1,0:T(8,128)(2,1)S(1)} %shard_map.132), channel_id=1, replica_groups=mesh['z'=8,'core'=2,'yh'=4,'yl'=2,'x'=4] {'yl','x'}, dimensions={0} | all-to-all | bytes 1245184 | tf_op jit(solution)/shard_map/all_to_all | solution.py:485
  99.0 0.2 shard_map.133
  99.2 14.8 %all_to_all.32.received = bf16[16,32,128]{2,1,0:T(8,128)(2,1)S(1)} all-to-all(bf16[16,32,128]{2,1,0:T(8,128)(2,1)S(1)} %shard_map.133), channel_id=1, replica_groups=mesh['z'=8,'core'=2,'yh'=4,'yl'=2,'x'=4] {'core','z'}, dimensions={0} | all-to-all | bytes 262144 | tf_op jit(solution)/shard_map/all_to_all | solution.py:494
  114.1 0.9 shard_map.134
  (12 shorter events, 0.0 us)
Async XLA Ops:
  1.5 17.7 %all-to-all-start = ((bf16[8,160,128]{2,1,0:T(8,128)(2,1)}), bf16[8,160,128]{2,1,0:T(8,128)(2,1)S(1)}, u32[]{:S(2)}, u32[]{:S(2)}) async-start(bf16[8,160,128]{2,1,0:T(8,128)(2,1)} %broadcast_in_dim.4), calls=%async_computation | async-start | bytes 655360 | tf_op jit(solution)/shard_map/all_to_all | solution.py:377
  20.5 16.8 %copy-start.6 = (f32[5120]{0:T(1024)S(1)}, f32[5120]{0:T(1024)}, u32[]{:S(2)}) copy-start(f32[5120]{0:T(1024)} %param.14) | copy-start | bytes 61444
  20.5 21.5 %copy-start = (bf16[208,5120]{1,0:T(8,128)(2,1)S(1)}, bf16[208,5120]{1,0:T(8,128)(2,1)}, u32[]{:S(2)}) copy-start(bf16[208,5120]{1,0:T(8,128)(2,1)} %get-tuple-element.35.weights) | copy-start | bytes 6389764
  20.5 21.5 %copy-start.4 = (s32[2]{0:T(128)S(1)}, s32[2]{0:T(128)}, u32[]{:S(2)}) copy-start(s32[2]{0:T(128)} %pad_add_fusion.place) | copy-start | bytes 28
  20.5 21.5 %copy-start.5 = (s32[128]{0:T(128)S(1)}, s32[128]{0:T(128)}, u32[]{:S(2)}) copy-start(s32[128]{0:T(128)} %param.23) | copy-start | bytes 1540
  20.6 21.4 %all-to-all-start.1 = ((bf16[4,8,160,128]{3,2,1,0:T(8,128)(2,1)}), bf16[4,8,160,128]{3,2,1,0:T(8,128)(2,1)S(1)}, u32[]{:S(2)}, u32[]{:S(2)}) async-start(bf16[4,8,160,128]{3,2,1,0:T(8,128)(2,1)} %broadcast_in_dim.5), calls=%async_computation.1 | async-start | bytes 2621440 | tf_op jit(solution)/shard_map/all_to_all | solution.py:422
  26.6 40.9 %collective-permute-start = (bf16[1152,128]{1,0:T(8,128)(2,1)}, bf16[1152,128]{1,0:T(8,128)(2,1)}, u32[]{:S(2)}, u32[]{:S(2)}) collective-permute-start(bf16[1152,128]{1,0:T(8,128)(2,1)} %get-tuple-element.40), channel_id=1, source_target_pairs={{0,8},{8,16},{16,24},{24,0},{1,9},{9,17},{17,25},{25,1},{2,10},{10... | collective-permute-start | bytes 884744 | tf_op jit(solution)/shard_map/ppermute | solution.py:418
  28.5 39.0 %collective-permute-start.1 = (bf16[1152,128]{1,0:T(8,128)(2,1)}, bf16[1152,128]{1,0:T(8,128)(2,1)}, u32[]{:S(2)}, u32[]{:S(2)}) collective-permute-start(bf16[1152,128]{1,0:T(8,128)(2,1)} %get-tuple-element.41), channel_id=1, source_target_pairs={{0,24},{8,0},{16,8},{24,16},{1,25},{9,1},{17,9},{25,17},{2,26},{10... | collective-permute-start | bytes 884744 | tf_op jit(solution)/shard_map/ppermute | solution.py:418
  34.0 33.5 %collective-permute-start.2 = (bf16[1152,128]{1,0:T(8,128)(2,1)}, bf16[1152,128]{1,0:T(8,128)(2,1)}, u32[]{:S(2)}, u32[]{:S(2)}) collective-permute-start(bf16[1152,128]{1,0:T(8,128)(2,1)} %get-tuple-element.42), channel_id=1, source_target_pairs={{0,16},{8,24},{16,0},{24,8},{1,17},{9,25},{17,1},{25,9},{2,18},{10... | collective-permute-start | bytes 884744 | tf_op jit(solution)/shard_map/ppermute | solution.py:418
  42.0 1.0 copy-start.1
  45.6 26.3 %copy-start.3 = (bf16[1152,128]{1,0:T(8,128)(2,1)S(1)}, bf16[1152,128]{1,0:T(8,128)(2,1)}, u32[]{:S(2)}) copy-start(bf16[1152,128]{1,0:T(8,128)(2,1)} %get-tuple-element.45.piece_0) | copy-start | bytes 884740
  67.5 11.5 %all-to-all-start.3 = ((bf16[8,288,128]{2,1,0:T(8,128)(2,1)}), bf16[8,288,128]{2,1,0:T(8,128)(2,1)S(1)}, u32[]{:S(2)}, u32[]{:S(2)}) async-start(bf16[8,288,128]{2,1,0:T(8,128)(2,1)} %get-tuple-element.43), calls=%async_computation.3 | async-start | bytes 1179648 | tf_op jit(solution)/shard_map/all_to_all | solution.py:462
  71.1 8.0 %copy-start.2 = (bf16[5,256,128]{2,1,0:T(8,128)(2,1)S(1)}, bf16[5,256,128]{2,1,0:T(8,128)(2,1)}, u32[]{:S(2)}) copy-start(bf16[5,256,128]{2,1,0:T(8,128)(2,1)} %get-tuple-element.36.smalls_far.smalls) | copy-start | bytes 983044
  71.1 2.4 %collective-permute-start.3 = (bf16[32,128]{1,0:T(8,128)(2,1)S(1)}, bf16[32,128]{1,0:T(8,128)(2,1)S(1)}, u32[]{:S(2)}, u32[]{:S(2)}) collective-permute-start(bf16[32,128]{1,0:T(8,128)(2,1)S(1)} %get-tuple-element.49), channel_id=1, source_target_pairs={{0,0},{4,8},{8,16},{12,24},{16,4},{20,12},{24,20},{28,28},{1,1},{5... | collective-permute-start | bytes 24584 | tf_op jit(solution)/shard_map/ppermute | solution.py:448
